TPU v7x, 32 devices: a whole 2x2x4 slice. The times are simulated.
32 devices in a mesh: var: 2 (over x), lat: 16 (over z, y, core).
Axes of the slice: x: 2, y: 2, z: 4, core: 2. Of those that a mesh axis runs over, the one named last changes fastest.
Arguments:
- grad_grid: bfloat16 [2, 768, 70, 1536], P('var', 'lat'), may hold values from -6 to 6
- remap: float32 [2, 70, 70], P('var'), may hold values from -0.75 to 0.75
- modes: float32 [2, 70, 70], P('var'), may hold values from -0.75 to 0.75
- balance: float32 [70, 70], replicated, may hold values from -0.75 to 0.75
- legendre: float32 [384, 768, 384], P('lat'), may hold values from -0.21875 to 0.21875
- control: float32 [2, 384, 140, 384], P('var', 'lat'), may hold values from -6 to 6
- step_size: float32 [2], P('var'), may hold values from 0.2 to 0.8
- owner_slots: int32 [384], replicated, may hold values from 0 to 383, each once
Outputs:
- updated: float32 [2, 384, 140, 384], P('var', 'lat')
- increment: bfloat16 [2, 768, 70, 1536], P('var', 'lat')
Inputs may be any that keep to these rules, and one draw needn't show every extreme that they name: `owner_slots`: each zonal wavenumber below 384 stands in exactly one owner slot; lat index d holds slots d * 24 to (d + 1) * 24 - 1.
All inputs are finite; a program needn't handle non-finite values.
Results may differ from a plain program's by a relative error of at most 0.001.
Values sent between devices are 32-bit elements; how exact they have to be, the bound alone decides.
No kernel may reach another device: no remote copies, remote signals or barrier semaphores. Data moves between devices by JAX's collectives and lax.ppermute only.
A program may use at most 192 MiB of HBM per device.

v0:
```python
import math

import jax
import jax.numpy as jnp
from jax import lax
from jax.sharding import PartitionSpec as P

highest = lax.Precision.HIGHEST


def from_behind(block, axis, distance):
    devices = range(lax.axis_size(axis))
    route = [(i - distance, i) for i in devices if i - distance in devices]
    return lax.ppermute(block, axis, route)


def make_waves(owner_slots, lon_count):
    longitude = lax.iota(jnp.int32, lon_count)
    phases = longitude[:, None] * owner_slots[None, :] % lon_count
    angles = phases.astype(jnp.float32) * (2.0 * math.pi / lon_count)
    factor = math.sqrt(2.0 / lon_count)
    return jnp.stack([jnp.cos(angles), jnp.sin(angles)], axis=1) * factor


def local(grad_grid, remap, modes, balance, legendre, control, step_size, owner_slots):
    lat_rows = grad_grid.shape[1]
    levels = grad_grid.shape[2]
    lon_count = grad_grid.shape[3]
    wave_count = owner_slots.shape[0]
    owned_count = legendre.shape[0]
    degrees = legendre.shape[2]
    wave_table = make_waves(owner_slots, lon_count)
    remap_var = remap[0]
    modes_var = modes[0]
    lifted = jnp.einsum(
        "ik,lij->lkj", remap_var, grad_grid[0].astype(jnp.float32), precision=highest
    )
    slab_coef = jnp.einsum("lkj,jcs->slck", lifted, wave_table, precision=highest)
    spectral = jnp.einsum(
        "sln,slq->sqn",
        legendre,
        lax.all_to_all(
            slab_coef.reshape(wave_count, lat_rows, 2 * levels),
            "lat",
            split_axis=0,
            concat_axis=1,
            tiled=True,
        ),
        precision=highest,
    )
    spec_four = spectral.reshape(owned_count, 2, levels, degrees)
    partner = from_behind(spec_four, "var", -1)
    blended = spec_four + jnp.einsum("ik,scin->sckn", balance, partner, precision=highest)
    spectral = jnp.einsum("ik,scin->sckn", modes_var, blended, precision=highest).reshape(
        owned_count, 2 * levels, degrees
    )
    own_control = control[0]
    updated = own_control - step_size[0] * (own_control + spectral)
    level_coef = jnp.einsum(
        "ki,scin->sckn",
        modes_var,
        updated.reshape(owned_count, 2, levels, degrees),
        precision=highest,
    )
    partner = from_behind(level_coef, "var", 1)
    level_coef = level_coef + jnp.einsum("ki,scin->sckn", balance, partner, precision=highest)
    level_coef = level_coef.reshape(owned_count, 2 * levels, degrees)
    fourier = jnp.einsum("sln,sqn->slq", legendre, level_coef, precision=highest)
    slab_back = lax.all_to_all(fourier, "lat", split_axis=1, concat_axis=0, tiled=True)
    slab_back = slab_back.reshape(wave_count, lat_rows, 2, levels)
    lowered = jnp.einsum("slck,jcs->lkj", slab_back, wave_table, precision=highest)
    increment = jnp.einsum("ik,lkj->lij", remap_var, lowered, precision=highest).astype(
        jnp.bfloat16
    )
    return (updated[None], increment[None])


def solution(mesh):
    return jax.shard_map(
        local,
        mesh=mesh,
        in_specs=(
            P("var", "lat", None, None),
            P("var", None, None),
            P("var", None, None),
            P(),
            P("lat", None, None),
            P("var", "lat", None, None),
            P("var"),
            P(),
        ),
        out_specs=(P("var", "lat", None, None), P("var", "lat", None, None)),
        check_vma=False,
    )
```

profile of v0, /device:TPU:15, one launch (start us, length us, event | category | flops | bytes accessed | tf_op | source)
XLA Modules:
  0.0 1648.6 jit_solution(11036552403875958279)
XLA Ops:
  0.6 0.0 copy-start
  0.6 11.3 fusion.53
  11.9 0.0 copy-start.3
  11.9 20.2 %fusion.12 = f32[48,1536,70]{1,2,0:T(8,128)} fusion(bf16[48,70,1536]{2,0,1:T(8,128)(2,1)} %bitcast.105, f32[1,70,70]{2,0,1:T(1,128)} %param.9), kind=kOutput, calls=%fused_computation.8 | convolution fusion | flops 4335206400 | bytes 30985360 | tf_op jit(solution)/shard_map/ik,lij->lkj/dot_general | solution.py:35
  32.1 0.0 copy-done.3
  32.2 61.6 %fusion.31 = f32[384,48,2,70]{0,3,1,2:T(8,128)S(1)} fusion(f32[48,1536,70]{1,2,0:T(8,128)} %fusion.12, f32[1536,1,384]{2,0,1:T(8,128)} %get-tuple-element.11, f32[1536,1,384]{2,0,1:T(8,128)S(1)} %get-tuple-element.10), kind=kOutput, calls=%fused_computation.31 | convolution fusion | flops 47565766656 | bytes 35684352 | tf_op jit(solution)/shard_map/lkj,jcs->slck/dot_general | solution.py:38
  93.8 6.0 copy.55
  99.8 19.0 %copy.56 = f32[384,48,140]{2,1,0:T(8,128)} copy(f32[384,48,140]{0,1,2:T(8,128)} %bitcast.104) | data formatting | bytes 20643840 | tf_op jit(solution)/shard_map/reshape | solution.py:43
  118.8 413.4 %all_to_all.33 = f32[384,48,140]{2,1,0:T(8,128)S(1)} all-to-all(f32[384,48,140]{2,1,0:T(8,128)} %copy.56), channel_id=1, replica_groups=mesh['var'=2,'lat'=16] {'lat'}, dimensions={0} | all-to-all | bytes 20643840 | tf_op jit(solution)/shard_map/all_to_all | solution.py:42
  532.2 6.9 copy.57
  539.1 47.3 %fusion.69 = f32[24,140,384]{2,1,0:T(8,128)} fusion(f32[24,768,140]{2,1,0:T(8,128)} %bitcast.101, f32[24,768,384]{2,1,0:T(8,128)} %param.12), kind=kOutput, calls=%fused_computation.61 | convolution fusion | flops 11890851840 | bytes 43794432 | tf_op jit(solution)/shard_map/sln,slq->sqn/dot_general | solution.py:39
  586.4 4.2 copy.59
  590.5 2.5 collective-permute-start
  593.7 0.0 copy-start.6
  593.7 109.5 %collective-permute-done = f32[24,2,70,384]{3,0,2,1:T(8,128)S(1)} collective-permute-done((f32[24,2,70,384]{3,0,2,1:T(8,128)S(1)}, f32[24,2,70,384]{3,0,2,1:T(8,128)S(1)}, u32[]{:S(2)}, u32[]{:S(2)}) %collective-permute-start) | collective-permute-done | bytes 5160992 | tf_op jit(solution)/shard_map/ppermute | solution.py:14
  703.2 0.0 copy-done
  703.2 0.0 slice-start
  703.2 5.5 fusion.20
  708.7 0.0 copy-done.6
  708.7 0.0 slice-start.1
  708.7 5.6 fusion.45
  714.3 0.0 copy-start.2
  714.3 0.0 slice-done
  714.4 0.0 slice-done.1
  714.4 6.2 fusion.40
  720.6 0.0 copy-done.2
  720.6 1.7 copy.67
  722.3 1.3 collective-permute-start.1
  723.6 112.6 %collective-permute-done.1 = f32[24,2,70,384]{3,0,2,1:T(8,128)S(1)} collective-permute-done((f32[24,2,70,384]{3,0,2,1:T(8,128)S(1)}, f32[24,2,70,384]{3,0,2,1:T(8,128)S(1)}, u32[]{:S(2)}, u32[]{:S(2)}) %collective-permute-start.1) | collective-permute-done | bytes 5160992 | tf_op jit(solution)/shard_map/ppermute | solution.py:14
  836.2 5.6 bitcast_add_fusion
  841.8 3.9 copy.69
  845.7 37.6 %fusion.36 = f32[24,768,140]{1,2,0:T(8,128)} fusion(f32[24,768,384]{2,1,0:T(8,128)} %param.12, f32[24,140,384]{2,0,1:T(8,128)} %bitcast.103), kind=kOutput, calls=%fused_computation.32 | convolution fusion | flops 11890851840 | bytes 43794432 | tf_op jit(solution)/shard_map/sln,sqn->slq/dot_general | solution.py:68
  883.3 18.9 %copy.71 = f32[24,768,140]{2,0,1:T(8,128)} copy(f32[24,768,140]{1,2,0:T(8,128)} %fusion.36) | data formatting | bytes 20643840 | tf_op jit(solution)/shard_map/sln,sqn->slq/dot_general | solution.py:68
  902.3 8.3 all-to-all-start.1
  910.6 4.2 copy.64
  914.7 5.4 fusion.28
  920.1 397.5 %all-to-all-done.1 = f32[24,768,140]{2,0,1:T(8,128)} async-done(((f32[24,768,140]{2,0,1:T(8,128)}), f32[24,768,140]{2,0,1:T(8,128)}, u32[]{:S(2)}, u32[]{:S(2)}) %all-to-all-start.1) | async-done | bytes 10321952 | tf_op jit(solution)/shard_map/all_to_all | solution.py:69
  1317.6 17.5 %copy.73 = f32[16,24,48,140]{3,2,1,0:T(8,128)} copy(f32[16,24,48,140]{3,1,2,0:T(8,128)} %bitcast.28) | data formatting | bytes 20643840 | tf_op jit(solution)/shard_map/all_to_all | solution.py:69
  1335.1 0.0 copy-start.4
  1335.1 22.8 %reshape.103 = f32[384,48,2,70]{3,2,1,0:T(2,128)} reshape(f32[16,24,48,140]{3,2,1,0:T(8,128)} %copy.73) | data formatting | bytes 20643840 | tf_op jit(solution)/shard_map/reshape | solution.py:70
  1357.9 0.0 copy-done.4
  1357.9 0.0 copy-start.5
  1357.9 247.6 %fusion.4 = f32[48,70,1536,1]{2,1,3,0:T(8,128)} fusion(f32[384,48,2,70]{3,2,1,0:T(2,128)} %reshape.103, f32[1536,1,384]{2,0,1:T(8,128)} %get-tuple-element.11, f32[1536,1,384]{2,0,1:T(8,128)S(1)} %copy-done.4), kind=kOutput, calls=%fused_computation.4 | convolution fusion | flops 47565766656 | bytes 35684352 | tf_op jit(solution)/shard_map/slck,jcs->lkj/dot_general | solution.py:71
  1605.6 0.0 copy-done.5
  1605.6 0.0 copy-start.1
  1605.6 31.2 %fusion.9 = bf16[1,48,70,1536]{3,2,1,0:T(8,128)(2,1)} fusion(f32[48,70,1536,1]{2,1,3,0:T(8,128)} %fusion.4, f32[1,70,70]{2,0,1:T(1,128)S(1)} %copy-done.5), kind=kOutput, calls=%fused_computation.7 | convolution fusion | flops 4340367360 | bytes 30985360 | tf_op jit(solution)/shard_map/ik,lkj->lij/dot_general | solution.py:72
  1636.9 11.5 copy.75
  1648.4 0.0 copy-done.1
  (1 shorter events, 0.0 us)
Async XLA Ops:
  0.6 702.5 %copy-start = (f32[70,70]{1,0:T(8,128)S(1)}, f32[70,70]{1,0:T(8,128)}, u32[]{:S(2)}) copy-start(f32[70,70]{1,0:T(8,128)} %param.11) | copy-start | bytes 58804
  11.9 20.2 %copy-start.3 = (f32[1536,1,384]{2,0,1:T(8,128)}, f32[1536,1,384]{2,0,1:T(8,128)S(1)}, u32[]{:S(2)}) copy-start(f32[1536,1,384]{2,0,1:T(8,128)S(1)} %get-tuple-element.10) | copy-start | bytes 7077892
  590.5 112.6 %collective-permute-start = (f32[24,2,70,384]{3,0,2,1:T(8,128)S(1)}, f32[24,2,70,384]{3,0,2,1:T(8,128)S(1)}, u32[]{:S(2)}, u32[]{:S(2)}) collective-permute-start(f32[24,2,70,384]{3,0,2,1:T(8,128)S(1)} %bitcast.106), channel_id=1, source_target_pairs={{16,0},{17,1},{18,2},{19,3},{20,4},{21,5},{22,6},{23,7},{24,8},{25... | collective-permute-start | bytes 15482888 | tf_op jit(solution)/shard_map/ppermute | solution.py:14
  593.7 115.0 %copy-start.6 = (f32[1,70,70]{2,0,1:T(1,128)S(1)}, f32[1,70,70]{2,0,1:T(1,128)}, u32[]{:S(2)}) copy-start(f32[1,70,70]{2,0,1:T(1,128)} %param.10) | copy-start | bytes 58804
  703.2 11.2 slice-start
  708.7 5.6 slice-start.1
  714.3 6.3 copy-start.2
  722.3 113.9 %collective-permute-start.1 = (f32[24,2,70,384]{3,0,2,1:T(8,128)S(1)}, f32[24,2,70,384]{3,0,2,1:T(8,128)S(1)}, u32[]{:S(2)}, u32[]{:S(2)}) collective-permute-start(f32[24,2,70,384]{3,0,2,1:T(8,128)S(1)} %copy.67), channel_id=1, source_target_pairs={{0,16},{1,17},{2,18},{3,19},{4,20},{5,21},{6,22},{7,23},{8,24},{9,... | collective-permute-start | bytes 15482888 | tf_op jit(solution)/shard_map/ppermute | solution.py:14
  902.3 415.4 %all-to-all-start.1 = ((f32[24,768,140]{2,0,1:T(8,128)}), f32[24,768,140]{2,0,1:T(8,128)}, u32[]{:S(2)}, u32[]{:S(2)}) async-start(f32[24,768,140]{2,0,1:T(8,128)} %copy.71), calls=%async_computation.1 | async-start | bytes 37748736 | tf_op jit(solution)/shard_map/all_to_all | solution.py:69
  1335.1 22.8 %copy-start.4 = (f32[1536,1,384]{2,0,1:T(8,128)S(1)}, f32[1536,1,384]{2,0,1:T(8,128)}, u32[]{:S(2)}) copy-start(f32[1536,1,384]{2,0,1:T(8,128)} %copy-done.3) | copy-start | bytes 7077892
  1357.9 247.7 %copy-start.5 = (f32[1,70,70]{2,0,1:T(1,128)S(1)}, f32[1,70,70]{2,0,1:T(1,128)}, u32[]{:S(2)}) copy-start(f32[1,70,70]{2,0,1:T(1,128)} %param.9) | copy-start | bytes 58804
  1605.6 42.8 %copy-start.1 = (f32[70,70]{1,0:T(8,128)S(1)}, f32[70,70]{1,0:T(8,128)}, u32[]{:S(2)}) copy-start(f32[70,70]{1,0:T(8,128)} %param.11) | copy-start | bytes 58804
where the time goes:
time: 1660 us; the launch traced here: 1650 us
  waiting for transfers between devices  620 us (37%)
  matrix products  469 us (28%)
  blocking collectives  413 us (25%)
  local copies, waits for them, and re-layouts  117 us (7%)
  other arithmetic  16.7 us (1%)
    all_to_all x1, blocking collectives, local(): lax.all_to_all(slab_coef.reshape(wave_count, lat_rows, 2 * levels), 'lat'...  413 us
    all_to_all x1, waiting for transfers between devices, local(): lax.all_to_all(fourier, 'lat', split_axis=1, concat_axis=0, tiled=True)  397 us
    dot_general x1, matrix products, local(): jnp.einsum('slck,jcs->lkj', slab_back, wave_table, precision=highest)  248 us
    ppermute x2, waiting for transfers between devices, from_behind(): return lax.ppermute(block, axis, route)  222 us
    dot_general x1, matrix products, local(): jnp.einsum('lkj,jcs->slck', lifted, wave_table, precision=highest)  61.6 us
    dot_general x1, matrix products, local(): jnp.einsum('sln,slq->sqn', legendre, lax.all_to_all(slab_coef.reshape(wav...  47.3 us
    dot_general x1, matrix products, local(): jnp.einsum('sln,sqn->slq', legendre, level_coef, precision=highest)  37.6 us
  transfers between devices with their start and end apart: 3, of which 3 were waited for; matrix products, arithmetic and copies ran while one was open for 1% of the time, Pallas kernels for 0%

commit v1 on v0

--- a/solution.py
+++ b/solution.py
@@ -1,17 +1,515 @@
+import copy
+import functools
 import math
 
 import jax
 import jax.numpy as jnp
+import numpy as np
 from jax import lax
+from jax.experimental import pallas as pl
+from jax.experimental.pallas import tpu as pltpu
 from jax.sharding import PartitionSpec as P
 
 highest = lax.Precision.HIGHEST
+LANES = 128
+COST_SHARE = 8
+VMEM_BYTES = 63 * 1024 * 1024
+NN = (((1,), (0,)), ((), ()))
+NT = (((1,), (1,)), ((), ()))
+
+
+def round_up(value, step):
+    return -(-value // step) * step
 
 
 def from_behind(block, axis, distance):
     devices = range(lax.axis_size(axis))
     route = [(i - distance, i) for i in devices if i - distance in devices]
     return lax.ppermute(block, axis, route)
+
+
+@functools.lru_cache(maxsize=None)
+def natural_waves(wave_count, lon_count):
+    phases = np.arange(wave_count)[:, None] * np.arange(lon_count)[None, :] % lon_count
+    angles = phases * (2.0 * math.pi / lon_count)
+    table = np.stack([np.cos(angles), np.sin(angles)], axis=1) * math.sqrt(2.0 / lon_count)
+    table = table.reshape(2 * wave_count, lon_count).astype(np.float32)
+    upper = table.astype(jnp.bfloat16)
+    lower = (table - upper.astype(np.float32)).astype(jnp.bfloat16)
+    return np.concatenate([upper, lower], axis=1)
+
+
+def chosen_waves(slots, wave_count, lon_count):
+    rows = (2 * slots[:, None] + lax.iota(jnp.int32, 2)[None, :]).reshape(-1)
+    onehot = (rows[:, None] == lax.iota(jnp.int32, 2 * wave_count)[None, :]).astype(jnp.bfloat16)
+    table = jnp.asarray(natural_waves(wave_count, lon_count))
+    return jnp.dot(onehot, table, preferred_element_type=jnp.float32).astype(jnp.bfloat16)
+
+
+def halves(x):
+    upper = x.astype(jnp.bfloat16)
+    return upper, (x - upper.astype(jnp.float32)).astype(jnp.bfloat16)
+
+
+def mxu(a, b, dims):
+    return lax.dot_general(a, b, dims, preferred_element_type=jnp.float32)
+
+
+def dot3(a, b, dims=NN):
+    (a_up, a_low), (b_up, b_low) = a, b
+    return mxu(a_up, b_up, dims) + (mxu(a_up, b_low, dims) + mxu(a_low, b_up, dims))
+
+
+def anywhere(arrays):
+    return [pl.BlockSpec(memory_space=pl.ANY)] * len(arrays)
+
+
+def behind(kernel, inputs, after):
+    def body(*refs):
+        kernel(*refs[:inputs], *refs[inputs + after :])
+
+    return body
+
+
+MARK = jax.ShapeDtypeStruct((8, LANES), jnp.float32)
+MARK_SPEC = pl.BlockSpec(MARK.shape, lambda *_: (0, 0))
+
+
+def cost(flops):
+    return pl.CostEstimate(flops=flops // COST_SHARE, bytes_accessed=0, transcendentals=0)
+
+
+def gate(block, *after):
+    return pl.pallas_call(
+        lambda *refs: None,
+        in_specs=anywhere((block, *after)),
+        out_specs=pl.BlockSpec(memory_space=pl.ANY),
+        out_shape=jax.ShapeDtypeStruct(block.shape, block.dtype),
+        input_output_aliases={0: 0},
+        cost_estimate=pl.CostEstimate(flops=0, bytes_accessed=0, transcendentals=0),
+        name="gate",
+    )(block, *after)
+
+
+class Rows:
+    def __init__(self, lats, levels, units):
+        self.levels, self.units = levels, units
+        self.full = lats * levels // LANES * LANES
+        self.tail = lats * levels - self.full
+        self.lanes = units * self.full + round_up(units * self.tail, LANES)
+
+    def end(self, unit):
+        return self.units * self.full + unit * self.tail
+
+    def pieces(self, unit, lat):
+        first, last = lat * self.levels, (lat + 1) * self.levels
+        pieces = []
+        if first < self.full:
+            stop = min(last, self.full)
+            pieces.append((slice(unit * self.full + first, unit * self.full + stop), slice(0, stop - first)))
+        if last > self.full:
+            start = max(first, self.full)
+            lane = self.end(unit) + start - self.full
+            pieces.append((slice(lane, lane + last - start), slice(start - first, self.levels)))
+        return pieces
+
+
+def dft_kernel(steps, place, grad_ref, wave_ref, out_ref, mark_ref, rows_ref):
+    mark_ref[...] = jnp.zeros(mark_ref.shape, jnp.float32)
+    levels, lats, lons = grad_ref.shape
+    waves = wave_ref.shape[0]
+    lead = rows_ref.shape[1] // lats
+    grad = grad_ref[...].reshape(levels * lats, lons)
+    terms = mxu(grad, jnp.concatenate([wave_ref[:, :lons], wave_ref[:, lons:]], axis=0), NT)
+    coef = terms[:, :waves] + terms[:, waves:]
+    for unit in range(place.units):
+        rows_ref[unit, 0 : levels * lats, :] = coef[:, unit * LANES : (unit + 1) * LANES]
+        if lead > levels:
+            rows_ref[unit, levels * lats :, :] = jnp.zeros(((lead - levels) * lats, LANES), jnp.float32)
+
+    for step in range(steps):
+
+        @pl.when(pl.program_id(0) == step)
+        def _(step=step):
+            if step == 0:
+                end = place.end(place.units)
+                out_ref[:, end:] = jnp.zeros((LANES, place.lanes - end), jnp.float32)
+            for unit in range(place.units):
+                for lat in range(lats):
+                    part = rows_ref[unit, pl.ds(lat, lead, stride=lats), :].T
+                    for lanes, chosen in place.pieces(unit, step * lats + lat):
+                        out_ref[:, lanes] = part[:, chosen]
+
+
+def forward_dft(grad, table, place, after):
+    levels, lats, lons = grad.shape
+    waves = table.shape[0]
+    block = 16
+    steps = lats // block
+    lead = round_up(levels, 8)
+    return pl.pallas_call(
+        behind(functools.partial(dft_kernel, steps, place), 2, len(after)),
+        grid=(steps,),
+        in_specs=[
+            pl.BlockSpec((levels, block, lons), lambda i: (0, i, 0)),
+            pl.BlockSpec(table.shape, lambda i: (0, 0)),
+            *anywhere(after),
+        ],
+        out_specs=[pl.BlockSpec((LANES, place.lanes), lambda i: (0, 0)), MARK_SPEC],
+        out_shape=[jax.ShapeDtypeStruct((LANES, place.lanes), jnp.float32), MARK],
+        scratch_shapes=[pltpu.VMEM((place.units, lead * block, LANES), jnp.float32)],
+        compiler_params=pltpu.CompilerParams(vmem_limit_bytes=VMEM_BYTES),
+        cost_estimate=cost(4 * levels * lats * lons * waves),
+        name="forward_dft",
+    )(grad, table, *after)
+
+
+def spectral_kernel(place, got_ref, end_ref, leg_ref, mat_ref, own_ref, send_ref, flat_ref, cols_ref):
+    devices, rows, width = got_ref.shape
+    slots, lat_count, _ = leg_ref.shape
+    lats = lat_count // devices
+    lead = mat_ref.shape[1] // 2
+    levels = place.levels
+    tiles = width // LANES
+    cols_ref[...] = jnp.zeros(cols_ref.shape, jnp.float32)
+    for tile in range(tiles):
+        piece = got_ref[:, :, tile * LANES : (tile + 1) * LANES]
+        flat_ref[tile] = piece.reshape(devices * rows, LANES)
+    flat_ref[tiles] = end_ref[...].reshape(devices * rows, LANES)
+    mat = halves(mat_ref[...])
+    for slot in range(slots):
+        turned = []
+        for part in range(2):
+            row = 2 * slot + part
+            lines = [flat_ref[t, pl.ds(row, devices, stride=rows), :] for t in range(tiles + 1)]
+            end = place.end(place.unit) % LANES
+            lines[tiles] = lines[tiles][:, end : end + place.tail]
+            line = jnp.concatenate(lines, axis=1)
+            for lat in range(lats):
+                cols_ref[pl.ds(row * lat_count + lat, devices, stride=lats), 0:levels] = line[
+                    :, lat * levels : (lat + 1) * levels
+                ]
+            turned.append(cols_ref[row * lat_count : (row + 1) * lat_count, :].T[:lead])
+        coef = dot3(halves(jnp.concatenate(turned, axis=0)), halves(leg_ref[slot]))
+        mixed = dot3(mat, halves(coef))
+        own_ref[slot] = mixed[: 2 * lead]
+        send_ref[slot] = mixed[2 * lead :]
+
+
+def spectral(got, place, unit, legendre, first, mat, after):
+    devices, rows, _ = got.shape
+    _, lat_count, degrees = legendre.shape
+    slots = rows // 2
+    lead = mat.shape[1]
+    place = copy.copy(place)
+    place.unit = unit
+    end_tile = place.end(unit) // LANES
+    shape = jax.ShapeDtypeStruct((slots, lead, degrees), jnp.float32)
+    spec = pl.BlockSpec(shape.shape, lambda i: (0, 0, 0))
+    return pl.pallas_call(
+        behind(functools.partial(spectral_kernel, place), 4, len(after)),
+        grid=(1,),
+        in_specs=[
+            pl.BlockSpec((devices, rows, place.full), lambda i: (0, 0, unit)),
+            pl.BlockSpec((devices, rows, LANES), lambda i: (0, 0, end_tile)),
+            pl.BlockSpec((slots, lat_count, degrees), lambda i: (first, 0, 0)),
+            pl.BlockSpec(mat.shape, lambda i: (0, 0)),
+            *anywhere(after),
+        ],
+        out_specs=[spec, spec],
+        out_shape=[shape, shape],
+        scratch_shapes=[
+            pltpu.VMEM((place.full // LANES + 1, devices * rows, LANES), jnp.float32),
+            pltpu.VMEM((rows * lat_count, LANES), jnp.float32),
+        ],
+        compiler_params=pltpu.CompilerParams(vmem_limit_bytes=VMEM_BYTES),
+        cost_estimate=cost(12 * slots * lat_count * degrees * lead),
+        name="spectral_adjoint",
+    )(got, got, legendre, mat, *after)
+
+
+def update_kernel(step_ref, own_ref, got_ref, control_ref, mode_ref, mat_ref, new_ref, keep_ref, send_ref):
+    lead = own_ref.shape[1]
+    mode = halves(mode_ref[...])
+    mat = halves(mat_ref[...])
+    for slot in range(own_ref.shape[0]):
+        adjoint = dot3(mode, halves(own_ref[slot] + got_ref[slot]))
+        control = control_ref[slot]
+        new = control - step_ref[0] * (control + adjoint)
+        new_ref[slot] = new
+        mixed = dot3(mat, halves(new))
+        keep_ref[slot] = mixed[:lead]
+        send_ref[slot] = mixed[lead:]
+
+
+def update(step_size, own, got, control, first, mode, mat, after):
+    slots, lead, degrees = own.shape
+    spec = pl.BlockSpec(own.shape, lambda i: (0, 0, 0))
+    shape = jax.ShapeDtypeStruct(own.shape, jnp.float32)
+    return pl.pallas_call(
+        behind(update_kernel, 6, len(after)),
+        grid=(1,),
+        in_specs=[
+            pl.BlockSpec(memory_space=pltpu.SMEM),
+            spec,
+            spec,
+            pl.BlockSpec(own.shape, lambda i: (first, 0, 0)),
+            pl.BlockSpec(mode.shape, lambda i: (0, 0)),
+            pl.BlockSpec(mat.shape, lambda i: (0, 0)),
+            *anywhere(after),
+        ],
+        out_specs=[spec, spec, spec],
+        out_shape=[shape, shape, shape],
+        compiler_params=pltpu.CompilerParams(vmem_limit_bytes=VMEM_BYTES),
+        cost_estimate=cost(36 * slots * lead * lead * degrees),
+        name="gradient_step",
+    )(step_size, own, got, control, mode, mat, *after)
+
+
+def back_kernel(place, *refs):
+    units = place.units
+    keep_refs, got_refs = refs[:units], refs[units : 2 * units]
+    leg_ref, mat_ref, out_ref, mark_ref, cols_ref, line_ref, flat_ref = refs[2 * units :]
+    mark_ref[...] = jnp.zeros(mark_ref.shape, jnp.float32)
+    devices, rows, _ = out_ref.shape
+    slots, lat_count, degrees = leg_ref.shape
+    lats = lat_count // devices
+    lead = mat_ref.shape[0] // 2
+    levels = place.levels
+    tiles = place.full // LANES
+    mat = halves(mat_ref[...])
+    gap = jnp.zeros((LANES - lead, degrees), jnp.float32)
+
+    for unit in range(units):
+
+        @pl.when(pl.program_id(0) == unit)
+        def _(unit=unit):
+            if unit == 0:
+                out_ref[:, :, units * place.full :] = jnp.zeros(
+                    (devices, rows, place.lanes - units * place.full), jnp.float32
+                )
+            if place.tail:
+                unused = (line_ref.shape[0], LANES - place.tail)
+                line_ref[:, place.full + place.tail :] = jnp.zeros(unused, jnp.float32)
+            for slot in range(slots):
+                coef = dot3(mat, halves(keep_refs[unit][slot] + got_refs[unit][slot]))
+                coef = jnp.concatenate([coef[:lead], gap, coef[lead:], gap], axis=0)
+                fourier = dot3(halves(leg_ref[slot]), halves(coef), NT)
+                for part in range(2):
+                    row = 2 * slot + part
+                    base = row * lat_count
+                    cols_ref[base : base + lat_count, :] = fourier[:, part * LANES : (part + 1) * LANES]
+                    line = slice(row * devices, (row + 1) * devices)
+                    for lat in range(lats):
+                        piece = cols_ref[pl.ds(base + lat, devices, stride=lats), :]
+                        line_ref[line, lat * levels : (lat + 1) * levels] = piece[:, :levels]
+                    for tile in range(line_ref.shape[1] // LANES):
+                        flat_ref[tile, pl.ds(row, devices, stride=rows), :] = line_ref[
+                            line, tile * LANES : (tile + 1) * LANES
+                        ]
+            for tile in range(tiles):
+                start = unit * place.full + tile * LANES
+                out_ref[:, :, start : start + LANES] = flat_ref[tile].reshape(devices, rows, LANES)
+            if place.tail:
+                lane = place.end(unit)
+                ends = flat_ref[tiles].reshape(devices, rows, LANES)[:, :, : place.tail]
+                out_ref[:, :, lane : lane + place.tail] = ends
+
+
+def spectral_back(keeps, gots, place, legendre, first, mat, devices, after):
+    slots, lead, degrees = keeps[0].shape
+    lat_count = legendre.shape[1]
+    rows = 2 * slots
+    units = place.units
+    spec = pl.BlockSpec(keeps[0].shape, lambda i: (0, 0, 0))
+    padded_row = place.full + (LANES if place.tail else 0)
+    shape = jax.ShapeDtypeStruct((devices, rows, place.lanes), jnp.float32)
+    return pl.pallas_call(
+        behind(functools.partial(back_kernel, place), 2 * units + 2, len(after)),
+        grid=(units,),
+        in_specs=[spec] * (2 * units)
+        + [
+            pl.BlockSpec((slots, lat_count, degrees), lambda i: (i + first, 0, 0)),
+            pl.BlockSpec(mat.shape, lambda i: (0, 0)),
+            *anywhere(after),
+        ],
+        out_specs=[pl.BlockSpec(shape.shape, lambda i: (0, 0, 0)), MARK_SPEC],
+        out_shape=[shape, MARK],
+        scratch_shapes=[
+            pltpu.VMEM((rows * lat_count, LANES), jnp.float32),
+            pltpu.VMEM((rows * devices, padded_row), jnp.float32),
+            pltpu.VMEM((padded_row // LANES, devices * rows, LANES), jnp.float32),
+        ],
+        compiler_params=pltpu.CompilerParams(vmem_limit_bytes=VMEM_BYTES),
+        cost_estimate=cost(12 * units * slots * lat_count * degrees * lead),
+        name="spectral_forward",
+    )(*keeps, *gots, legendre, mat, *after)
+
+
+def inverse_kernel(steps, place, has_total, coef_ref, up_ref, low_ref, *refs):
+    total_ref = refs[0] if has_total else None
+    out_ref, rows_ref, left_ref = refs[has_total:]
+    levels, lats, columns = out_ref.shape
+    waves = up_ref.shape[0]
+
+    for step in range(steps):
+
+        @pl.when((pl.program_id(0) == step) & (pl.program_id(1) == 0))
+        def _(step=step):
+            for unit in range(place.units):
+                for lat in range(lats):
+                    parts = [coef_ref[:, at] for at, _ in place.pieces(unit, step * lats + lat)]
+                    part = parts[0] if len(parts) == 1 else jnp.concatenate(parts, axis=1)
+                    rows_ref[unit, pl.ds(lat, levels, stride=lats), :] = part.T
+                high, rest = halves(rows_ref[unit])
+                for term, value in enumerate((high, rest, high)):
+                    start = term * waves + unit * LANES
+                    left_ref[:, start : start + LANES] = value
+
+    right = jnp.concatenate([up_ref[...], up_ref[...], low_ref[...]], axis=0)
+    result = mxu(left_ref[...], right, NN).reshape(levels, lats, columns)
+    if has_total:
+        result = result + total_ref[...]
+    out_ref[...] = result.astype(out_ref.dtype)
+
+
+def inverse_dft(coef, place, table, total, lats, dtype, after):
+    waves = table.shape[0]
+    lons = table.shape[1] // 2
+    levels = place.levels
+    block = 16
+    steps = lats // block
+    columns = 512 if lons % 512 == 0 else lons
+    turns = lons // columns
+    grid_spec = pl.BlockSpec((levels, block, columns), lambda i, j: (0, i, j))
+    totals = [] if total is None else [total]
+    return pl.pallas_call(
+        behind(functools.partial(inverse_kernel, steps, place, len(totals)), 3 + len(totals), len(after)),
+        grid=(steps, turns),
+        in_specs=[
+            pl.BlockSpec(coef.shape, lambda i, j: (0, 0)),
+            pl.BlockSpec((waves, columns), lambda i, j: (0, j)),
+            pl.BlockSpec((waves, columns), lambda i, j: (0, j + turns)),
+        ]
+        + [grid_spec] * len(totals)
+        + anywhere(after),
+        out_specs=grid_spec,
+        out_shape=jax.ShapeDtypeStruct((levels, lats, lons), dtype),
+        scratch_shapes=[
+            pltpu.VMEM((place.units, levels * block, LANES), jnp.float32),
+            pltpu.VMEM((levels * block, 3 * waves), jnp.bfloat16),
+        ],
+        compiler_params=pltpu.CompilerParams(vmem_limit_bytes=VMEM_BYTES),
+        cost_estimate=cost(6 * levels * lats * lons * waves),
+        name="inverse_dft",
+    )(coef, table, table, *totals, *after)
+
+
+def padded(matrix, lead):
+    return jnp.pad(matrix, ((0, lead - matrix.shape[0]), (0, lead - matrix.shape[1])))
+
+
+def on_both(matrix, lead):
+    return jnp.kron(jnp.eye(2, dtype=jnp.float32), padded(matrix, lead))
+
+
+def exchange(block):
+    return lax.all_to_all(block, "lat", split_axis=0, concat_axis=0, tiled=True)
+
+
+def tiled_local(grad_grid, remap, modes, balance, legendre, control, step_size, owner_slots):
+    _, lats, levels, lons = grad_grid.shape
+    owned, _, degrees = legendre.shape
+    wave_count = owner_slots.shape[0]
+    devices = wave_count // owned
+    lead = round_up(levels, 8)
+    grad = jnp.transpose(grad_grid[0], (1, 0, 2))
+    units = owned // 4
+    sizes = [2, units - 3, 1] if units > 3 else [units]
+    place = [Rows(lats, levels, size) for size in sizes]
+    members, first = [], 0
+    for size in sizes:
+        members.append(list(range(first, first + size)))
+        first += size
+    by_owner = owner_slots.reshape(devices, units, 4).transpose(1, 0, 2)
+
+    waves = [chosen_waves(by_owner[m[0] : m[-1] + 1].reshape(-1), wave_count, lons) for m in members]
+    mix = functools.partial(jnp.einsum, precision=highest)
+    adjoint_mat = jnp.concatenate(
+        [on_both(remap[0].T, lead), on_both(mix("ik,kj->ji", remap[0], balance), lead)]
+    )
+    mode_mat = on_both(modes[0].T, lead)
+    forward_mat = jnp.concatenate(
+        [on_both(modes[0], lead), on_both(mix("ik,kj->ij", balance, modes[0]), lead)]
+    )
+    remap_mat = on_both(remap[0], lead)
+    own_control = control[0].reshape(owned, 2, levels, degrees)
+    own_control = jnp.pad(own_control, ((0, 0), (0, 0), (0, lead - levels), (0, 0)))
+    own_control = own_control.reshape(owned, 2 * lead, degrees)
+    own, send, other, new, keep, back_send, back_other = ({} for _ in range(7))
+
+    def dft(c, *after):
+        coef, mark = forward_dft(grad, waves[c], place[c], after)
+        return coef.reshape(devices, 8, place[c].lanes), mark
+
+    def adjoint(c, got, *after):
+        for at, u in enumerate(members[c]):
+            own[u], send[u] = spectral(got, place[c], at, legendre, u, adjoint_mat, after)
+            other[u] = from_behind(send[u], "var", -1)
+
+    def gradient_step(c, *after):
+        for u in members[c]:
+            new[u], keep[u], back_send[u] = update(
+                step_size, own[u], other[u], own_control, u, mode_mat, forward_mat, after
+            )
+            back_other[u] = from_behind(back_send[u], "var", 1)
+
+    def forward(c, *after):
+        keeps, gots = [keep[u] for u in members[c]], [back_other[u] for u in members[c]]
+        return spectral_back(
+            keeps, gots, place[c], legendre, members[c][0], remap_mat, devices, after
+        )
+
+    def inverse(c, arrived, total, dtype, *after):
+        coef = arrived.reshape(LANES, place[c].lanes)
+        return inverse_dft(coef, place[c], waves[c], total, lats, dtype, after)
+
+    def all_new():
+        updated = jnp.concatenate([new[u] for u in range(units)]).reshape(owned, 2, lead, degrees)
+        return updated[:, :, :levels].reshape(owned, 2 * levels, degrees)
+
+    if len(sizes) == 3:
+        coef_a, _ = dft(0)
+        got_a = exchange(coef_a)
+        coef_b, _ = dft(1)
+        coef_c, mark = dft(2)
+        got_b = exchange(gate(coef_b, got_a, mark))
+        adjoint(0, got_a)
+        gradient_step(0)
+        back_a, mark = forward(0)
+        got_c = exchange(gate(coef_c, got_b, mark))
+        adjoint(1, got_b)
+        arrived_a = exchange(gate(back_a, got_c, *[own[u] for u in members[1]], other[members[1][0]]))
+        adjoint(2, got_c)
+        gradient_step(1)
+        back_b, _ = forward(1, own[members[2][0]])
+        arrived_b = exchange(gate(back_b, arrived_a, own[members[2][0]]))
+        gradient_step(2, arrived_a)
+        updated = all_new()
+        back_c, _ = forward(2)
+        total = inverse(0, arrived_a, None, jnp.float32)
+        arrived_c = exchange(gate(back_c, arrived_b, total, updated))
+        total = inverse(1, arrived_b, total, jnp.float32)
+        total = inverse(2, arrived_c, total, jnp.bfloat16)
+    else:
+        coef, _ = dft(0)
+        adjoint(0, exchange(coef))
+        gradient_step(0)
+        updated = all_new()
+        back, _ = forward(0)
+        total = inverse(0, exchange(back), None, jnp.bfloat16)
+    increment = jnp.transpose(total, (1, 0, 2))
+    return (updated[None], increment[None])
 
 
 def make_waves(owner_slots, lon_count):
@@ -22,7 +520,7 @@
     return jnp.stack([jnp.cos(angles), jnp.sin(angles)], axis=1) * factor
 
 
-def local(grad_grid, remap, modes, balance, legendre, control, step_size, owner_slots):
+def plain_local(grad_grid, remap, modes, balance, legendre, control, step_size, owner_slots):
     lat_rows = grad_grid.shape[1]
     levels = grad_grid.shape[2]
     lon_count = grad_grid.shape[3]
@@ -36,7 +534,7 @@
         "ik,lij->lkj", remap_var, grad_grid[0].astype(jnp.float32), precision=highest
     )
     slab_coef = jnp.einsum("lkj,jcs->slck", lifted, wave_table, precision=highest)
-    spectral = jnp.einsum(
+    spectral_coef = jnp.einsum(
         "sln,slq->sqn",
         legendre,
         lax.all_to_all(
@@ -48,14 +546,14 @@
         ),
         precision=highest,
     )
-    spec_four = spectral.reshape(owned_count, 2, levels, degrees)
+    spec_four = spectral_coef.reshape(owned_count, 2, levels, degrees)
     partner = from_behind(spec_four, "var", -1)
     blended = spec_four + jnp.einsum("ik,scin->sckn", balance, partner, precision=highest)
-    spectral = jnp.einsum("ik,scin->sckn", modes_var, blended, precision=highest).reshape(
+    spectral_coef = jnp.einsum("ik,scin->sckn", modes_var, blended, precision=highest).reshape(
         owned_count, 2 * levels, degrees
     )
     own_control = control[0]
-    updated = own_control - step_size[0] * (own_control + spectral)
+    updated = own_control - step_size[0] * (own_control + spectral_coef)
     level_coef = jnp.einsum(
         "ki,scin->sckn",
         modes_var,
@@ -73,6 +571,22 @@
         jnp.bfloat16
     )
     return (updated[None], increment[None])
+
+
+def local(*arrays):
+    grad_grid, legendre = arrays[0], arrays[4]
+    devices = legendre.shape[1] // grad_grid.shape[1]
+    levels = grad_grid.shape[2]
+    tail = grad_grid.shape[1] * levels % LANES
+    fits = (
+        legendre.shape[0] % 4 == 0
+        and grad_grid.shape[1] % 16 == 0
+        and devices * 8 == LANES
+        and round_up(levels, 8) <= LANES
+        and tail > 0
+        and LANES % tail == 0
+    )
+    return (tiled_local if fits else plain_local)(*arrays)
 
 
 def solution(mesh):

time: 1660 us -> 558 us (0.34)
  matrix products: 469 us -> 15.2 us
  blocking collectives: 413 us -> 0 us
  waiting for transfers between devices: 620 us -> 215 us
  Pallas kernels: 0 us -> 236 us
  local copies, waits for them, and re-layouts: 117 us -> 24.2 us
  starting transfers between devices: 12.1 us -> 58.1 us
    dot_general x10 -> x5, matrix products: 469 us -> 15.2 us  [the longest x3 14.7 us: chosen_waves(): jnp.dot(onehot, table, preferred_element_type=jnp.float32)]
    all_to_all x1 -> x0, blocking collectives: 413 us -> none  [local(): lax.all_to_all(slab_coef.reshape(wave_count, lat_rows, 2 * levels), 'lat'...]
    all_to_all x1 -> x6, waiting for transfers between devices: 397 us -> 123 us  [exchange(): return lax.all_to_all(block, 'lat', split_axis=0, concat_axis=0, tiled=True)]
    pallas_call x0 -> x26, Pallas kernels: none -> 236 us  [the longest x3 71.1 us: inverse_dft(): pl.pallas_call(behind(functools.partial(inverse_kernel, steps, place, len...]
    ppermute x2 -> x12, waiting for transfers between devices: 222 us -> 92.2 us  [from_behind(): return lax.ppermute(block, axis, route)]
    reshape x2 -> x3, local copies, waits for them, and re-layouts: 41.8 us -> 4.62 us  [the longest x1 3.72 us: all_new(): return updated[:, :, :levels].reshape(owned, 2 * levels, degrees)]
    all_to_all x1 -> x6, starting transfers between devices: 8.31 us -> 35.2 us  [exchange(): return lax.all_to_all(block, 'lat', split_axis=0, concat_axis=0, tiled=True)]
    all_to_all x2 -> x0, local copies, waits for them, and re-layouts: 24.4 us -> none  [the longest x1 17.5 us: local(): lax.all_to_all(fourier, 'lat', split_axis=1, concat_axis=0, tiled=True)]
  transfers between devices with their start and end apart: 3 -> 18, of which waited for: 3 -> 13; matrix products, arithmetic and copies ran while one was open for 1% -> 6% of each run, Pallas kernels for 0% -> 37%
where the time goes in v1:
time: 558 us; the launch traced here: 552 us
  Pallas kernels  236 us (42%)
  waiting for transfers between devices  215 us (39%)
  starting transfers between devices  58.1 us (10%)
  local copies, waits for them, and re-layouts  24.2 us (4%)
  matrix products  15.2 us (3%)
    all_to_all x6, waiting for transfers between devices, exchange(): return lax.all_to_all(block, 'lat', split_axis=0, concat_axis=0, tiled=True)  123 us
    ppermute x12, waiting for transfers between devices, from_behind(): return lax.ppermute(block, axis, route)  92.2 us
    pallas_call x3, Pallas kernels, inverse_dft(): pl.pallas_call(behind(functools.partial(inverse_kernel, steps, place, len...  71.1 us
    pallas_call x6, Pallas kernels, spectral(): pl.pallas_call(behind(functools.partial(spectral_kernel, place), 4, len(a...  49.1 us
    pallas_call x3, Pallas kernels, spectral_back(): pl.pallas_call(behind(functools.partial(back_kernel, place), 2 * units +...  43.6 us
    pallas_call x3, Pallas kernels, forward_dft(): pl.pallas_call(behind(functools.partial(dft_kernel, steps, place), 2, len...  41.5 us
    all_to_all x6, starting transfers between devices, exchange(): return lax.all_to_all(block, 'lat', split_axis=0, concat_axis=0, tiled=True)  35.2 us
    pallas_call x6, Pallas kernels, update(): pl.pallas_call(behind(update_kernel, 6, len(after)), grid=(1,), in_specs=...  30.5 us
  transfers between devices with their start and end apart: 18, of which 13 were waited for; matrix products, arithmetic and copies ran while one was open for 6% of the time, Pallas kernels for 37%

profile of v1, /device:TPU:15, one launch (start us, length us, event | category | flops | bytes accessed | tf_op | source)
XLA Modules:
  0.0 551.7 jit_solution(17966021383376828775)
XLA Ops:
  2.0 4.9 convolution_convert_fusion.1.refs_1_.refs_2_
  6.9 13.7 %forward_dft.3 = (f32[128,6784]{1,0:T(8,128)}, f32[8,128]{1,0:T(8,128)}) custom-call(bf16[70,48,1536]{2,1,0:T(8,128)(2,1)} %bitcast.44, bf16[256,3072]{1,0:T(8,128)(2,1)} %convolution_convert_fusion.1.refs_1_.refs_2_), custom_call_target="tpu_custom_call" | custom-call | flops 660602880 | tf_op jit(solution)/shard_map/forward_dft/pallas_call | solution.py:150
  20.6 6.9 %all-to-all-start = ((f32[16,8,6784]{2,1,0:T(8,128)}), f32[16,8,6784]{2,1,0:T(8,128)}, u32[]{:S(2)}, u32[]{:S(2)}) async-start(f32[16,8,6784]{2,1,0:T(8,128)} %bitcast.54), calls=%async_computation | async-start | bytes 6946816 | tf_op jit(solution)/shard_map/all_to_all | solution.py:417
  28.4 4.0 convolution_convert_fusion.2.refs_1_.refs_2_
  32.4 8.9 %forward_dft.5 = (f32[128,3456]{1,0:T(8,128)}, f32[8,128]{1,0:T(8,128)}) custom-call(bf16[70,48,1536]{2,1,0:T(8,128)(2,1)} %bitcast.45, bf16[128,3072]{1,0:T(8,128)(2,1)} %convolution_convert_fusion.2.refs_1_.refs_2_), custom_call_target="tpu_custom_call" | custom-call | flops 330301440 | tf_op jit(solution)/shard_map/forward_dft/pallas_call | solution.py:150
  41.3 5.7 %convolution_convert_fusion.refs_1_.refs_2_ = bf16[384,3072]{1,0:T(8,128)(2,1)} fusion(bf16[768,3072]{1,0:T(8,128)(2,1)} %constant.2.clone, s32[384]{0:T(512)S(1)} %add.81), kind=kOutput, calls=%fused_computation | convolution fusion | flops 1813413888 | bytes 7079424 | tf_op jit(solution)/shard_map/dot_general | solution.py:46
  47.0 18.9 %forward_dft.4 = (f32[128,10112]{1,0:T(8,128)}, f32[8,128]{1,0:T(8,128)}) custom-call(bf16[70,48,1536]{2,1,0:T(8,128)(2,1)} %bitcast.46, bf16[384,3072]{1,0:T(8,128)(2,1)} %convolution_convert_fusion.refs_1_.refs_2_), custom_call_target="tpu_custom_call" | custom-call | flops 990904320 | tf_op jit(solution)/shard_map/forward_dft/pallas_call | solution.py:150
  65.9 38.5 %all-to-all-done.refs_0_.refs_1_ = f32[16,8,6784]{2,1,0:T(8,128)} async-done(((f32[16,8,6784]{2,1,0:T(8,128)}), f32[16,8,6784]{2,1,0:T(8,128)}, u32[]{:S(2)}, u32[]{:S(2)}) %all-to-all-start) | async-done | bytes 3473440 | tf_op jit(solution)/shard_map/all_to_all | solution.py:417
  104.4 5.6 %all-to-all-start.1 = ((f32[16,8,10112]{2,1,0:T(8,128)}), f32[16,8,10112]{2,1,0:T(8,128)}, u32[]{:S(2)}, u32[]{:S(2)}) async-start(f32[16,8,10112]{2,1,0:T(8,128)} %gate.5), calls=%async_computation.1 | async-start | bytes 10354688 | tf_op jit(solution)/shard_map/all_to_all | solution.py:417
  110.8 1.0 broadcast_multiply_fusion
  112.9 8.1 %spectral_adjoint.6 = (f32[4,144,384]{2,1,0:T(8,128)}, f32[4,144,384]{2,1,0:T(8,128)}) custom-call(f32[16,8,6784]{2,1,0:T(8,128)} %all-to-all-done.refs_0_.refs_1_, f32[16,8,6784]{2,1,0:T(8,128)} %all-to-all-done.refs_0_.refs_1_, f32[24,768,384]{2,1,0:T(8,128)} %refs_6_.1, f32[288,144]{1,0:T(8,128)} %copy-done.4), custom_call_target="tpu_custom_call" | custom-call | flops 254803968 | tf_op jit(solution)/shard_map/spectral_adjoint/pallas_call | solution.py:209
  121.0 3.1 collective-permute-start
  124.1 8.2 %spectral_adjoint.7 = (f32[4,144,384]{2,1,0:T(8,128)}, f32[4,144,384]{2,1,0:T(8,128)}) custom-call(f32[16,8,6784]{2,1,0:T(8,128)} %all-to-all-done.refs_0_.refs_1_, f32[16,8,6784]{2,1,0:T(8,128)} %all-to-all-done.refs_0_.refs_1_, f32[24,768,384]{2,1,0:T(8,128)} %refs_6_.1, f32[288,144]{1,0:T(8,128)} %copy-done.4), custom_call_target="tpu_custom_call" | custom-call | flops 254803968 | tf_op jit(solution)/shard_map/spectral_adjoint/pallas_call | solution.py:209
  132.3 2.2 collective-permute-start.1
  136.2 3.5 copy.30
  139.7 2.7 pad.25
  143.2 5.1 gradient_step.6
  148.3 1.5 collective-permute-start.5
  149.8 11.3 %collective-permute-done.1.refs_2_ = f32[4,144,384]{2,1,0:T(8,128)} collective-permute-done((f32[4,144,384]{2,1,0:T(8,128)}, f32[4,144,384]{2,1,0:T(8,128)}, u32[]{:S(2)}, u32[]{:S(2)}) %collective-permute-start.1) | collective-permute-done | bytes 884768 | tf_op jit(solution)/shard_map/ppermute | solution.py:28
  161.1 5.0 gradient_step.7
  166.1 1.3 collective-permute-start.6
  167.4 1.7 mul.178.refs_5_.refs_3_.refs_7_
  169.1 1.6 collective-permute-done.5.refs_2_
  170.7 19.4 %collective-permute-done.6.refs_3_ = f32[4,144,384]{2,1,0:T(8,128)} collective-permute-done((f32[4,144,384]{2,1,0:T(8,128)}, f32[4,144,384]{2,1,0:T(8,128)}, u32[]{:S(2)}, u32[]{:S(2)}) %collective-permute-start.6) | collective-permute-done | bytes 884768 | tf_op jit(solution)/shard_map/ppermute | solution.py:28
  190.2 14.5 %spectral_forward.3 = (f32[16,8,6784]{2,1,0:T(8,128)}, f32[8,128]{1,0:T(8,128)}) custom-call(f32[4,144,384]{2,1,0:T(8,128)} %get-tuple-element.59.refs_0_, f32[4,144,384]{2,1,0:T(8,128)} %get-tuple-element.60.refs_1_, f32[4,144,384]{2,1,0:T(8,128)} %copy-done.8, f32[4,144,384]{2,1,0:T(8,128)} %collective-permute-done.6.refs_3_, f32[24,768,384]{2,1,0:T(8,128)} %refs_6_.1, ...), custom_call_target="tpu_custom_call" | custom-call | flops 509607936 | tf_op jit(solution)/shard_map/spectral_forward/pallas_call | solution.py:327
  204.6 18.8 %all-to-all-done.1.refs_0_.refs_1_ = f32[16,8,10112]{2,1,0:T(8,128)} async-done(((f32[16,8,10112]{2,1,0:T(8,128)}), f32[16,8,10112]{2,1,0:T(8,128)}, u32[]{:S(2)}, u32[]{:S(2)}) %all-to-all-start.1) | async-done | bytes 5177376 | tf_op jit(solution)/shard_map/all_to_all | solution.py:417
  223.4 5.2 all-to-all-start.2
  228.7 8.3 %spectral_adjoint.8 = (f32[4,144,384]{2,1,0:T(8,128)}, f32[4,144,384]{2,1,0:T(8,128)}) custom-call(f32[16,8,10112]{2,1,0:T(8,128)} %all-to-all-done.1.refs_0_.refs_1_, f32[16,8,10112]{2,1,0:T(8,128)} %all-to-all-done.1.refs_0_.refs_1_, f32[24,768,384]{2,1,0:T(8,128)} %refs_6_.1, f32[288,144]{1,0:T(8,128)} %copy-done.4), custom_call_target="tpu_custom_call" | custom-call | flops 254803968 | tf_op jit(solution)/shard_map/spectral_adjoint/pallas_call | solution.py:209
  237.0 2.2 collective-permute-start.2
  239.2 8.2 %spectral_adjoint.10 = (f32[4,144,384]{2,1,0:T(8,128)}, f32[4,144,384]{2,1,0:T(8,128)}) custom-call(f32[16,8,10112]{2,1,0:T(8,128)} %all-to-all-done.1.refs_0_.refs_1_, f32[16,8,10112]{2,1,0:T(8,128)} %all-to-all-done.1.refs_0_.refs_1_, f32[24,768,384]{2,1,0:T(8,128)} %refs_6_.1, f32[288,144]{1,0:T(8,128)} %copy-done.4), custom_call_target="tpu_custom_call" | custom-call | flops 254803968 | tf_op jit(solution)/shard_map/spectral_adjoint/pallas_call | solution.py:209
  247.4 8.2 %spectral_adjoint.9 = (f32[4,144,384]{2,1,0:T(8,128)}, f32[4,144,384]{2,1,0:T(8,128)}) custom-call(f32[16,8,10112]{2,1,0:T(8,128)} %all-to-all-done.1.refs_0_.refs_1_, f32[16,8,10112]{2,1,0:T(8,128)} %all-to-all-done.1.refs_0_.refs_1_, f32[24,768,384]{2,1,0:T(8,128)} %refs_6_.1, f32[288,144]{1,0:T(8,128)} %copy-done.4), custom_call_target="tpu_custom_call" | custom-call | flops 254803968 | tf_op jit(solution)/shard_map/spectral_adjoint/pallas_call | solution.py:209
  255.5 2.6 collective-permute-done.2.refs_2_.refs_5_
  258.1 10.9 %all-to-all-done.2.refs_0_.refs_1_ = f32[16,8,3456]{2,1,0:T(8,128)} async-done(((f32[16,8,3456]{2,1,0:T(8,128)}), f32[16,8,3456]{2,1,0:T(8,128)}, u32[]{:S(2)}, u32[]{:S(2)}) %all-to-all-start.2) | async-done | bytes 1769504 | tf_op jit(solution)/shard_map/all_to_all | solution.py:417
  269.0 4.9 all-to-all-start.3
  273.9 3.1 collective-permute-start.3
  277.0 2.6 collective-permute-start.4
  279.6 5.1 gradient_step.8
  284.7 1.3 collective-permute-start.9
  286.0 9.1 %collective-permute-done.3.refs_2_ = f32[4,144,384]{2,1,0:T(8,128)} collective-permute-done((f32[4,144,384]{2,1,0:T(8,128)}, f32[4,144,384]{2,1,0:T(8,128)}, u32[]{:S(2)}, u32[]{:S(2)}) %collective-permute-start.3) | collective-permute-done | bytes 884768 | tf_op jit(solution)/shard_map/ppermute | solution.py:28
  295.0 5.1 gradient_step.9
  300.1 1.3 collective-permute-start.10
  301.4 12.6 %collective-permute-done.4.refs_2_ = f32[4,144,384]{2,1,0:T(8,128)} collective-permute-done((f32[4,144,384]{2,1,0:T(8,128)}, f32[4,144,384]{2,1,0:T(8,128)}, u32[]{:S(2)}, u32[]{:S(2)}) %collective-permute-start.4) | collective-permute-done | bytes 884768 | tf_op jit(solution)/shard_map/ppermute | solution.py:28
  314.0 5.0 gradient_step.10
  319.0 1.3 collective-permute-start.11
  320.3 8.1 %spectral_adjoint.11 = (f32[4,144,384]{2,1,0:T(8,128)}, f32[4,144,384]{2,1,0:T(8,128)}) custom-call(f32[16,8,3456]{2,1,0:T(8,128)} %all-to-all-done.2.refs_0_.refs_1_, f32[16,8,3456]{2,1,0:T(8,128)} %all-to-all-done.2.refs_0_.refs_1_, f32[24,768,384]{2,1,0:T(8,128)} %refs_6_.1, f32[288,144]{1,0:T(8,128)} %copy-done.4), custom_call_target="tpu_custom_call" | custom-call | flops 254803968 | tf_op jit(solution)/shard_map/spectral_adjoint/pallas_call | solution.py:209
  328.5 16.9 %collective-permute-done.11.refs_5_ = f32[4,144,384]{2,1,0:T(8,128)} collective-permute-done((f32[4,144,384]{2,1,0:T(8,128)}, f32[4,144,384]{2,1,0:T(8,128)}, u32[]{:S(2)}, u32[]{:S(2)}) %collective-permute-start.11) | collective-permute-done | bytes 884768 | tf_op jit(solution)/shard_map/ppermute | solution.py:28
  345.4 20.5 %spectral_forward.5 = (f32[16,8,10112]{2,1,0:T(8,128)}, f32[8,128]{1,0:T(8,128)}) custom-call(f32[4,144,384]{2,1,0:T(8,128)} %get-tuple-element.71.refs_0_, f32[4,144,384]{2,1,0:T(8,128)} %get-tuple-element.72.refs_1_, f32[4,144,384]{2,1,0:T(8,128)} %get-tuple-element.73.refs_2_, f32[4,144,384]{2,1,0:T(8,128)} %copy-done.6, ...), custom_call_target="tpu_custom_call" | custom-call | flops 764411904 | tf_op jit(solution)/shard_map/spectral_forward/pallas_call | solution.py:327
  365.8 7.3 %all-to-all-start.4 = ((f32[16,8,10112]{2,1,0:T(8,128)}), f32[16,8,10112]{2,1,0:T(8,128)}, u32[]{:S(2)}, u32[]{:S(2)}) async-start(f32[16,8,10112]{2,1,0:T(8,128)} %gate.8), calls=%async_computation.4 | async-start | bytes 10354688 | tf_op jit(solution)/shard_map/all_to_all | solution.py:417
  373.2 1.3 collective-permute-start.7
  374.5 18.7 %collective-permute-done.7.refs_2_ = f32[4,144,384]{2,1,0:T(8,128)S(1)} collective-permute-done((f32[4,144,384]{2,1,0:T(8,128)S(1)}, f32[4,144,384]{2,1,0:T(8,128)S(1)}, u32[]{:S(2)}, u32[]{:S(2)}) %collective-permute-start.7) | collective-permute-done | bytes 884768 | tf_op jit(solution)/shard_map/ppermute | solution.py:28
  394.2 5.1 gradient_step.11
  399.3 1.8 collective-permute-start.8
  401.0 1.2 constant_dynamic-update-slice_fusion.9
  402.3 1.2 constant_dynamic-update-slice_fusion.8
  403.5 1.2 constant_dynamic-update-slice_fusion.7
  405.0 1.7 copy.38
  406.6 3.7 copy.35.refs_3_
  410.6 20.6 %inverse_dft.3.refs_2_.refs_3_ = f32[70,48,1536]{2,1,0:T(8,128)} custom-call(f32[128,6784]{1,0:T(8,128)} %bitcast.13.refs_0_, bf16[256,3072]{1,0:T(8,128)(2,1)} %convolution_convert_fusion.1.refs_1_.refs_2_, bf16[256,3072]{1,0:T(8,128)(2,1)} %convolution_convert_fusion.1.refs_1_.refs_2_), custom_call_target="tpu_custom_call" | custom-call | flops 990904320 | tf_op jit(solution)/shard_map/inverse_dft/pallas_call | solution.py:386
  432.1 8.7 %spectral_forward.4 = (f32[16,8,3456]{2,1,0:T(8,128)}, f32[8,128]{1,0:T(8,128)}) custom-call(f32[4,144,384]{2,1,0:T(8,128)} %get-tuple-element.68.refs_0_, f32[4,144,384]{2,1,0:T(8,128)} %copy-done.7, f32[24,768,384]{2,1,0:T(8,128)} %refs_6_.1, f32[144,144]{1,0:T(8,128)} %mul.178.refs_5_.refs_3_.refs_7_), custom_call_target="tpu_custom_call" | custom-call | flops 254803968 | tf_op jit(solution)/shard_map/spectral_forward/pallas_call | solution.py:327
  440.8 45.9 %all-to-all-done.4.refs_1_ = f32[16,8,10112]{2,1,0:T(8,128)} async-done(((f32[16,8,10112]{2,1,0:T(8,128)}), f32[16,8,10112]{2,1,0:T(8,128)}, u32[]{:S(2)}, u32[]{:S(2)}) %all-to-all-start.4) | async-done | bytes 5177376 | tf_op jit(solution)/shard_map/all_to_all | solution.py:417
  486.7 5.3 all-to-all-start.5
  492.0 31.6 %inverse_dft.4.refs_3_ = f32[70,48,1536]{2,1,0:T(8,128)} custom-call(f32[128,10112]{1,0:T(8,128)} %bitcast.16.refs_0_, bf16[384,3072]{1,0:T(8,128)(2,1)} %convolution_convert_fusion.refs_1_.refs_2_, bf16[384,3072]{1,0:T(8,128)(2,1)} %convolution_convert_fusion.refs_1_.refs_2_, f32[70,48,1536]{2,1,0:T(8,128)} %inverse_dft.3.refs_2_.refs_3_), custom_call_target="tpu_custom_call" | custom-call | flops 1486356480 | tf_op jit(solution)/shard_map/inverse_dft/pallas_call | solution.py:386
  523.6 8.7 %all-to-all-done.5 = f32[16,8,3456]{2,1,0:T(8,128)} async-done(((f32[16,8,3456]{2,1,0:T(8,128)}), f32[16,8,3456]{2,1,0:T(8,128)}, u32[]{:S(2)}, u32[]{:S(2)}) %all-to-all-start.5) | async-done | bytes 1769504 | tf_op jit(solution)/shard_map/all_to_all | solution.py:417
  532.4 18.9 %inverse_dft.5 = bf16[70,48,1536]{2,1,0:T(8,128)(2,1)} custom-call(f32[128,3456]{1,0:T(8,128)} %bitcast.15.refs_0_, bf16[128,3072]{1,0:T(8,128)(2,1)} %convolution_convert_fusion.2.refs_1_.refs_2_, bf16[128,3072]{1,0:T(8,128)(2,1)} %convolution_convert_fusion.2.refs_1_.refs_2_, f32[70,48,1536]{2,1,0:T(8,128)} %inverse_dft.4.refs_3_), custom_call_target="tpu_custom_call" | custom-call | flops 495452160 | tf_op jit(solution)/shard_map/inverse_dft/pallas_call | solution.py:386
  (84 shorter events, 8.0 us)
Async XLA Ops:
  0.6 109.6 %copy-start = (f32[70,70]{1,0:T(8,128)S(1)}, f32[70,70]{1,0:T(8,128)}, u32[]{:S(2)}) copy-start(f32[70,70]{1,0:T(8,128)} %param.12) | copy-start | bytes 58804
  20.6 83.8 %all-to-all-start = ((f32[16,8,6784]{2,1,0:T(8,128)}), f32[16,8,6784]{2,1,0:T(8,128)}, u32[]{:S(2)}, u32[]{:S(2)}) async-start(f32[16,8,6784]{2,1,0:T(8,128)} %bitcast.54), calls=%async_computation | async-start | bytes 6946816 | tf_op jit(solution)/shard_map/all_to_all | solution.py:417
  104.4 5.6 %copy-start.14 = (f32[1,70,70]{2,0,1:T(1,128)S(1)}, f32[1,70,70]{2,0,1:T(1,128)}, u32[]{:S(2)}) copy-start(f32[1,70,70]{2,0,1:T(1,128)} %param.10) | copy-start | bytes 58804
  104.4 5.7 %copy-start.13 = (f32[1,70,70]{2,0,1:T(1,128)S(1)}, f32[1,70,70]{2,0,1:T(1,128)}, u32[]{:S(2)}) copy-start(f32[1,70,70]{2,0,1:T(1,128)} %param.11) | copy-start | bytes 58804
  104.4 119.0 %all-to-all-start.1 = ((f32[16,8,10112]{2,1,0:T(8,128)}), f32[16,8,10112]{2,1,0:T(8,128)}, u32[]{:S(2)}, u32[]{:S(2)}) async-start(f32[16,8,10112]{2,1,0:T(8,128)} %gate.5), calls=%async_computation.1 | async-start | bytes 10354688 | tf_op jit(solution)/shard_map/all_to_all | solution.py:417
  112.1 0.8 copy-start.4
  121.0 21.5 %collective-permute-start = (f32[4,144,384]{2,1,0:T(8,128)}, f32[4,144,384]{2,1,0:T(8,128)}, u32[]{:S(2)}, u32[]{:S(2)}) collective-permute-start(f32[4,144,384]{2,1,0:T(8,128)} %get-tuple-element.42), channel_id=1, source_target_pairs={{16,0},{17,1},{18,2},{19,3},{20,4},{21,5},{22,6},{23,7},{24,8},{25... | collective-permute-start | bytes 2654216 | tf_op jit(solution)/shard_map/ppermute | solution.py:28
  132.3 28.8 %collective-permute-start.1 = (f32[4,144,384]{2,1,0:T(8,128)}, f32[4,144,384]{2,1,0:T(8,128)}, u32[]{:S(2)}, u32[]{:S(2)}) collective-permute-start(f32[4,144,384]{2,1,0:T(8,128)} %get-tuple-element.45), channel_id=1, source_target_pairs={{16,0},{17,1},{18,2},{19,3},{20,4},{21,5},{22,6},{23,7},{24,8},{25... | collective-permute-start | bytes 2654216 | tf_op jit(solution)/shard_map/ppermute | solution.py:28
  142.5 0.7 copy-start.3
  148.3 22.4 %collective-permute-start.5 = (f32[4,144,384]{2,1,0:T(8,128)}, f32[4,144,384]{2,1,0:T(8,128)S(1)}, u32[]{:S(2)}, u32[]{:S(2)}) collective-permute-start(f32[4,144,384]{2,1,0:T(8,128)} %get-tuple-element.61), channel_id=1, source_target_pairs={{0,16},{1,17},{2,18},{3,19},{4,20},{5,21},{6,22},{7,23},{8,24},{9,... | collective-permute-start | bytes 2654216 | tf_op jit(solution)/shard_map/ppermute | solution.py:28
  166.1 24.1 %collective-permute-start.6 = (f32[4,144,384]{2,1,0:T(8,128)}, f32[4,144,384]{2,1,0:T(8,128)}, u32[]{:S(2)}, u32[]{:S(2)}) collective-permute-start(f32[4,144,384]{2,1,0:T(8,128)} %get-tuple-element.62), channel_id=1, source_target_pairs={{0,16},{1,17},{2,18},{3,19},{4,20},{5,21},{6,22},{7,23},{8,24},{9,... | collective-permute-start | bytes 2654216 | tf_op jit(solution)/shard_map/ppermute | solution.py:28
  170.7 19.4 %copy-start.8 = (f32[4,144,384]{2,1,0:T(8,128)}, f32[4,144,384]{2,1,0:T(8,128)S(1)}, u32[]{:S(2)}) copy-start(f32[4,144,384]{2,1,0:T(8,128)S(1)} %collective-permute-done.5.refs_2_) | copy-start | bytes 2654212
  223.4 45.6 %all-to-all-start.2 = ((f32[16,8,3456]{2,1,0:T(8,128)}), f32[16,8,3456]{2,1,0:T(8,128)}, u32[]{:S(2)}, u32[]{:S(2)}) async-start(f32[16,8,3456]{2,1,0:T(8,128)} %gate.6), calls=%async_computation.2 | async-start | bytes 3538944 | tf_op jit(solution)/shard_map/all_to_all | solution.py:417
  237.0 21.1 %collective-permute-start.2 = (f32[4,144,384]{2,1,0:T(8,128)}, f32[4,144,384]{2,1,0:T(8,128)S(1)}, u32[]{:S(2)}, u32[]{:S(2)}) collective-permute-start(f32[4,144,384]{2,1,0:T(8,128)} %get-tuple-element.50), channel_id=1, source_target_pairs={{16,0},{17,1},{18,2},{19,3},{20,4},{21,5},{22,6},{23,7},{24,8},{25... | collective-permute-start | bytes 2654216 | tf_op jit(solution)/shard_map/ppermute | solution.py:28
  258.1 10.9 %copy-start.5 = (f32[4,144,384]{2,1,0:T(8,128)}, f32[4,144,384]{2,1,0:T(8,128)S(1)}, u32[]{:S(2)}) copy-start(f32[4,144,384]{2,1,0:T(8,128)S(1)} %collective-permute-done.2.refs_2_.refs_5_) | copy-start | bytes 2654212
  269.0 96.8 %all-to-all-start.3 = ((f32[16,8,6784]{2,1,0:T(8,128)}), f32[16,8,6784]{2,1,0:T(8,128)}, u32[]{:S(2)}, u32[]{:S(2)}) async-start(f32[16,8,6784]{2,1,0:T(8,128)} %gate.7), calls=%async_computation.3 | async-start | bytes 6946816 | tf_op jit(solution)/shard_map/all_to_all | solution.py:417
  273.9 21.1 %collective-permute-start.3 = (f32[4,144,384]{2,1,0:T(8,128)}, f32[4,144,384]{2,1,0:T(8,128)}, u32[]{:S(2)}, u32[]{:S(2)}) collective-permute-start(f32[4,144,384]{2,1,0:T(8,128)} %get-tuple-element.53), channel_id=1, source_target_pairs={{16,0},{17,1},{18,2},{19,3},{20,4},{21,5},{22,6},{23,7},{24,8},{25... | collective-permute-start | bytes 2654216 | tf_op jit(solution)/shard_map/ppermute | solution.py:28
  277.0 37.0 %collective-permute-start.4 = (f32[4,144,384]{2,1,0:T(8,128)}, f32[4,144,384]{2,1,0:T(8,128)}, u32[]{:S(2)}, u32[]{:S(2)}) collective-permute-start(f32[4,144,384]{2,1,0:T(8,128)} %get-tuple-element.56), channel_id=1, source_target_pairs={{16,0},{17,1},{18,2},{19,3},{20,4},{21,5},{22,6},{23,7},{24,8},{25... | collective-permute-start | bytes 2654216 | tf_op jit(solution)/shard_map/ppermute | solution.py:28
  284.7 43.8 %collective-permute-start.9 = (f32[4,144,384]{2,1,0:T(8,128)}, f32[4,144,384]{2,1,0:T(8,128)S(1)}, u32[]{:S(2)}, u32[]{:S(2)}) collective-permute-start(f32[4,144,384]{2,1,0:T(8,128)} %get-tuple-element.74), channel_id=1, source_target_pairs={{0,16},{1,17},{2,18},{3,19},{4,20},{5,21},{6,22},{7,23},{8,24},{9,... | collective-permute-start | bytes 2654216 | tf_op jit(solution)/shard_map/ppermute | solution.py:28
  300.1 28.3 %collective-permute-start.10 = (f32[4,144,384]{2,1,0:T(8,128)}, f32[4,144,384]{2,1,0:T(8,128)}, u32[]{:S(2)}, u32[]{:S(2)}) collective-permute-start(f32[4,144,384]{2,1,0:T(8,128)} %get-tuple-element.75), channel_id=1, source_target_pairs={{0,16},{1,17},{2,18},{3,19},{4,20},{5,21},{6,22},{7,23},{8,24},{9,... | collective-permute-start | bytes 2654216 | tf_op jit(solution)/shard_map/ppermute | solution.py:28
  319.0 26.3 %collective-permute-start.11 = (f32[4,144,384]{2,1,0:T(8,128)}, f32[4,144,384]{2,1,0:T(8,128)}, u32[]{:S(2)}, u32[]{:S(2)}) collective-permute-start(f32[4,144,384]{2,1,0:T(8,128)} %get-tuple-element.76), channel_id=1, source_target_pairs={{0,16},{1,17},{2,18},{3,19},{4,20},{5,21},{6,22},{7,23},{8,24},{9,... | collective-permute-start | bytes 2654216 | tf_op jit(solution)/shard_map/ppermute | solution.py:28
  328.5 16.9 %copy-start.6 = (f32[4,144,384]{2,1,0:T(8,128)}, f32[4,144,384]{2,1,0:T(8,128)S(1)}, u32[]{:S(2)}) copy-start(f32[4,144,384]{2,1,0:T(8,128)S(1)} %collective-permute-done.9.refs_3_) | copy-start | bytes 2654212
  365.8 7.3 %copy-start.15 = (f32[4,144,384]{2,1,0:T(8,128)S(1)}, f32[4,144,384]{2,1,0:T(8,128)}, u32[]{:S(2)}) copy-start(f32[4,144,384]{2,1,0:T(8,128)} %get-tuple-element.65) | copy-start | bytes 2654212
  365.8 120.8 %all-to-all-start.4 = ((f32[16,8,10112]{2,1,0:T(8,128)}), f32[16,8,10112]{2,1,0:T(8,128)}, u32[]{:S(2)}, u32[]{:S(2)}) async-start(f32[16,8,10112]{2,1,0:T(8,128)} %gate.8), calls=%async_computation.4 | async-start | bytes 10354688 | tf_op jit(solution)/shard_map/all_to_all | solution.py:417
  373.2 20.1 %collective-permute-start.7 = (f32[4,144,384]{2,1,0:T(8,128)S(1)}, f32[4,144,384]{2,1,0:T(8,128)S(1)}, u32[]{:S(2)}, u32[]{:S(2)}) collective-permute-start(f32[4,144,384]{2,1,0:T(8,128)S(1)} %copy-done.15), channel_id=1, source_target_pairs={{16,0},{17,1},{18,2},{19,3},{20,4},{21,5},{22,6},{23,7},{24,8},{25... | collective-permute-start | bytes 2654216 | tf_op jit(solution)/shard_map/ppermute | solution.py:28
  393.3 0.9 copy-start.12
  399.2 5.5 copy-start.9
  399.3 5.6 %copy-start.10 = (f32[4,144,384]{2,1,0:T(8,128)S(1)}, f32[4,144,384]{2,1,0:T(8,128)}, u32[]{:S(2)}) copy-start(f32[4,144,384]{2,1,0:T(8,128)} %get-tuple-element.57) | copy-start | bytes 2654212
  399.3 5.6 %copy-start.11 = (f32[4,144,384]{2,1,0:T(8,128)S(1)}, f32[4,144,384]{2,1,0:T(8,128)}, u32[]{:S(2)}) copy-start(f32[4,144,384]{2,1,0:T(8,128)} %get-tuple-element.67) | copy-start | bytes 2654212
  399.3 31.9 %collective-permute-start.8 = (f32[4,144,384]{2,1,0:T(8,128)}, f32[4,144,384]{2,1,0:T(8,128)S(1)}, u32[]{:S(2)}, u32[]{:S(2)}) collective-permute-start(f32[4,144,384]{2,1,0:T(8,128)} %get-tuple-element.69), channel_id=1, source_target_pairs={{0,16},{1,17},{2,18},{3,19},{4,20},{5,21},{6,22},{7,23},{8,24},{9,... | collective-permute-start | bytes 2654216 | tf_op jit(solution)/shard_map/ppermute | solution.py:28
  406.6 3.9 copy-start.2
  431.1 0.9 copy-start.7
  486.7 45.7 %all-to-all-start.5 = ((f32[16,8,3456]{2,1,0:T(8,128)}), f32[16,8,3456]{2,1,0:T(8,128)}, u32[]{:S(2)}, u32[]{:S(2)}) async-start(f32[16,8,3456]{2,1,0:T(8,128)} %gate.9), calls=%async_computation.5 | async-start | bytes 3538944 | tf_op jit(solution)/shard_map/all_to_all | solution.py:417
  532.3 18.9 %copy-start.1 = (f32[70,70]{1,0:T(8,128)S(1)}, f32[70,70]{1,0:T(8,128)}, u32[]{:S(2)}) copy-start(f32[70,70]{1,0:T(8,128)} %param.12) | copy-start | bytes 58804

commit v2 on v1

--- a/solution.py
+++ b/solution.py
@@ -4,7 +4,6 @@
 
 import jax
 import jax.numpy as jnp
-import numpy as np
 from jax import lax
 from jax.experimental import pallas as pl
 from jax.experimental.pallas import tpu as pltpu
@@ -28,22 +27,22 @@
     return lax.ppermute(block, axis, route)
 
 
-@functools.lru_cache(maxsize=None)
-def natural_waves(wave_count, lon_count):
-    phases = np.arange(wave_count)[:, None] * np.arange(lon_count)[None, :] % lon_count
-    angles = phases * (2.0 * math.pi / lon_count)
-    table = np.stack([np.cos(angles), np.sin(angles)], axis=1) * math.sqrt(2.0 / lon_count)
-    table = table.reshape(2 * wave_count, lon_count).astype(np.float32)
-    upper = table.astype(jnp.bfloat16)
-    lower = (table - upper.astype(np.float32)).astype(jnp.bfloat16)
-    return np.concatenate([upper, lower], axis=1)
-
-
-def chosen_waves(slots, wave_count, lon_count):
-    rows = (2 * slots[:, None] + lax.iota(jnp.int32, 2)[None, :]).reshape(-1)
-    onehot = (rows[:, None] == lax.iota(jnp.int32, 2 * wave_count)[None, :]).astype(jnp.bfloat16)
-    table = jnp.asarray(natural_waves(wave_count, lon_count))
-    return jnp.dot(onehot, table, preferred_element_type=jnp.float32).astype(jnp.bfloat16)
+def sine(x):
+    square = x * x
+    tail = 1.0
+    for divisor in (156, 110, 72, 42, 20, 6):
+        tail = 1.0 - square * (tail * (1.0 / divisor))
+    return x * tail
+
+
+def wave_rows(slots, lons):
+    shape = (slots.shape[0], lons)
+    lon = lax.broadcasted_iota(jnp.int32, shape, 1)
+    part = lax.broadcasted_iota(jnp.int32, shape, 0) % 2
+    phase = (slots * lon - part * (lons // 4)).astype(jnp.float32)
+    phase = phase - jnp.floor(phase * (1.0 / lons)) * lons
+    half = sine((phase - lons / 2) * (math.pi / lons))
+    return (2.0 * half * half - 1.0) * math.sqrt(2.0 / lons)
 
 
 def halves(x):
@@ -114,11 +113,18 @@
         return pieces
 
 
-def dft_kernel(steps, place, grad_ref, wave_ref, out_ref, mark_ref, rows_ref):
+def dft_kernel(steps, place, slot_ref, grad_ref, out_ref, wave_ref, mark_ref, rows_ref):
     mark_ref[...] = jnp.zeros(mark_ref.shape, jnp.float32)
     levels, lats, lons = grad_ref.shape
     waves = wave_ref.shape[0]
     lead = rows_ref.shape[1] // lats
+
+    @pl.when(pl.program_id(0) == 0)
+    def _():
+        for unit in range(place.units):
+            at = slice(unit * LANES, (unit + 1) * LANES)
+            wave_ref[at, :lons], wave_ref[at, lons:] = halves(wave_rows(slot_ref[at, :], lons))
+
     grad = grad_ref[...].reshape(levels * lats, lons)
     terms = mxu(grad, jnp.concatenate([wave_ref[:, :lons], wave_ref[:, lons:]], axis=0), NT)
     coef = terms[:, :waves] + terms[:, waves:]
@@ -141,9 +147,9 @@
                         out_ref[:, lanes] = part[:, chosen]
 
 
-def forward_dft(grad, table, place, after):
+def forward_dft(slots, grad, place, after):
     levels, lats, lons = grad.shape
-    waves = table.shape[0]
+    waves = slots.shape[0]
     block = 16
     steps = lats // block
     lead = round_up(levels, 8)
@@ -151,17 +157,25 @@
         behind(functools.partial(dft_kernel, steps, place), 2, len(after)),
         grid=(steps,),
         in_specs=[
+            pl.BlockSpec(slots.shape, lambda i: (0, 0)),
             pl.BlockSpec((levels, block, lons), lambda i: (0, i, 0)),
-            pl.BlockSpec(table.shape, lambda i: (0, 0)),
             *anywhere(after),
         ],
-        out_specs=[pl.BlockSpec((LANES, place.lanes), lambda i: (0, 0)), MARK_SPEC],
-        out_shape=[jax.ShapeDtypeStruct((LANES, place.lanes), jnp.float32), MARK],
+        out_specs=[
+            pl.BlockSpec((LANES, place.lanes), lambda i: (0, 0)),
+            pl.BlockSpec((waves, 2 * lons), lambda i: (0, 0)),
+            MARK_SPEC,
+        ],
+        out_shape=[
+            jax.ShapeDtypeStruct((LANES, place.lanes), jnp.float32),
+            jax.ShapeDtypeStruct((waves, 2 * lons), jnp.bfloat16),
+            MARK,
+        ],
         scratch_shapes=[pltpu.VMEM((place.units, lead * block, LANES), jnp.float32)],
         compiler_params=pltpu.CompilerParams(vmem_limit_bytes=VMEM_BYTES),
         cost_estimate=cost(4 * levels * lats * lons * waves),
         name="forward_dft",
-    )(grad, table, *after)
+    )(slots, grad, *after)
 
 
 def spectral_kernel(place, got_ref, end_ref, leg_ref, mat_ref, own_ref, send_ref, flat_ref, cols_ref):
@@ -354,7 +368,7 @@
 
     for step in range(steps):
 
-        @pl.when((pl.program_id(0) == step) & (pl.program_id(1) == 0))
+        @pl.when(pl.program_id(0) == step)
         def _(step=step):
             for unit in range(place.units):
                 for lat in range(lats):
@@ -366,11 +380,14 @@
                     start = term * waves + unit * LANES
                     left_ref[:, start : start + LANES] = value
 
-    right = jnp.concatenate([up_ref[...], up_ref[...], low_ref[...]], axis=0)
-    result = mxu(left_ref[...], right, NN).reshape(levels, lats, columns)
-    if has_total:
-        result = result + total_ref[...]
-    out_ref[...] = result.astype(out_ref.dtype)
+    width = 512 if columns % 512 == 0 else columns
+    for first in range(0, columns, width):
+        at = slice(first, first + width)
+        right = jnp.concatenate([up_ref[:, at], up_ref[:, at], low_ref[:, at]], axis=0)
+        result = mxu(left_ref[...], right, NN).reshape(levels, lats, width)
+        if has_total:
+            result = result + total_ref[:, :, at]
+        out_ref[:, :, at] = result.astype(out_ref.dtype)
 
 
 def inverse_dft(coef, place, table, total, lats, dtype, after):
@@ -379,17 +396,15 @@
     levels = place.levels
     block = 16
     steps = lats // block
-    columns = 512 if lons % 512 == 0 else lons
-    turns = lons // columns
-    grid_spec = pl.BlockSpec((levels, block, columns), lambda i, j: (0, i, j))
+    grid_spec = pl.BlockSpec((levels, block, lons), lambda i: (0, i, 0))
     totals = [] if total is None else [total]
     return pl.pallas_call(
         behind(functools.partial(inverse_kernel, steps, place, len(totals)), 3 + len(totals), len(after)),
-        grid=(steps, turns),
+        grid=(steps,),
         in_specs=[
-            pl.BlockSpec(coef.shape, lambda i, j: (0, 0)),
-            pl.BlockSpec((waves, columns), lambda i, j: (0, j)),
-            pl.BlockSpec((waves, columns), lambda i, j: (0, j + turns)),
+            pl.BlockSpec(coef.shape, lambda i: (0, 0)),
+            pl.BlockSpec((waves, lons), lambda i: (0, 0)),
+            pl.BlockSpec((waves, lons), lambda i: (0, 1)),
         ]
         + [grid_spec] * len(totals)
         + anywhere(after),
@@ -425,7 +440,7 @@
     lead = round_up(levels, 8)
     grad = jnp.transpose(grad_grid[0], (1, 0, 2))
     units = owned // 4
-    sizes = [2, units - 3, 1] if units > 3 else [units]
+    sizes = [1, units - 3, 2] if units > 3 else [units]
     place = [Rows(lats, levels, size) for size in sizes]
     members, first = [], 0
     for size in sizes:
@@ -433,7 +448,8 @@
         first += size
     by_owner = owner_slots.reshape(devices, units, 4).transpose(1, 0, 2)
 
-    waves = [chosen_waves(by_owner[m[0] : m[-1] + 1].reshape(-1), wave_count, lons) for m in members]
+    row_slots = jnp.repeat(by_owner.reshape(units * LANES // 2), 2)[:, None]
+    waves = {}
     mix = functools.partial(jnp.einsum, precision=highest)
     adjoint_mat = jnp.concatenate(
         [on_both(remap[0].T, lead), on_both(mix("ik,kj->ji", remap[0], balance), lead)]
@@ -449,19 +465,22 @@
     own, send, other, new, keep, back_send, back_other = ({} for _ in range(7))
 
     def dft(c, *after):
-        coef, mark = forward_dft(grad, waves[c], place[c], after)
+        rows = slice(members[c][0] * LANES, (members[c][-1] + 1) * LANES)
+        coef, waves[c], mark = forward_dft(row_slots[rows], grad, place[c], after)
         return coef.reshape(devices, 8, place[c].lanes), mark
 
     def adjoint(c, got, *after):
         for at, u in enumerate(members[c]):
             own[u], send[u] = spectral(got, place[c], at, legendre, u, adjoint_mat, after)
             other[u] = from_behind(send[u], "var", -1)
+            after = (own[u],)
 
     def gradient_step(c, *after):
         for u in members[c]:
             new[u], keep[u], back_send[u] = update(
                 step_size, own[u], other[u], own_control, u, mode_mat, forward_mat, after
             )
+            after = (new[u], *[back_other[v] for v in (u - 1,) if v in members[c]])
             back_other[u] = from_behind(back_send[u], "var", 1)
 
     def forward(c, *after):
@@ -489,16 +508,16 @@
         back_a, mark = forward(0)
         got_c = exchange(gate(coef_c, got_b, mark))
         adjoint(1, got_b)
-        arrived_a = exchange(gate(back_a, got_c, *[own[u] for u in members[1]], other[members[1][0]]))
+        gradient_step(1)
+        arrived_a = exchange(gate(back_a, got_c, new[members[1][-1]], back_other[members[1][-2]]))
         adjoint(2, got_c)
-        gradient_step(1)
-        back_b, _ = forward(1, own[members[2][0]])
-        arrived_b = exchange(gate(back_b, arrived_a, own[members[2][0]]))
+        back_b, _ = forward(1, own[members[2][-1]])
+        arrived_b = exchange(gate(back_b, arrived_a))
         gradient_step(2, arrived_a)
-        updated = all_new()
         back_c, _ = forward(2)
         total = inverse(0, arrived_a, None, jnp.float32)
-        arrived_c = exchange(gate(back_c, arrived_b, total, updated))
+        arrived_c = exchange(gate(back_c, arrived_b, total))
+        updated = all_new()
         total = inverse(1, arrived_b, total, jnp.float32)
         total = inverse(2, arrived_c, total, jnp.bfloat16)
     else:
@@ -584,6 +603,7 @@
         and devices * 8 == LANES
         and round_up(levels, 8) <= LANES
         and tail > 0
+        and grad_grid.shape[3] % 4 == 0
         and LANES % tail == 0
     )
     return (tiled_local if fits else plain_local)(*arrays)

time: 558 us -> 548 us (0.982)
  matrix products: 15.2 us -> 0.47 us
    dot_general x3 -> x0, matrix products: 14.7 us -> none  [chosen_waves(): jnp.dot(onehot, table, preferred_element_type=jnp.float32)]
    pallas_call x3, Pallas kernels: 41.5 us -> 52.3 us  [forward_dft(): pl.pallas_call(behind(functools.partial(dft_kernel, steps, place), 2, len...]
    ppermute x12, waiting for transfers between devices: 92.2 us -> 100 us  [from_behind(): return lax.ppermute(block, axis, route)]
    pallas_call x3, Pallas kernels: 71.1 us -> 63.8 us  [inverse_dft(): pl.pallas_call(behind(functools.partial(inverse_kernel, steps, place, len...]
    slice x0 -> x12, local copies, waits for them, and re-layouts: none -> 6.5 us  [the longest x1 3.91 us: all_new(): return updated[:, :, :levels].reshape(owned, 2 * levels, degrees)]
    all_to_all x6, waiting for transfers between devices: 123 us -> 116 us  [exchange(): return lax.all_to_all(block, 'lat', split_axis=0, concat_axis=0, tiled=True)]
  transfers between devices with their start and end apart: 18 -> 18, of which waited for: 13 -> 12; matrix products, arithmetic and copies ran while one was open for 6% -> 3% of each run, Pallas kernels for 37% -> 38%
where the time goes in v2:
time: 548 us; the launch traced here: 543 us
  Pallas kernels  239 us (44%)
  waiting for transfers between devices  217 us (40%)
  starting transfers between devices  59.8 us (11%)
  local copies, waits for them, and re-layouts  24.2 us (4%)
    all_to_all x6, waiting for transfers between devices, exchange(): return lax.all_to_all(block, 'lat', split_axis=0, concat_axis=0, tiled=True)  116 us
    ppermute x12, waiting for transfers between devices, from_behind(): return lax.ppermute(block, axis, route)  100 us
    pallas_call x3, Pallas kernels, inverse_dft(): pl.pallas_call(behind(functools.partial(inverse_kernel, steps, place, len...  63.8 us
    pallas_call x3, Pallas kernels, forward_dft(): pl.pallas_call(behind(functools.partial(dft_kernel, steps, place), 2, len...  52.3 us
    pallas_call x6, Pallas kernels, spectral(): pl.pallas_call(behind(functools.partial(spectral_kernel, place), 4, len(a...  49 us
    pallas_call x3, Pallas kernels, spectral_back(): pl.pallas_call(behind(functools.partial(back_kernel, place), 2 * units +...  43.7 us
    all_to_all x6, starting transfers between devices, exchange(): return lax.all_to_all(block, 'lat', split_axis=0, concat_axis=0, tiled=True)  38.3 us
    pallas_call x6, Pallas kernels, update(): pl.pallas_call(behind(update_kernel, 6, len(after)), grid=(1,), in_specs=...  30.6 us
  transfers between devices with their start and end apart: 18, of which 12 were waited for; matrix products, arithmetic and copies ran while one was open for 3% of the time, Pallas kernels for 38%

profile of v2, /device:TPU:15, one launch (start us, length us, event | category | flops | bytes accessed | tf_op | source)
XLA Modules:
  0.0 543.3 jit_solution(1513911735762190295)
XLA Ops:
  0.6 0.8 reshape.77
  2.4 10.6 %forward_dft.3 = (f32[128,3456]{1,0:T(8,128)}, bf16[128,3072]{1,0:T(8,128)(2,1)}, f32[8,128]{1,0:T(8,128)}) custom-call(s32[128,1]{1,0:T(8,128)} %slice.43.refs_0_, bf16[70,48,1536]{2,1,0:T(8,128)(2,1)} %bitcast.40), custom_call_target="tpu_custom_call" | custom-call | flops 330301440 | tf_op jit(solution)/shard_map/forward_dft/pallas_call | solution.py:156
  13.0 7.0 %all-to-all-start = ((f32[16,8,3456]{2,1,0:T(8,128)}), f32[16,8,3456]{2,1,0:T(8,128)}, u32[]{:S(2)}, u32[]{:S(2)}) async-start(f32[16,8,3456]{2,1,0:T(8,128)} %bitcast.49), calls=%async_computation | async-start | bytes 3538944 | tf_op jit(solution)/shard_map/all_to_all | solution.py:432
  22.0 17.2 %forward_dft.5 = (f32[128,6784]{1,0:T(8,128)}, bf16[256,3072]{1,0:T(8,128)(2,1)}, f32[8,128]{1,0:T(8,128)}) custom-call(s32[256,1]{1,0:T(8,128)} %slice.45.refs_0_, bf16[70,48,1536]{2,1,0:T(8,128)(2,1)} %bitcast.41), custom_call_target="tpu_custom_call" | custom-call | flops 660602880 | tf_op jit(solution)/shard_map/forward_dft/pallas_call | solution.py:156
  39.2 24.4 %forward_dft.4 = (f32[128,10112]{1,0:T(8,128)}, bf16[384,3072]{1,0:T(8,128)(2,1)}, f32[8,128]{1,0:T(8,128)}) custom-call(s32[384,1]{1,0:T(8,128)} %slice.44.refs_0_, bf16[70,48,1536]{2,1,0:T(8,128)(2,1)} %bitcast.42), custom_call_target="tpu_custom_call" | custom-call | flops 990904320 | tf_op jit(solution)/shard_map/forward_dft/pallas_call | solution.py:156
  63.6 6.5 %all-to-all-start.1 = ((f32[16,8,10112]{2,1,0:T(8,128)}), f32[16,8,10112]{2,1,0:T(8,128)}, u32[]{:S(2)}, u32[]{:S(2)}) async-start(f32[16,8,10112]{2,1,0:T(8,128)} %gate.5), calls=%async_computation.1 | async-start | bytes 10354688 | tf_op jit(solution)/shard_map/all_to_all | solution.py:432
  70.9 1.0 broadcast_multiply_fusion
  72.9 8.2 %spectral_adjoint.6 = (f32[4,144,384]{2,1,0:T(8,128)}, f32[4,144,384]{2,1,0:T(8,128)}) custom-call(f32[16,8,3456]{2,1,0:T(8,128)} %all-to-all-done.refs_0_.refs_1_, f32[16,8,3456]{2,1,0:T(8,128)} %all-to-all-done.refs_0_.refs_1_, f32[24,768,384]{2,1,0:T(8,128)} %refs_6_.1, f32[288,144]{1,0:T(8,128)} %copy-done.2), custom_call_target="tpu_custom_call" | custom-call | flops 254803968 | tf_op jit(solution)/shard_map/spectral_adjoint/pallas_call | solution.py:223
  81.1 3.0 collective-permute-start
  84.8 0.8 mul.118.refs_4_
  85.9 3.5 copy.22
  89.3 2.7 pad.25
  92.1 10.1 %collective-permute-done.refs_2_ = f32[4,144,384]{2,1,0:T(8,128)} collective-permute-done((f32[4,144,384]{2,1,0:T(8,128)}, f32[4,144,384]{2,1,0:T(8,128)}, u32[]{:S(2)}, u32[]{:S(2)}) %collective-permute-start) | collective-permute-done | bytes 884768 | tf_op jit(solution)/shard_map/ppermute | solution.py:27
  102.2 5.1 gradient_step.6
  107.3 1.3 collective-permute-start.5
  108.6 1.7 mul.127.refs_3_.refs_5_.refs_7_
  110.3 19.4 %collective-permute-done.5.refs_1_ = f32[4,144,384]{2,1,0:T(8,128)S(1)} collective-permute-done((f32[4,144,384]{2,1,0:T(8,128)}, f32[4,144,384]{2,1,0:T(8,128)S(1)}, u32[]{:S(2)}, u32[]{:S(2)}) %collective-permute-start.5) | collective-permute-done | bytes 884768 | tf_op jit(solution)/shard_map/ppermute | solution.py:27
  129.7 0.9 copy-done.11
  130.6 8.7 %spectral_forward.3 = (f32[16,8,3456]{2,1,0:T(8,128)}, f32[8,128]{1,0:T(8,128)}) custom-call(f32[4,144,384]{2,1,0:T(8,128)} %get-tuple-element.60.refs_0_, f32[4,144,384]{2,1,0:T(8,128)} %copy-done.11, f32[24,768,384]{2,1,0:T(8,128)} %refs_6_.1, f32[144,144]{1,0:T(8,128)} %mul.127.refs_3_.refs_5_.refs_7_), custom_call_target="tpu_custom_call" | custom-call | flops 254803968 | tf_op jit(solution)/shard_map/spectral_forward/pallas_call | solution.py:341
  139.3 44.2 %all-to-all-done.1.refs_0_.refs_1_ = f32[16,8,10112]{2,1,0:T(8,128)} async-done(((f32[16,8,10112]{2,1,0:T(8,128)}), f32[16,8,10112]{2,1,0:T(8,128)}, u32[]{:S(2)}, u32[]{:S(2)}) %all-to-all-start.1) | async-done | bytes 5177376 | tf_op jit(solution)/shard_map/all_to_all | solution.py:432
  183.5 5.1 all-to-all-start.2
  188.6 8.1 %spectral_adjoint.7 = (f32[4,144,384]{2,1,0:T(8,128)}, f32[4,144,384]{2,1,0:T(8,128)}) custom-call(f32[16,8,10112]{2,1,0:T(8,128)} %all-to-all-done.1.refs_0_.refs_1_, f32[16,8,10112]{2,1,0:T(8,128)} %all-to-all-done.1.refs_0_.refs_1_, f32[24,768,384]{2,1,0:T(8,128)} %refs_6_.1, f32[288,144]{1,0:T(8,128)} %copy-done.2), custom_call_target="tpu_custom_call" | custom-call | flops 254803968 | tf_op jit(solution)/shard_map/spectral_adjoint/pallas_call | solution.py:223
  196.7 2.2 collective-permute-start.1
  198.9 8.2 %spectral_adjoint.8 = (f32[4,144,384]{2,1,0:T(8,128)}, f32[4,144,384]{2,1,0:T(8,128)}) custom-call(f32[16,8,10112]{2,1,0:T(8,128)} %all-to-all-done.1.refs_0_.refs_1_, f32[16,8,10112]{2,1,0:T(8,128)} %all-to-all-done.1.refs_0_.refs_1_, f32[24,768,384]{2,1,0:T(8,128)} %refs_6_.1, f32[288,144]{1,0:T(8,128)} %copy-done.2, ...), custom_call_target="tpu_custom_call" | custom-call | flops 254803968 | tf_op jit(solution)/shard_map/spectral_adjoint/pallas_call | solution.py:223
  207.1 2.2 collective-permute-start.2
  209.3 8.2 %spectral_adjoint.9 = (f32[4,144,384]{2,1,0:T(8,128)}, f32[4,144,384]{2,1,0:T(8,128)}) custom-call(f32[16,8,10112]{2,1,0:T(8,128)} %all-to-all-done.1.refs_0_.refs_1_, f32[16,8,10112]{2,1,0:T(8,128)} %all-to-all-done.1.refs_0_.refs_1_, f32[24,768,384]{2,1,0:T(8,128)} %refs_6_.1, f32[288,144]{1,0:T(8,128)} %copy-done.2, ...), custom_call_target="tpu_custom_call" | custom-call | flops 254803968 | tf_op jit(solution)/shard_map/spectral_adjoint/pallas_call | solution.py:223
  217.5 2.6 collective-permute-start.3
  220.1 0.9 copy-done.14
  221.0 5.1 gradient_step.7
  226.1 1.3 collective-permute-start.4
  227.4 9.4 %collective-permute-done.2.refs_2_ = f32[4,144,384]{2,1,0:T(8,128)} collective-permute-done((f32[4,144,384]{2,1,0:T(8,128)}, f32[4,144,384]{2,1,0:T(8,128)}, u32[]{:S(2)}, u32[]{:S(2)}) %collective-permute-start.2) | collective-permute-done | bytes 884768 | tf_op jit(solution)/shard_map/ppermute | solution.py:27
  236.8 5.1 gradient_step.8
  241.9 1.3 collective-permute-start.7
  243.2 12.6 %collective-permute-done.3.refs_2_ = f32[4,144,384]{2,1,0:T(8,128)} collective-permute-done((f32[4,144,384]{2,1,0:T(8,128)}, f32[4,144,384]{2,1,0:T(8,128)}, u32[]{:S(2)}, u32[]{:S(2)}) %collective-permute-start.3) | collective-permute-done | bytes 884768 | tf_op jit(solution)/shard_map/ppermute | solution.py:27
  255.8 0.9 copy-done.4
  256.7 5.1 gradient_step.9
  261.8 6.1 %collective-permute-done.7.refs_3_.refs_4_ = f32[4,144,384]{2,1,0:T(8,128)} collective-permute-done((f32[4,144,384]{2,1,0:T(8,128)}, f32[4,144,384]{2,1,0:T(8,128)}, u32[]{:S(2)}, u32[]{:S(2)}) %collective-permute-start.7) | collective-permute-done | bytes 884768 | tf_op jit(solution)/shard_map/ppermute | solution.py:27
  267.8 7.2 %all-to-all-start.3 = ((f32[16,8,3456]{2,1,0:T(8,128)}), f32[16,8,3456]{2,1,0:T(8,128)}, u32[]{:S(2)}, u32[]{:S(2)}) async-start(f32[16,8,3456]{2,1,0:T(8,128)} %gate.7), calls=%async_computation.3 | async-start | bytes 3538944 | tf_op jit(solution)/shard_map/all_to_all | solution.py:432
  275.0 1.3 collective-permute-start.11
  276.3 8.2 %spectral_adjoint.10 = (f32[4,144,384]{2,1,0:T(8,128)}, f32[4,144,384]{2,1,0:T(8,128)}) custom-call(f32[16,8,6784]{2,1,0:T(8,128)} %all-to-all-done.2.refs_0_.refs_1_, f32[16,8,6784]{2,1,0:T(8,128)} %all-to-all-done.2.refs_0_.refs_1_, f32[24,768,384]{2,1,0:T(8,128)} %refs_6_.1, f32[288,144]{1,0:T(8,128)} %copy-done.2), custom_call_target="tpu_custom_call" | custom-call | flops 254803968 | tf_op jit(solution)/shard_map/spectral_adjoint/pallas_call | solution.py:223
  284.4 8.2 %spectral_adjoint.11 = (f32[4,144,384]{2,1,0:T(8,128)}, f32[4,144,384]{2,1,0:T(8,128)}) custom-call(f32[16,8,6784]{2,1,0:T(8,128)} %all-to-all-done.2.refs_0_.refs_1_, f32[16,8,6784]{2,1,0:T(8,128)} %all-to-all-done.2.refs_0_.refs_1_, f32[24,768,384]{2,1,0:T(8,128)} %refs_6_.1, f32[288,144]{1,0:T(8,128)} %copy-done.2, ...), custom_call_target="tpu_custom_call" | custom-call | flops 254803968 | tf_op jit(solution)/shard_map/spectral_adjoint/pallas_call | solution.py:223
  292.7 5.4 collective-permute-done.11.refs_5_
  298.1 1.0 copy-done.10
  299.0 20.5 %spectral_forward.5 = (f32[16,8,10112]{2,1,0:T(8,128)}, f32[8,128]{1,0:T(8,128)}) custom-call(f32[4,144,384]{2,1,0:T(8,128)} %get-tuple-element.76.refs_0_, f32[4,144,384]{2,1,0:T(8,128)} %get-tuple-element.77.refs_1_, f32[4,144,384]{2,1,0:T(8,128)} %get-tuple-element.78.refs_2_, f32[4,144,384]{2,1,0:T(8,128)} %copy-done.4, ...), custom_call_target="tpu_custom_call" | custom-call | flops 764411904 | tf_op jit(solution)/shard_map/spectral_forward/pallas_call | solution.py:341
  319.5 6.9 %all-to-all-start.4 = ((f32[16,8,10112]{2,1,0:T(8,128)}), f32[16,8,10112]{2,1,0:T(8,128)}, u32[]{:S(2)}, u32[]{:S(2)}) async-start(f32[16,8,10112]{2,1,0:T(8,128)} %gate.8), calls=%async_computation.4 | async-start | bytes 10354688 | tf_op jit(solution)/shard_map/all_to_all | solution.py:432
  326.4 1.3 collective-permute-start.6
  327.8 2.4 collective-permute-start.8
  330.2 16.2 %collective-permute-done.6.refs_2_ = f32[4,144,384]{2,1,0:T(8,128)S(1)} collective-permute-done((f32[4,144,384]{2,1,0:T(8,128)S(1)}, f32[4,144,384]{2,1,0:T(8,128)S(1)}, u32[]{:S(2)}, u32[]{:S(2)}) %collective-permute-start.6) | collective-permute-done | bytes 884768 | tf_op jit(solution)/shard_map/ppermute | solution.py:27
  346.4 1.0 copy-done.12
  347.4 5.1 gradient_step.10
  352.4 1.3 collective-permute-start.9
  353.7 11.7 %collective-permute-done.8.refs_2_ = f32[4,144,384]{2,1,0:T(8,128)} collective-permute-done((f32[4,144,384]{2,1,0:T(8,128)}, f32[4,144,384]{2,1,0:T(8,128)}, u32[]{:S(2)}, u32[]{:S(2)}) %collective-permute-start.8) | collective-permute-done | bytes 884768 | tf_op jit(solution)/shard_map/ppermute | solution.py:27
  365.5 5.1 gradient_step.11
  370.6 1.3 collective-permute-start.10
  371.8 13.4 %inverse_dft.3.refs_2_.refs_3_ = f32[70,48,1536]{2,1,0:T(8,128)} custom-call(f32[128,3456]{1,0:T(8,128)} %bitcast.13.refs_0_, bf16[128,3072]{1,0:T(8,128)(2,1)} %get-tuple-element.81.refs_1_.refs_2_, bf16[128,3072]{1,0:T(8,128)(2,1)} %get-tuple-element.81.refs_1_.refs_2_), custom_call_target="tpu_custom_call" | custom-call | flops 495452160 | tf_op jit(solution)/shard_map/inverse_dft/pallas_call | solution.py:401
  385.3 9.3 %collective-permute-done.10.refs_3_ = f32[4,144,384]{2,1,0:T(8,128)} collective-permute-done((f32[4,144,384]{2,1,0:T(8,128)}, f32[4,144,384]{2,1,0:T(8,128)}, u32[]{:S(2)}, u32[]{:S(2)}) %collective-permute-start.10) | collective-permute-done | bytes 884768 | tf_op jit(solution)/shard_map/ppermute | solution.py:27
  394.6 14.5 %spectral_forward.4 = (f32[16,8,6784]{2,1,0:T(8,128)}, f32[8,128]{1,0:T(8,128)}) custom-call(f32[4,144,384]{2,1,0:T(8,128)} %get-tuple-element.71.refs_0_, f32[4,144,384]{2,1,0:T(8,128)} %get-tuple-element.72.refs_1_, f32[4,144,384]{2,1,0:T(8,128)} %copy-done.9, f32[4,144,384]{2,1,0:T(8,128)} %collective-permute-done.10.refs_3_, f32[24,768,384]{2,1,0:T(8,128)} %refs_6_.1, ...), custom_call_target="tpu_custom_call" | custom-call | flops 509607936 | tf_op jit(solution)/shard_map/spectral_forward/pallas_call | solution.py:341
  409.1 30.9 %all-to-all-done.4.refs_1_ = f32[16,8,10112]{2,1,0:T(8,128)} async-done(((f32[16,8,10112]{2,1,0:T(8,128)}), f32[16,8,10112]{2,1,0:T(8,128)}, u32[]{:S(2)}, u32[]{:S(2)}) %all-to-all-start.4) | async-done | bytes 5177376 | tf_op jit(solution)/shard_map/all_to_all | solution.py:432
  440.0 5.7 %all-to-all-start.5 = ((f32[16,8,6784]{2,1,0:T(8,128)}), f32[16,8,6784]{2,1,0:T(8,128)}, u32[]{:S(2)}, u32[]{:S(2)}) async-start(f32[16,8,6784]{2,1,0:T(8,128)} %gate.9), calls=%async_computation.5 | async-start | bytes 6946816 | tf_op jit(solution)/shard_map/all_to_all | solution.py:432
  445.7 1.4 constant_dynamic-update-slice_fusion.9
  447.5 3.9 copy.28
  451.4 29.8 %inverse_dft.4.refs_3_ = f32[70,48,1536]{2,1,0:T(8,128)} custom-call(f32[128,10112]{1,0:T(8,128)} %bitcast.15.refs_0_, bf16[384,3072]{1,0:T(8,128)(2,1)} %get-tuple-element.83.refs_1_.refs_2_, bf16[384,3072]{1,0:T(8,128)(2,1)} %get-tuple-element.83.refs_1_.refs_2_, f32[70,48,1536]{2,1,0:T(8,128)} %inverse_dft.3.refs_2_.refs_3_), custom_call_target="tpu_custom_call" | custom-call | flops 1486356480 | tf_op jit(solution)/shard_map/inverse_dft/pallas_call | solution.py:401
  481.2 41.4 %all-to-all-done.5 = f32[16,8,6784]{2,1,0:T(8,128)} async-done(((f32[16,8,6784]{2,1,0:T(8,128)}), f32[16,8,6784]{2,1,0:T(8,128)}, u32[]{:S(2)}, u32[]{:S(2)}) %all-to-all-start.5) | async-done | bytes 3473440 | tf_op jit(solution)/shard_map/all_to_all | solution.py:432
  522.6 20.5 %inverse_dft.5 = bf16[70,48,1536]{2,1,0:T(8,128)(2,1)} custom-call(f32[128,6784]{1,0:T(8,128)} %bitcast.14.refs_0_, bf16[256,3072]{1,0:T(8,128)(2,1)} %get-tuple-element.82.refs_1_.refs_2_, bf16[256,3072]{1,0:T(8,128)(2,1)} %get-tuple-element.82.refs_1_.refs_2_, f32[70,48,1536]{2,1,0:T(8,128)} %inverse_dft.4.refs_3_), custom_call_target="tpu_custom_call" | custom-call | flops 990904320 | tf_op jit(solution)/shard_map/inverse_dft/pallas_call | solution.py:401
  (82 shorter events, 5.2 us)
Async XLA Ops:
  0.6 69.7 %copy-start = (f32[70,70]{1,0:T(8,128)S(1)}, f32[70,70]{1,0:T(8,128)}, u32[]{:S(2)}) copy-start(f32[70,70]{1,0:T(8,128)} %param.11) | copy-start | bytes 58804
  13.0 50.6 %all-to-all-start = ((f32[16,8,3456]{2,1,0:T(8,128)}), f32[16,8,3456]{2,1,0:T(8,128)}, u32[]{:S(2)}, u32[]{:S(2)}) async-start(f32[16,8,3456]{2,1,0:T(8,128)} %bitcast.49), calls=%async_computation | async-start | bytes 3538944 | tf_op jit(solution)/shard_map/all_to_all | solution.py:432
  63.6 6.5 %copy-start.16 = (f32[1,70,70]{2,0,1:T(1,128)S(1)}, f32[1,70,70]{2,0,1:T(1,128)}, u32[]{:S(2)}) copy-start(f32[1,70,70]{2,0,1:T(1,128)} %param.9) | copy-start | bytes 58804
  63.6 6.6 %copy-start.15 = (f32[1,70,70]{2,0,1:T(1,128)S(1)}, f32[1,70,70]{2,0,1:T(1,128)}, u32[]{:S(2)}) copy-start(f32[1,70,70]{2,0,1:T(1,128)} %param.10) | copy-start | bytes 58804
  63.6 119.9 %all-to-all-start.1 = ((f32[16,8,10112]{2,1,0:T(8,128)}), f32[16,8,10112]{2,1,0:T(8,128)}, u32[]{:S(2)}, u32[]{:S(2)}) async-start(f32[16,8,10112]{2,1,0:T(8,128)} %gate.5), calls=%async_computation.1 | async-start | bytes 10354688 | tf_op jit(solution)/shard_map/all_to_all | solution.py:432
  72.2 0.7 copy-start.2
  81.1 21.1 %collective-permute-start = (f32[4,144,384]{2,1,0:T(8,128)}, f32[4,144,384]{2,1,0:T(8,128)}, u32[]{:S(2)}, u32[]{:S(2)}) collective-permute-start(f32[4,144,384]{2,1,0:T(8,128)} %get-tuple-element.45), channel_id=1, source_target_pairs={{16,0},{17,1},{18,2},{19,3},{20,4},{21,5},{22,6},{23,7},{24,8},{25... | collective-permute-start | bytes 2654216 | tf_op jit(solution)/shard_map/ppermute | solution.py:27
  92.1 10.1 %copy-start.3 = (f32[288,144]{1,0:T(8,128)}, f32[288,144]{1,0:T(8,128)S(1)}, u32[]{:S(2)}) copy-start(f32[288,144]{1,0:T(8,128)S(1)} %constant_dynamic-update-slice_fusion.2.refs_5_) | copy-start | bytes 497668
  107.3 22.4 %collective-permute-start.5 = (f32[4,144,384]{2,1,0:T(8,128)}, f32[4,144,384]{2,1,0:T(8,128)S(1)}, u32[]{:S(2)}, u32[]{:S(2)}) collective-permute-start(f32[4,144,384]{2,1,0:T(8,128)} %get-tuple-element.61), channel_id=1, source_target_pairs={{0,16},{1,17},{2,18},{3,19},{4,20},{5,21},{6,22},{7,23},{8,24},{9,... | collective-permute-start | bytes 2654216 | tf_op jit(solution)/shard_map/ppermute | solution.py:27
  129.7 0.9 copy-start.11
  183.5 84.3 %all-to-all-start.2 = ((f32[16,8,6784]{2,1,0:T(8,128)}), f32[16,8,6784]{2,1,0:T(8,128)}, u32[]{:S(2)}, u32[]{:S(2)}) async-start(f32[16,8,6784]{2,1,0:T(8,128)} %gate.6), calls=%async_computation.2 | async-start | bytes 6946816 | tf_op jit(solution)/shard_map/all_to_all | solution.py:432
  196.7 23.3 %collective-permute-start.1 = (f32[4,144,384]{2,1,0:T(8,128)}, f32[4,144,384]{2,1,0:T(8,128)S(1)}, u32[]{:S(2)}, u32[]{:S(2)}) collective-permute-start(f32[4,144,384]{2,1,0:T(8,128)} %get-tuple-element.50), channel_id=1, source_target_pairs={{16,0},{17,1},{18,2},{19,3},{20,4},{21,5},{22,6},{23,7},{24,8},{25... | collective-permute-start | bytes 2654216 | tf_op jit(solution)/shard_map/ppermute | solution.py:27
  207.1 29.7 %collective-permute-start.2 = (f32[4,144,384]{2,1,0:T(8,128)}, f32[4,144,384]{2,1,0:T(8,128)}, u32[]{:S(2)}, u32[]{:S(2)}) collective-permute-start(f32[4,144,384]{2,1,0:T(8,128)} %get-tuple-element.53), channel_id=1, source_target_pairs={{16,0},{17,1},{18,2},{19,3},{20,4},{21,5},{22,6},{23,7},{24,8},{25... | collective-permute-start | bytes 2654216 | tf_op jit(solution)/shard_map/ppermute | solution.py:27
  217.5 38.3 %collective-permute-start.3 = (f32[4,144,384]{2,1,0:T(8,128)}, f32[4,144,384]{2,1,0:T(8,128)}, u32[]{:S(2)}, u32[]{:S(2)}) collective-permute-start(f32[4,144,384]{2,1,0:T(8,128)} %get-tuple-element.56), channel_id=1, source_target_pairs={{16,0},{17,1},{18,2},{19,3},{20,4},{21,5},{22,6},{23,7},{24,8},{25... | collective-permute-start | bytes 2654216 | tf_op jit(solution)/shard_map/ppermute | solution.py:27
  220.1 1.0 copy-start.14
  226.1 29.6 %collective-permute-start.4 = (f32[4,144,384]{2,1,0:T(8,128)}, f32[4,144,384]{2,1,0:T(8,128)S(1)}, u32[]{:S(2)}, u32[]{:S(2)}) collective-permute-start(f32[4,144,384]{2,1,0:T(8,128)} %get-tuple-element.57), channel_id=1, source_target_pairs={{0,16},{1,17},{2,18},{3,19},{4,20},{5,21},{6,22},{7,23},{8,24},{9,... | collective-permute-start | bytes 2654216 | tf_op jit(solution)/shard_map/ppermute | solution.py:27
  241.9 25.9 %collective-permute-start.7 = (f32[4,144,384]{2,1,0:T(8,128)}, f32[4,144,384]{2,1,0:T(8,128)}, u32[]{:S(2)}, u32[]{:S(2)}) collective-permute-start(f32[4,144,384]{2,1,0:T(8,128)} %get-tuple-element.66), channel_id=1, source_target_pairs={{0,16},{1,17},{2,18},{3,19},{4,20},{5,21},{6,22},{7,23},{8,24},{9,... | collective-permute-start | bytes 2654216 | tf_op jit(solution)/shard_map/ppermute | solution.py:27
  255.7 0.9 copy-start.4
  267.8 51.7 %all-to-all-start.3 = ((f32[16,8,3456]{2,1,0:T(8,128)}), f32[16,8,3456]{2,1,0:T(8,128)}, u32[]{:S(2)}, u32[]{:S(2)}) async-start(f32[16,8,3456]{2,1,0:T(8,128)} %gate.7), calls=%async_computation.3 | async-start | bytes 3538944 | tf_op jit(solution)/shard_map/all_to_all | solution.py:432
  275.0 23.1 %collective-permute-start.11 = (f32[4,144,384]{2,1,0:T(8,128)}, f32[4,144,384]{2,1,0:T(8,128)S(1)}, u32[]{:S(2)}, u32[]{:S(2)}) collective-permute-start(f32[4,144,384]{2,1,0:T(8,128)} %get-tuple-element.79), channel_id=1, source_target_pairs={{0,16},{1,17},{2,18},{3,19},{4,20},{5,21},{6,22},{7,23},{8,24},{9,... | collective-permute-start | bytes 2654216 | tf_op jit(solution)/shard_map/ppermute | solution.py:27
  298.1 1.0 copy-start.10
  319.5 6.9 %copy-start.17 = (f32[4,144,384]{2,1,0:T(8,128)S(1)}, f32[4,144,384]{2,1,0:T(8,128)}, u32[]{:S(2)}) copy-start(f32[4,144,384]{2,1,0:T(8,128)} %get-tuple-element.64) | copy-start | bytes 2654212
  319.5 120.4 %all-to-all-start.4 = ((f32[16,8,10112]{2,1,0:T(8,128)}), f32[16,8,10112]{2,1,0:T(8,128)}, u32[]{:S(2)}, u32[]{:S(2)}) async-start(f32[16,8,10112]{2,1,0:T(8,128)} %gate.8), calls=%async_computation.4 | async-start | bytes 10354688 | tf_op jit(solution)/shard_map/all_to_all | solution.py:432
  326.4 20.0 %collective-permute-start.6 = (f32[4,144,384]{2,1,0:T(8,128)S(1)}, f32[4,144,384]{2,1,0:T(8,128)S(1)}, u32[]{:S(2)}, u32[]{:S(2)}) collective-permute-start(f32[4,144,384]{2,1,0:T(8,128)S(1)} %copy-done.17), channel_id=1, source_target_pairs={{16,0},{17,1},{18,2},{19,3},{20,4},{21,5},{22,6},{23,7},{24,8},{25... | collective-permute-start | bytes 2654216 | tf_op jit(solution)/shard_map/ppermute | solution.py:27
  327.8 37.7 %collective-permute-start.8 = (f32[4,144,384]{2,1,0:T(8,128)}, f32[4,144,384]{2,1,0:T(8,128)}, u32[]{:S(2)}, u32[]{:S(2)}) collective-permute-start(f32[4,144,384]{2,1,0:T(8,128)} %get-tuple-element.69), channel_id=1, source_target_pairs={{16,0},{17,1},{18,2},{19,3},{20,4},{21,5},{22,6},{23,7},{24,8},{25... | collective-permute-start | bytes 2654216 | tf_op jit(solution)/shard_map/ppermute | solution.py:27
  346.4 1.0 copy-start.12
  352.4 32.8 %collective-permute-start.9 = (f32[4,144,384]{2,1,0:T(8,128)}, f32[4,144,384]{2,1,0:T(8,128)S(1)}, u32[]{:S(2)}, u32[]{:S(2)}) collective-permute-start(f32[4,144,384]{2,1,0:T(8,128)} %get-tuple-element.73), channel_id=1, source_target_pairs={{0,16},{1,17},{2,18},{3,19},{4,20},{5,21},{6,22},{7,23},{8,24},{9,... | collective-permute-start | bytes 2654216 | tf_op jit(solution)/shard_map/ppermute | solution.py:27
  370.6 24.1 %collective-permute-start.10 = (f32[4,144,384]{2,1,0:T(8,128)}, f32[4,144,384]{2,1,0:T(8,128)}, u32[]{:S(2)}, u32[]{:S(2)}) collective-permute-start(f32[4,144,384]{2,1,0:T(8,128)} %get-tuple-element.74), channel_id=1, source_target_pairs={{0,16},{1,17},{2,18},{3,19},{4,20},{5,21},{6,22},{7,23},{8,24},{9,... | collective-permute-start | bytes 2654216 | tf_op jit(solution)/shard_map/ppermute | solution.py:27
  385.3 9.4 %copy-start.9 = (f32[4,144,384]{2,1,0:T(8,128)}, f32[4,144,384]{2,1,0:T(8,128)S(1)}, u32[]{:S(2)}) copy-start(f32[4,144,384]{2,1,0:T(8,128)S(1)} %collective-permute-done.9.refs_2_) | copy-start | bytes 2654212
  440.0 7.1 %copy-start.5 = (f32[4,144,384]{2,1,0:T(8,128)S(1)}, f32[4,144,384]{2,1,0:T(8,128)}, u32[]{:S(2)}) copy-start(f32[4,144,384]{2,1,0:T(8,128)} %get-tuple-element.51.refs_6_) | copy-start | bytes 2654212
  440.0 7.2 %copy-start.6 = (f32[4,144,384]{2,1,0:T(8,128)S(1)}, f32[4,144,384]{2,1,0:T(8,128)}, u32[]{:S(2)}) copy-start(f32[4,144,384]{2,1,0:T(8,128)} %get-tuple-element.54.refs_6_) | copy-start | bytes 2654212
  440.0 7.3 %copy-start.7 = (f32[4,144,384]{2,1,0:T(8,128)S(1)}, f32[4,144,384]{2,1,0:T(8,128)}, u32[]{:S(2)}) copy-start(f32[4,144,384]{2,1,0:T(8,128)} %get-tuple-element.58.refs_2_) | copy-start | bytes 2654212
  440.0 82.6 %all-to-all-start.5 = ((f32[16,8,6784]{2,1,0:T(8,128)}), f32[16,8,6784]{2,1,0:T(8,128)}, u32[]{:S(2)}, u32[]{:S(2)}) async-start(f32[16,8,6784]{2,1,0:T(8,128)} %gate.9), calls=%async_computation.5 | async-start | bytes 6946816 | tf_op jit(solution)/shard_map/all_to_all | solution.py:432
  445.7 1.6 copy-start.8
  445.7 1.7 copy-start.13
  522.6 20.5 %copy-start.1 = (f32[70,70]{1,0:T(8,128)S(1)}, f32[70,70]{1,0:T(8,128)}, u32[]{:S(2)}) copy-start(f32[70,70]{1,0:T(8,128)} %param.11) | copy-start | bytes 58804

commit v3 on v2

--- a/solution.py
+++ b/solution.py
@@ -475,23 +475,28 @@
             other[u] = from_behind(send[u], "var", -1)
             after = (own[u],)
 
-    def gradient_step(c, *after):
-        for u in members[c]:
+    def gradient_step(group, *after):
+        for u in group:
             new[u], keep[u], back_send[u] = update(
                 step_size, own[u], other[u], own_control, u, mode_mat, forward_mat, after
             )
-            after = (new[u], *[back_other[v] for v in (u - 1,) if v in members[c]])
+            after = (new[u],)
             back_other[u] = from_behind(back_send[u], "var", 1)
 
-    def forward(c, *after):
-        keeps, gots = [keep[u] for u in members[c]], [back_other[u] for u in members[c]]
-        return spectral_back(
-            keeps, gots, place[c], legendre, members[c][0], remap_mat, devices, after
-        )
-
-    def inverse(c, arrived, total, dtype, *after):
-        coef = arrived.reshape(LANES, place[c].lanes)
-        return inverse_dft(coef, place[c], waves[c], total, lats, dtype, after)
+    def forward(group, *after):
+        keeps, gots = [keep[u] for u in group], [back_other[u] for u in group]
+        at = Rows(lats, levels, len(group))
+        return spectral_back(keeps, gots, at, legendre, group[0], remap_mat, devices, after)
+
+    def inverse(group, arrived, total, dtype, *after):
+        at = Rows(lats, levels, len(group))
+        rows = []
+        for c, chunk in enumerate(members):
+            shared = [u - chunk[0] for u in group if u in chunk]
+            if shared:
+                rows.append(waves[c][shared[0] * LANES : (shared[-1] + 1) * LANES])
+        coef = arrived.reshape(LANES, at.lanes)
+        return inverse_dft(coef, at, jnp.concatenate(rows), total, lats, dtype, after)
 
     def all_new():
         updated = jnp.concatenate([new[u] for u in range(units)]).reshape(owned, 2, lead, degrees)
@@ -501,32 +506,34 @@
         coef_a, _ = dft(0)
         got_a = exchange(coef_a)
         coef_b, _ = dft(1)
-        coef_c, mark = dft(2)
-        got_b = exchange(gate(coef_b, got_a, mark))
+        got_b = exchange(gate(coef_b, got_a))
+        coef_c, _ = dft(2, got_a)
         adjoint(0, got_a)
-        gradient_step(0)
-        back_a, mark = forward(0)
-        got_c = exchange(gate(coef_c, got_b, mark))
+        gradient_step(members[0])
+        got_c = exchange(gate(coef_c, got_b, back_other[0]))
         adjoint(1, got_b)
-        gradient_step(1)
-        arrived_a = exchange(gate(back_a, got_c, new[members[1][-1]], back_other[members[1][-2]]))
+        gradient_step(members[1][:-1])
+        early, middle, late = members[0] + members[1][:1], members[1][1:] + members[2][:1], members[2][1:]
+        back_a, mark = forward(early)
+        gradient_step(members[1][-1:], mark)
+        arrived_a = exchange(gate(back_a, got_c, back_other[members[1][-2]], other[members[1][-1]]))
         adjoint(2, got_c)
-        back_b, _ = forward(1, own[members[2][-1]])
-        arrived_b = exchange(gate(back_b, arrived_a))
-        gradient_step(2, arrived_a)
-        back_c, _ = forward(2)
-        total = inverse(0, arrived_a, None, jnp.float32)
+        gradient_step(members[2])
+        back_b, _ = forward(middle)
+        arrived_b = exchange(gate(back_b, arrived_a, own[members[2][-1]]))
+        back_c, _ = forward(late)
+        total = inverse(early, arrived_a, None, jnp.float32)
         arrived_c = exchange(gate(back_c, arrived_b, total))
         updated = all_new()
-        total = inverse(1, arrived_b, total, jnp.float32)
-        total = inverse(2, arrived_c, total, jnp.bfloat16)
+        total = inverse(middle, arrived_b, total, jnp.float32)
+        total = inverse(late, arrived_c, total, jnp.bfloat16)
     else:
         coef, _ = dft(0)
         adjoint(0, exchange(coef))
-        gradient_step(0)
+        gradient_step(members[0])
         updated = all_new()
-        back, _ = forward(0)
-        total = inverse(0, exchange(back), None, jnp.bfloat16)
+        back, _ = forward(members[0])
+        total = inverse(members[0], exchange(back), None, jnp.bfloat16)
     increment = jnp.transpose(total, (1, 0, 2))
     return (updated[None], increment[None])
 

time: 548 us -> 535 us (0.976)
  waiting for transfers between devices: 217 us -> 193 us
    ppermute x12, waiting for transfers between devices: 100 us -> 85.2 us  [from_behind(): return lax.ppermute(block, axis, route)]
    all_to_all x6, waiting for transfers between devices: 116 us -> 108 us  [exchange(): return lax.all_to_all(block, 'lat', split_axis=0, concat_axis=0, tiled=True)]
  transfers between devices with their start and end apart: 18 -> 18, of which waited for: 12 -> 13; matrix products, arithmetic and copies ran while one was open for 3% -> 5% of each run, Pallas kernels for 38% -> 40%
where the time goes in v3:
time: 535 us; the launch traced here: 530 us
  Pallas kernels  240 us (45%)
  waiting for transfers between devices  193 us (36%)
  starting transfers between devices  63.1 us (12%)
  local copies, waits for them, and re-layouts  26.5 us (5%)
    all_to_all x6, waiting for transfers between devices, exchange(): return lax.all_to_all(block, 'lat', split_axis=0, concat_axis=0, tiled=True)  108 us
    ppermute x12, waiting for transfers between devices, from_behind(): return lax.ppermute(block, axis, route)  85.2 us
    pallas_call x3, Pallas kernels, inverse_dft(): pl.pallas_call(behind(functools.partial(inverse_kernel, steps, place, len...  65.2 us
    pallas_call x3, Pallas kernels, forward_dft(): pl.pallas_call(behind(functools.partial(dft_kernel, steps, place), 2, len...  51.8 us
    pallas_call x6, Pallas kernels, spectral(): pl.pallas_call(behind(functools.partial(spectral_kernel, place), 4, len(a...  48.9 us
    pallas_call x3, Pallas kernels, spectral_back(): pl.pallas_call(behind(functools.partial(back_kernel, place), 2 * units +...  43.5 us
    all_to_all x6, starting transfers between devices, exchange(): return lax.all_to_all(block, 'lat', split_axis=0, concat_axis=0, tiled=True)  36.8 us
    pallas_call x6, Pallas kernels, update(): pl.pallas_call(behind(update_kernel, 6, len(after)), grid=(1,), in_specs=...  30.6 us
  transfers between devices with their start and end apart: 18, of which 13 were waited for; matrix products, arithmetic and copies ran while one was open for 5% of the time, Pallas kernels for 40%

profile of v3, /device:TPU:15, one launch (start us, length us, event | category | flops | bytes accessed | tf_op | source)
XLA Modules:
  0.0 530.0 jit_solution(12566929412736425949)
XLA Ops:
  2.4 10.6 %forward_dft.3 = (f32[128,3456]{1,0:T(8,128)}, bf16[128,3072]{1,0:T(8,128)(2,1)}, f32[8,128]{1,0:T(8,128)}) custom-call(s32[128,1]{1,0:T(8,128)} %slice.59.refs_0_, bf16[70,48,1536]{2,1,0:T(8,128)(2,1)} %bitcast.40), custom_call_target="tpu_custom_call" | custom-call | flops 330301440 | tf_op jit(solution)/shard_map/forward_dft/pallas_call | solution.py:156
  13.0 6.9 %all-to-all-start = ((f32[16,8,3456]{2,1,0:T(8,128)}), f32[16,8,3456]{2,1,0:T(8,128)}, u32[]{:S(2)}, u32[]{:S(2)}) async-start(f32[16,8,3456]{2,1,0:T(8,128)} %bitcast.49), calls=%async_computation | async-start | bytes 3538944 | tf_op jit(solution)/shard_map/all_to_all | solution.py:432
  20.9 23.9 %forward_dft.4 = (f32[128,10112]{1,0:T(8,128)}, bf16[384,3072]{1,0:T(8,128)(2,1)}, f32[8,128]{1,0:T(8,128)}) custom-call(s32[384,1]{1,0:T(8,128)} %slice.60.refs_0_, bf16[70,48,1536]{2,1,0:T(8,128)(2,1)} %bitcast.41), custom_call_target="tpu_custom_call" | custom-call | flops 990904320 | tf_op jit(solution)/shard_map/forward_dft/pallas_call | solution.py:156
  44.8 15.4 %all-to-all-done.refs_0_.refs_1_.refs_2_ = f32[16,8,3456]{2,1,0:T(8,128)} async-done(((f32[16,8,3456]{2,1,0:T(8,128)}), f32[16,8,3456]{2,1,0:T(8,128)}, u32[]{:S(2)}, u32[]{:S(2)}) %all-to-all-start) | async-done | bytes 1769504 | tf_op jit(solution)/shard_map/all_to_all | solution.py:432
  60.2 5.0 all-to-all-start.1
  66.1 1.0 broadcast_multiply_fusion
  68.1 8.1 %spectral_adjoint.6 = (f32[4,144,384]{2,1,0:T(8,128)}, f32[4,144,384]{2,1,0:T(8,128)}) custom-call(f32[16,8,3456]{2,1,0:T(8,128)} %all-to-all-done.refs_0_.refs_1_.refs_2_, f32[16,8,3456]{2,1,0:T(8,128)} %all-to-all-done.refs_0_.refs_1_.refs_2_, f32[24,768,384]{2,1,0:T(8,128)} %refs_6_.1, f32[288,144]{1,0:T(8,128)} %copy-done.2), custom_call_target="tpu_custom_call" | custom-call | flops 254803968 | tf_op jit(solution)/shard_map/spectral_adjoint/pallas_call | solution.py:223
  76.2 3.1 collective-permute-start
  81.0 3.5 copy.22
  84.5 2.7 pad.25
  87.3 10.0 %collective-permute-done.refs_2_ = f32[4,144,384]{2,1,0:T(8,128)} collective-permute-done((f32[4,144,384]{2,1,0:T(8,128)}, f32[4,144,384]{2,1,0:T(8,128)}, u32[]{:S(2)}, u32[]{:S(2)}) %collective-permute-start) | collective-permute-done | bytes 884768 | tf_op jit(solution)/shard_map/ppermute | solution.py:27
  97.3 5.1 gradient_step.6
  102.4 1.7 collective-permute-start.4
  105.9 17.2 %forward_dft.5 = (f32[128,6784]{1,0:T(8,128)}, bf16[256,3072]{1,0:T(8,128)(2,1)}, f32[8,128]{1,0:T(8,128)}) custom-call(s32[256,1]{1,0:T(8,128)} %slice.61.refs_0_, bf16[70,48,1536]{2,1,0:T(8,128)(2,1)} %bitcast.42, f32[16,8,3456]{2,1,0:T(8,128)} %all-to-all-done.refs_0_.refs_1_.refs_2_), custom_call_target="tpu_custom_call" | custom-call | flops 660602880 | tf_op jit(solution)/shard_map/forward_dft/pallas_call | solution.py:156
  123.1 1.6 collective-permute-done.4.refs_2_
  124.8 54.0 %all-to-all-done.1.refs_0_.refs_1_ = f32[16,8,10112]{2,1,0:T(8,128)} async-done(((f32[16,8,10112]{2,1,0:T(8,128)}), f32[16,8,10112]{2,1,0:T(8,128)}, u32[]{:S(2)}, u32[]{:S(2)}) %all-to-all-start.1) | async-done | bytes 5177376 | tf_op jit(solution)/shard_map/all_to_all | solution.py:432
  178.8 4.9 all-to-all-start.2
  183.7 8.2 %spectral_adjoint.7 = (f32[4,144,384]{2,1,0:T(8,128)}, f32[4,144,384]{2,1,0:T(8,128)}) custom-call(f32[16,8,10112]{2,1,0:T(8,128)} %all-to-all-done.1.refs_0_.refs_1_, f32[16,8,10112]{2,1,0:T(8,128)} %all-to-all-done.1.refs_0_.refs_1_, f32[24,768,384]{2,1,0:T(8,128)} %refs_6_.1, f32[288,144]{1,0:T(8,128)} %copy-done.2), custom_call_target="tpu_custom_call" | custom-call | flops 254803968 | tf_op jit(solution)/shard_map/spectral_adjoint/pallas_call | solution.py:223
  191.9 2.4 collective-permute-start.1
  194.3 8.2 %spectral_adjoint.8 = (f32[4,144,384]{2,1,0:T(8,128)}, f32[4,144,384]{2,1,0:T(8,128)}) custom-call(f32[16,8,10112]{2,1,0:T(8,128)} %all-to-all-done.1.refs_0_.refs_1_, f32[16,8,10112]{2,1,0:T(8,128)} %all-to-all-done.1.refs_0_.refs_1_, f32[24,768,384]{2,1,0:T(8,128)} %refs_6_.1, f32[288,144]{1,0:T(8,128)} %copy-done.2, ...), custom_call_target="tpu_custom_call" | custom-call | flops 254803968 | tf_op jit(solution)/shard_map/spectral_adjoint/pallas_call | solution.py:223
  202.5 2.2 collective-permute-start.2
  204.7 8.3 %collective-permute-done.1.refs_2_ = f32[4,144,384]{2,1,0:T(8,128)S(1)} collective-permute-done((f32[4,144,384]{2,1,0:T(8,128)}, f32[4,144,384]{2,1,0:T(8,128)S(1)}, u32[]{:S(2)}, u32[]{:S(2)}) %collective-permute-start.1) | collective-permute-done | bytes 884768 | tf_op jit(solution)/shard_map/ppermute | solution.py:27
  213.0 0.9 copy-done.16
  213.9 5.1 gradient_step.7
  219.0 1.3 collective-permute-start.5
  220.3 8.2 %spectral_adjoint.9 = (f32[4,144,384]{2,1,0:T(8,128)}, f32[4,144,384]{2,1,0:T(8,128)}) custom-call(f32[16,8,10112]{2,1,0:T(8,128)} %all-to-all-done.1.refs_0_.refs_1_, f32[16,8,10112]{2,1,0:T(8,128)} %all-to-all-done.1.refs_0_.refs_1_, f32[24,768,384]{2,1,0:T(8,128)} %refs_6_.1, f32[288,144]{1,0:T(8,128)} %copy-done.2, ...), custom_call_target="tpu_custom_call" | custom-call | flops 254803968 | tf_op jit(solution)/shard_map/spectral_adjoint/pallas_call | solution.py:223
  228.4 5.1 collective-permute-start.3
  233.6 5.1 gradient_step.8
  238.6 1.7 collective-permute-start.9
  240.3 1.7 mul.127.refs_5_.refs_3_.refs_7_
  242.0 14.5 %spectral_forward.3 = (f32[16,8,6784]{2,1,0:T(8,128)}, f32[8,128]{1,0:T(8,128)}) custom-call(f32[4,144,384]{2,1,0:T(8,128)} %get-tuple-element.55.refs_0_, f32[4,144,384]{2,1,0:T(8,128)} %get-tuple-element.56.refs_1_, f32[4,144,384]{2,1,0:T(8,128)} %copy-done.4, f32[4,144,384]{2,1,0:T(8,128)} %collective-permute-done.5.refs_3_, f32[24,768,384]{2,1,0:T(8,128)} %refs_6_.1, ...), custom_call_target="tpu_custom_call" | custom-call | flops 509607936 | tf_op jit(solution)/shard_map/spectral_forward/pallas_call | solution.py:341
  256.5 3.1 collective-permute-done.9.refs_3_.refs_2_
  259.6 1.5 all-to-all-done.2.refs_0_.refs_1_
  261.0 7.5 %all-to-all-start.3 = ((f32[16,8,6784]{2,1,0:T(8,128)}), f32[16,8,6784]{2,1,0:T(8,128)}, u32[]{:S(2)}, u32[]{:S(2)}) async-start(f32[16,8,6784]{2,1,0:T(8,128)} %gate.7), calls=%async_computation.3 | async-start | bytes 6946816 | tf_op jit(solution)/shard_map/all_to_all | solution.py:432
  268.6 8.1 %spectral_adjoint.10 = (f32[4,144,384]{2,1,0:T(8,128)}, f32[4,144,384]{2,1,0:T(8,128)}) custom-call(f32[16,8,6784]{2,1,0:T(8,128)} %all-to-all-done.2.refs_0_.refs_1_, f32[16,8,6784]{2,1,0:T(8,128)} %all-to-all-done.2.refs_0_.refs_1_, f32[24,768,384]{2,1,0:T(8,128)} %refs_6_.1, f32[288,144]{1,0:T(8,128)} %copy-done.2), custom_call_target="tpu_custom_call" | custom-call | flops 254803968 | tf_op jit(solution)/shard_map/spectral_adjoint/pallas_call | solution.py:223
  276.7 3.2 collective-permute-start.6
  279.9 5.2 gradient_step.9
  285.0 1.3 collective-permute-start.10
  286.3 11.4 %collective-permute-done.6.refs_2_ = f32[4,144,384]{2,1,0:T(8,128)} collective-permute-done((f32[4,144,384]{2,1,0:T(8,128)}, f32[4,144,384]{2,1,0:T(8,128)}, u32[]{:S(2)}, u32[]{:S(2)}) %collective-permute-start.6) | collective-permute-done | bytes 884768 | tf_op jit(solution)/shard_map/ppermute | solution.py:27
  297.7 5.1 gradient_step.10
  302.9 1.3 collective-permute-start.11
  304.2 8.1 %spectral_adjoint.11 = (f32[4,144,384]{2,1,0:T(8,128)}, f32[4,144,384]{2,1,0:T(8,128)}) custom-call(f32[16,8,6784]{2,1,0:T(8,128)} %all-to-all-done.2.refs_0_.refs_1_, f32[16,8,6784]{2,1,0:T(8,128)} %all-to-all-done.2.refs_0_.refs_1_, f32[24,768,384]{2,1,0:T(8,128)} %refs_6_.1, f32[288,144]{1,0:T(8,128)} %copy-done.2, ...), custom_call_target="tpu_custom_call" | custom-call | flops 254803968 | tf_op jit(solution)/shard_map/spectral_adjoint/pallas_call | solution.py:223
  312.3 14.6 %collective-permute-done.11.refs_5_ = f32[4,144,384]{2,1,0:T(8,128)} collective-permute-done((f32[4,144,384]{2,1,0:T(8,128)}, f32[4,144,384]{2,1,0:T(8,128)}, u32[]{:S(2)}, u32[]{:S(2)}) %collective-permute-start.11) | collective-permute-done | bytes 884768 | tf_op jit(solution)/shard_map/ppermute | solution.py:27
  326.9 20.3 %spectral_forward.5 = (f32[16,8,10112]{2,1,0:T(8,128)}, f32[8,128]{1,0:T(8,128)}) custom-call(f32[4,144,384]{2,1,0:T(8,128)} %get-tuple-element.71.refs_0_, f32[4,144,384]{2,1,0:T(8,128)} %get-tuple-element.72.refs_1_, f32[4,144,384]{2,1,0:T(8,128)} %get-tuple-element.73.refs_2_, f32[4,144,384]{2,1,0:T(8,128)} %collective-permute-done.9.refs_3_.refs_2_, ...), custom_call_target="tpu_custom_call" | custom-call | flops 764411904 | tf_op jit(solution)/shard_map/spectral_forward/pallas_call | solution.py:341
  347.2 7.2 %all-to-all-start.4 = ((f32[16,8,10112]{2,1,0:T(8,128)}), f32[16,8,10112]{2,1,0:T(8,128)}, u32[]{:S(2)}, u32[]{:S(2)}) async-start(f32[16,8,10112]{2,1,0:T(8,128)} %gate.8), calls=%async_computation.4 | async-start | bytes 10354688 | tf_op jit(solution)/shard_map/all_to_all | solution.py:432
  354.4 1.8 collective-permute-start.7
  356.1 18.3 %collective-permute-done.7.refs_2_ = f32[4,144,384]{2,1,0:T(8,128)S(1)} collective-permute-done((f32[4,144,384]{2,1,0:T(8,128)S(1)}, f32[4,144,384]{2,1,0:T(8,128)S(1)}, u32[]{:S(2)}, u32[]{:S(2)}) %collective-permute-start.7) | collective-permute-done | bytes 884768 | tf_op jit(solution)/shard_map/ppermute | solution.py:27
  374.5 0.9 copy-done.10
  375.4 5.1 gradient_step.11
  380.5 1.3 collective-permute-start.8
  381.8 1.2 slice.55
  383.0 2.5 pad_maximum_fusion.1.refs_1_.refs_2_
  385.5 17.8 %collective-permute-done.8.refs_1_ = f32[4,144,384]{2,1,0:T(8,128)S(1)} collective-permute-done((f32[4,144,384]{2,1,0:T(8,128)}, f32[4,144,384]{2,1,0:T(8,128)S(1)}, u32[]{:S(2)}, u32[]{:S(2)}) %collective-permute-start.8) | collective-permute-done | bytes 884768 | tf_op jit(solution)/shard_map/ppermute | solution.py:27
  403.2 0.9 copy-done.9
  404.1 8.7 %spectral_forward.4 = (f32[16,8,3456]{2,1,0:T(8,128)}, f32[8,128]{1,0:T(8,128)}) custom-call(f32[4,144,384]{2,1,0:T(8,128)} %get-tuple-element.68.refs_0_, f32[4,144,384]{2,1,0:T(8,128)} %copy-done.9, f32[24,768,384]{2,1,0:T(8,128)} %refs_6_.1, f32[144,144]{1,0:T(8,128)} %mul.127.refs_5_.refs_3_.refs_7_), custom_call_target="tpu_custom_call" | custom-call | flops 254803968 | tf_op jit(solution)/shard_map/spectral_forward/pallas_call | solution.py:341
  412.9 19.3 %inverse_dft.3.refs_2_.refs_3_ = f32[70,48,1536]{2,1,0:T(8,128)} custom-call(f32[128,6784]{1,0:T(8,128)} %bitcast.13.refs_0_, bf16[256,3072]{1,0:T(8,128)(2,1)} %pad_maximum_fusion.1.refs_1_.refs_2_, bf16[256,3072]{1,0:T(8,128)(2,1)} %pad_maximum_fusion.1.refs_1_.refs_2_), custom_call_target="tpu_custom_call" | custom-call | flops 990904320 | tf_op jit(solution)/shard_map/inverse_dft/pallas_call | solution.py:401
  432.2 35.7 %all-to-all-done.4.refs_1_ = f32[16,8,10112]{2,1,0:T(8,128)} async-done(((f32[16,8,10112]{2,1,0:T(8,128)}), f32[16,8,10112]{2,1,0:T(8,128)}, u32[]{:S(2)}, u32[]{:S(2)}) %all-to-all-start.4) | async-done | bytes 5177376 | tf_op jit(solution)/shard_map/all_to_all | solution.py:432
  467.9 5.4 %all-to-all-start.5 = ((f32[16,8,3456]{2,1,0:T(8,128)}), f32[16,8,3456]{2,1,0:T(8,128)}, u32[]{:S(2)}, u32[]{:S(2)}) async-start(f32[16,8,3456]{2,1,0:T(8,128)} %gate.9), calls=%async_computation.5 | async-start | bytes 3538944 | tf_op jit(solution)/shard_map/all_to_all | solution.py:432
  473.4 2.5 fusion.2
  476.0 1.6 pad_maximum_fusion.refs_1_.refs_2_
  478.8 3.9 copy.28
  482.7 29.8 %inverse_dft.4.refs_3_ = f32[70,48,1536]{2,1,0:T(8,128)} custom-call(f32[128,10112]{1,0:T(8,128)} %bitcast.15.refs_0_, bf16[384,3072]{1,0:T(8,128)(2,1)} %pad_maximum_fusion.refs_1_.refs_2_, bf16[384,3072]{1,0:T(8,128)(2,1)} %pad_maximum_fusion.refs_1_.refs_2_, f32[70,48,1536]{2,1,0:T(8,128)} %inverse_dft.3.refs_2_.refs_3_), custom_call_target="tpu_custom_call" | custom-call | flops 1486356480 | tf_op jit(solution)/shard_map/inverse_dft/pallas_call | solution.py:401
  512.5 1.1 all-to-all-done.5
  513.6 16.2 %inverse_dft.5 = bf16[70,48,1536]{2,1,0:T(8,128)(2,1)} custom-call(f32[128,3456]{1,0:T(8,128)} %bitcast.14.refs_0_, bf16[128,3072]{1,0:T(8,128)(2,1)} %get-tuple-element.83.refs_1_.refs_2_, bf16[128,3072]{1,0:T(8,128)(2,1)} %get-tuple-element.83.refs_1_.refs_2_, f32[70,48,1536]{2,1,0:T(8,128)} %inverse_dft.4.refs_3_), custom_call_target="tpu_custom_call" | custom-call | flops 495452160 | tf_op jit(solution)/shard_map/inverse_dft/pallas_call | solution.py:401
  (93 shorter events, 8.7 us)
Async XLA Ops:
  0.6 64.9 %copy-start = (f32[70,70]{1,0:T(8,128)S(1)}, f32[70,70]{1,0:T(8,128)}, u32[]{:S(2)}) copy-start(f32[70,70]{1,0:T(8,128)} %param.11) | copy-start | bytes 58804
  1.4 18.4 %copy-start.19 = (s32[16,6,4]{2,1,0:T(8,128)}, s32[16,6,4]{2,1,0:T(8,128)S(1)}, u32[]{:S(2)}) copy-start(s32[16,6,4]{2,1,0:T(8,128)S(1)} %reshape.77) | copy-start | bytes 4612
  13.0 47.2 %all-to-all-start = ((f32[16,8,3456]{2,1,0:T(8,128)}), f32[16,8,3456]{2,1,0:T(8,128)}, u32[]{:S(2)}, u32[]{:S(2)}) async-start(f32[16,8,3456]{2,1,0:T(8,128)} %bitcast.49), calls=%async_computation | async-start | bytes 3538944 | tf_op jit(solution)/shard_map/all_to_all | solution.py:432
  60.2 5.0 copy-start.18
  60.2 5.1 copy-start.17
  60.2 118.6 %all-to-all-start.1 = ((f32[16,8,10112]{2,1,0:T(8,128)}), f32[16,8,10112]{2,1,0:T(8,128)}, u32[]{:S(2)}, u32[]{:S(2)}) async-start(f32[16,8,10112]{2,1,0:T(8,128)} %gate.5), calls=%async_computation.1 | async-start | bytes 10354688 | tf_op jit(solution)/shard_map/all_to_all | solution.py:432
  67.4 0.7 copy-start.2
  76.2 21.1 %collective-permute-start = (f32[4,144,384]{2,1,0:T(8,128)}, f32[4,144,384]{2,1,0:T(8,128)}, u32[]{:S(2)}, u32[]{:S(2)}) collective-permute-start(f32[4,144,384]{2,1,0:T(8,128)} %get-tuple-element.44), channel_id=1, source_target_pairs={{16,0},{17,1},{18,2},{19,3},{20,4},{21,5},{22,6},{23,7},{24,8},{25... | collective-permute-start | bytes 2654216 | tf_op jit(solution)/shard_map/ppermute | solution.py:27
  87.3 10.1 %copy-start.3 = (f32[288,144]{1,0:T(8,128)}, f32[288,144]{1,0:T(8,128)S(1)}, u32[]{:S(2)}) copy-start(f32[288,144]{1,0:T(8,128)S(1)} %constant_dynamic-update-slice_fusion.2.refs_5_) | copy-start | bytes 497668
  102.4 22.4 %collective-permute-start.4 = (f32[4,144,384]{2,1,0:T(8,128)}, f32[4,144,384]{2,1,0:T(8,128)S(1)}, u32[]{:S(2)}, u32[]{:S(2)}) collective-permute-start(f32[4,144,384]{2,1,0:T(8,128)} %get-tuple-element.57), channel_id=1, source_target_pairs={{0,16},{1,17},{2,18},{3,19},{4,20},{5,21},{6,22},{7,23},{8,24},{9,... | collective-permute-start | bytes 2654216 | tf_op jit(solution)/shard_map/ppermute | solution.py:27
  124.8 54.0 %copy-start.4 = (f32[4,144,384]{2,1,0:T(8,128)}, f32[4,144,384]{2,1,0:T(8,128)S(1)}, u32[]{:S(2)}) copy-start(f32[4,144,384]{2,1,0:T(8,128)S(1)} %collective-permute-done.4.refs_2_) | copy-start | bytes 2654212
  178.8 82.2 %all-to-all-start.2 = ((f32[16,8,6784]{2,1,0:T(8,128)}), f32[16,8,6784]{2,1,0:T(8,128)}, u32[]{:S(2)}, u32[]{:S(2)}) async-start(f32[16,8,6784]{2,1,0:T(8,128)} %gate.6), calls=%async_computation.2 | async-start | bytes 6946816 | tf_op jit(solution)/shard_map/all_to_all | solution.py:432
  191.9 21.1 %collective-permute-start.1 = (f32[4,144,384]{2,1,0:T(8,128)}, f32[4,144,384]{2,1,0:T(8,128)S(1)}, u32[]{:S(2)}, u32[]{:S(2)}) collective-permute-start(f32[4,144,384]{2,1,0:T(8,128)} %get-tuple-element.48), channel_id=1, source_target_pairs={{16,0},{17,1},{18,2},{19,3},{20,4},{21,5},{22,6},{23,7},{24,8},{25... | collective-permute-start | bytes 2654216 | tf_op jit(solution)/shard_map/ppermute | solution.py:27
  202.5 31.1 %collective-permute-start.2 = (f32[4,144,384]{2,1,0:T(8,128)}, f32[4,144,384]{2,1,0:T(8,128)}, u32[]{:S(2)}, u32[]{:S(2)}) collective-permute-start(f32[4,144,384]{2,1,0:T(8,128)} %get-tuple-element.51), channel_id=1, source_target_pairs={{16,0},{17,1},{18,2},{19,3},{20,4},{21,5},{22,6},{23,7},{24,8},{25... | collective-permute-start | bytes 2654216 | tf_op jit(solution)/shard_map/ppermute | solution.py:27
  213.0 0.9 copy-start.16
  219.0 23.0 %collective-permute-start.5 = (f32[4,144,384]{2,1,0:T(8,128)}, f32[4,144,384]{2,1,0:T(8,128)}, u32[]{:S(2)}, u32[]{:S(2)}) collective-permute-start(f32[4,144,384]{2,1,0:T(8,128)} %get-tuple-element.58), channel_id=1, source_target_pairs={{0,16},{1,17},{2,18},{3,19},{4,20},{5,21},{6,22},{7,23},{8,24},{9,... | collective-permute-start | bytes 2654216 | tf_op jit(solution)/shard_map/ppermute | solution.py:27
  228.4 28.0 %collective-permute-start.3 = (f32[4,144,384]{2,1,0:T(8,128)}, f32[4,144,384]{2,1,0:T(8,128)S(1)}, u32[]{:S(2)}, u32[]{:S(2)}) collective-permute-start(f32[4,144,384]{2,1,0:T(8,128)} %get-tuple-element.54), channel_id=1, source_target_pairs={{16,0},{17,1},{18,2},{19,3},{20,4},{21,5},{22,6},{23,7},{24,8},{25... | collective-permute-start | bytes 2654216 | tf_op jit(solution)/shard_map/ppermute | solution.py:27
  238.6 20.9 %collective-permute-start.9 = (f32[4,144,384]{2,1,0:T(8,128)}, f32[4,144,384]{2,1,0:T(8,128)}, u32[]{:S(2)}, u32[]{:S(2)}) collective-permute-start(f32[4,144,384]{2,1,0:T(8,128)} %get-tuple-element.74), channel_id=1, source_target_pairs={{0,16},{1,17},{2,18},{3,19},{4,20},{5,21},{6,22},{7,23},{8,24},{9,... | collective-permute-start | bytes 2654216 | tf_op jit(solution)/shard_map/ppermute | solution.py:27
  256.5 4.5 copy-start.7
  261.0 86.2 %all-to-all-start.3 = ((f32[16,8,6784]{2,1,0:T(8,128)}), f32[16,8,6784]{2,1,0:T(8,128)}, u32[]{:S(2)}, u32[]{:S(2)}) async-start(f32[16,8,6784]{2,1,0:T(8,128)} %gate.7), calls=%async_computation.3 | async-start | bytes 6946816 | tf_op jit(solution)/shard_map/all_to_all | solution.py:432
  276.7 21.1 %collective-permute-start.6 = (f32[4,144,384]{2,1,0:T(8,128)}, f32[4,144,384]{2,1,0:T(8,128)}, u32[]{:S(2)}, u32[]{:S(2)}) collective-permute-start(f32[4,144,384]{2,1,0:T(8,128)} %get-tuple-element.63), channel_id=1, source_target_pairs={{16,0},{17,1},{18,2},{19,3},{20,4},{21,5},{22,6},{23,7},{24,8},{25... | collective-permute-start | bytes 2654216 | tf_op jit(solution)/shard_map/ppermute | solution.py:27
  285.0 27.2 %collective-permute-start.10 = (f32[4,144,384]{2,1,0:T(8,128)}, f32[4,144,384]{2,1,0:T(8,128)S(1)}, u32[]{:S(2)}, u32[]{:S(2)}) collective-permute-start(f32[4,144,384]{2,1,0:T(8,128)} %get-tuple-element.75), channel_id=1, source_target_pairs={{0,16},{1,17},{2,18},{3,19},{4,20},{5,21},{6,22},{7,23},{8,24},{9,... | collective-permute-start | bytes 2654216 | tf_op jit(solution)/shard_map/ppermute | solution.py:27
  302.9 24.1 %collective-permute-start.11 = (f32[4,144,384]{2,1,0:T(8,128)}, f32[4,144,384]{2,1,0:T(8,128)}, u32[]{:S(2)}, u32[]{:S(2)}) collective-permute-start(f32[4,144,384]{2,1,0:T(8,128)} %get-tuple-element.76), channel_id=1, source_target_pairs={{0,16},{1,17},{2,18},{3,19},{4,20},{5,21},{6,22},{7,23},{8,24},{9,... | collective-permute-start | bytes 2654216 | tf_op jit(solution)/shard_map/ppermute | solution.py:27
  312.3 14.6 %copy-start.15 = (f32[4,144,384]{2,1,0:T(8,128)}, f32[4,144,384]{2,1,0:T(8,128)S(1)}, u32[]{:S(2)}) copy-start(f32[4,144,384]{2,1,0:T(8,128)S(1)} %collective-permute-done.10.refs_4_) | copy-start | bytes 2654212
  347.2 7.2 %copy-start.20 = (f32[4,144,384]{2,1,0:T(8,128)S(1)}, f32[4,144,384]{2,1,0:T(8,128)}, u32[]{:S(2)}) copy-start(f32[4,144,384]{2,1,0:T(8,128)} %get-tuple-element.66) | copy-start | bytes 2654212
  347.2 120.7 %all-to-all-start.4 = ((f32[16,8,10112]{2,1,0:T(8,128)}), f32[16,8,10112]{2,1,0:T(8,128)}, u32[]{:S(2)}, u32[]{:S(2)}) async-start(f32[16,8,10112]{2,1,0:T(8,128)} %gate.8), calls=%async_computation.4 | async-start | bytes 10354688 | tf_op jit(solution)/shard_map/all_to_all | solution.py:432
  354.4 20.1 %collective-permute-start.7 = (f32[4,144,384]{2,1,0:T(8,128)S(1)}, f32[4,144,384]{2,1,0:T(8,128)S(1)}, u32[]{:S(2)}, u32[]{:S(2)}) collective-permute-start(f32[4,144,384]{2,1,0:T(8,128)S(1)} %copy-done.20), channel_id=1, source_target_pairs={{16,0},{17,1},{18,2},{19,3},{20,4},{21,5},{22,6},{23,7},{24,8},{25... | collective-permute-start | bytes 2654216 | tf_op jit(solution)/shard_map/ppermute | solution.py:27
  374.5 0.9 copy-start.10
  380.5 22.8 %collective-permute-start.8 = (f32[4,144,384]{2,1,0:T(8,128)}, f32[4,144,384]{2,1,0:T(8,128)S(1)}, u32[]{:S(2)}, u32[]{:S(2)}) collective-permute-start(f32[4,144,384]{2,1,0:T(8,128)} %get-tuple-element.69), channel_id=1, source_target_pairs={{0,16},{1,17},{2,18},{3,19},{4,20},{5,21},{6,22},{7,23},{8,24},{9,... | collective-permute-start | bytes 2654216 | tf_op jit(solution)/shard_map/ppermute | solution.py:27
  403.2 0.9 copy-start.9
  467.9 5.4 %copy-start.8 = (bf16[384,3072]{1,0:T(8,128)(2,1)S(1)}, bf16[384,3072]{1,0:T(8,128)(2,1)}, u32[]{:S(2)}) copy-start(bf16[384,3072]{1,0:T(8,128)(2,1)} %get-tuple-element.80) | copy-start | bytes 7077892
  467.9 45.7 %all-to-all-start.5 = ((f32[16,8,3456]{2,1,0:T(8,128)}), f32[16,8,3456]{2,1,0:T(8,128)}, u32[]{:S(2)}, u32[]{:S(2)}) async-start(f32[16,8,3456]{2,1,0:T(8,128)} %gate.9), calls=%async_computation.5 | async-start | bytes 3538944 | tf_op jit(solution)/shard_map/all_to_all | solution.py:432
  473.3 4.2 copy-start.11
  473.4 4.2 copy-start.5
  473.4 4.3 copy-start.12
  476.0 1.8 copy-start.13
  476.0 2.3 copy-start.6
  477.5 1.2 copy-start.14
  513.6 16.2 %copy-start.1 = (f32[70,70]{1,0:T(8,128)S(1)}, f32[70,70]{1,0:T(8,128)}, u32[]{:S(2)}) copy-start(f32[70,70]{1,0:T(8,128)} %param.11) | copy-start | bytes 58804

commit v4 on v3

--- a/solution.py
+++ b/solution.py
@@ -113,7 +113,7 @@
         return pieces
 
 
-def dft_kernel(steps, place, slot_ref, grad_ref, out_ref, wave_ref, mark_ref, rows_ref):
+def dft_kernel(steps, place, slot_ref, grad_ref, out_ref, wave_ref, mark_ref, rows_ref, right_ref):
     mark_ref[...] = jnp.zeros(mark_ref.shape, jnp.float32)
     levels, lats, lons = grad_ref.shape
     waves = wave_ref.shape[0]
@@ -123,10 +123,14 @@
     def _():
         for unit in range(place.units):
             at = slice(unit * LANES, (unit + 1) * LANES)
-            wave_ref[at, :lons], wave_ref[at, lons:] = halves(wave_rows(slot_ref[at, :], lons))
+            rows = wave_rows(slot_ref[at, :], lons)
+            wave_ref[at, :lons], wave_ref[at, lons:] = halves(rows)
+            high, rest = halves(rows.T)
+            right_ref[:, at] = high
+            right_ref[:, waves + unit * LANES : waves + (unit + 1) * LANES] = rest
 
     grad = grad_ref[...].reshape(levels * lats, lons)
-    terms = mxu(grad, jnp.concatenate([wave_ref[:, :lons], wave_ref[:, lons:]], axis=0), NT)
+    terms = mxu(grad, right_ref[...], NN)
     coef = terms[:, :waves] + terms[:, waves:]
     for unit in range(place.units):
         rows_ref[unit, 0 : levels * lats, :] = coef[:, unit * LANES : (unit + 1) * LANES]
@@ -171,7 +175,10 @@
             jax.ShapeDtypeStruct((waves, 2 * lons), jnp.bfloat16),
             MARK,
         ],
-        scratch_shapes=[pltpu.VMEM((place.units, lead * block, LANES), jnp.float32)],
+        scratch_shapes=[
+            pltpu.VMEM((place.units, lead * block, LANES), jnp.float32),
+            pltpu.VMEM((lons, 2 * waves), jnp.bfloat16),
+        ],
         compiler_params=pltpu.CompilerParams(vmem_limit_bytes=VMEM_BYTES),
         cost_estimate=cost(4 * levels * lats * lons * waves),
         name="forward_dft",
@@ -280,10 +287,10 @@
     )(step_size, own, got, control, mode, mat, *after)
 
 
-def back_kernel(place, *refs):
-    units = place.units
+def back_kernel(place, units, skip, *refs):
     keep_refs, got_refs = refs[:units], refs[units : 2 * units]
-    leg_ref, mat_ref, out_ref, mark_ref, cols_ref, line_ref, flat_ref = refs[2 * units :]
+    leg_ref, mat_ref = refs[2 * units : 2 * units + 2]
+    out_ref, mark_ref, cols_ref, line_ref, flat_ref = refs[-5:]
     mark_ref[...] = jnp.zeros(mark_ref.shape, jnp.float32)
     devices, rows, _ = out_ref.shape
     slots, lat_count, degrees = leg_ref.shape
@@ -298,10 +305,11 @@
 
         @pl.when(pl.program_id(0) == unit)
         def _(unit=unit):
-            if unit == 0:
-                out_ref[:, :, units * place.full :] = jnp.zeros(
-                    (devices, rows, place.lanes - units * place.full), jnp.float32
-                )
+            if unit == 0 and skip:
+                out_ref[...] = refs[2 * units + 2][...]
+            elif unit == 0:
+                ends = place.units * place.full
+                out_ref[:, :, ends:] = jnp.zeros((devices, rows, place.lanes - ends), jnp.float32)
             if place.tail:
                 unused = (line_ref.shape[0], LANES - place.tail)
                 line_ref[:, place.full + place.tail :] = jnp.zeros(unused, jnp.float32)
@@ -322,29 +330,32 @@
                             line, tile * LANES : (tile + 1) * LANES
                         ]
             for tile in range(tiles):
-                start = unit * place.full + tile * LANES
+                start = (skip + unit) * place.full + tile * LANES
                 out_ref[:, :, start : start + LANES] = flat_ref[tile].reshape(devices, rows, LANES)
             if place.tail:
-                lane = place.end(unit)
+                lane = place.end(skip + unit)
                 ends = flat_ref[tiles].reshape(devices, rows, LANES)[:, :, : place.tail]
                 out_ref[:, :, lane : lane + place.tail] = ends
 
 
-def spectral_back(keeps, gots, place, legendre, first, mat, devices, after):
+def spectral_back(keeps, gots, place, legendre, first, mat, devices, before, skip, after):
     slots, lead, degrees = keeps[0].shape
     lat_count = legendre.shape[1]
     rows = 2 * slots
-    units = place.units
+    units = len(keeps)
     spec = pl.BlockSpec(keeps[0].shape, lambda i: (0, 0, 0))
     padded_row = place.full + (LANES if place.tail else 0)
     shape = jax.ShapeDtypeStruct((devices, rows, place.lanes), jnp.float32)
     return pl.pallas_call(
-        behind(functools.partial(back_kernel, place), 2 * units + 2, len(after)),
+        behind(
+            functools.partial(back_kernel, place, units, skip), 2 * units + 2 + len(before), len(after)
+        ),
         grid=(units,),
         in_specs=[spec] * (2 * units)
         + [
             pl.BlockSpec((slots, lat_count, degrees), lambda i: (i + first, 0, 0)),
             pl.BlockSpec(mat.shape, lambda i: (0, 0)),
+            *[pl.BlockSpec(b.shape, lambda i: (0, 0, 0)) for b in before],
             *anywhere(after),
         ],
         out_specs=[pl.BlockSpec(shape.shape, lambda i: (0, 0, 0)), MARK_SPEC],
@@ -357,7 +368,7 @@
         compiler_params=pltpu.CompilerParams(vmem_limit_bytes=VMEM_BYTES),
         cost_estimate=cost(12 * units * slots * lat_count * degrees * lead),
         name="spectral_forward",
-    )(*keeps, *gots, legendre, mat, *after)
+    )(*keeps, *gots, legendre, mat, *before, *after)
 
 
 def inverse_kernel(steps, place, has_total, coef_ref, up_ref, low_ref, *refs):
@@ -483,10 +494,16 @@
             after = (new[u],)
             back_other[u] = from_behind(back_send[u], "var", 1)
 
-    def forward(group, *after):
-        keeps, gots = [keep[u] for u in group], [back_other[u] for u in group]
+    def forward(group, parts=1):
         at = Rows(lats, levels, len(group))
-        return spectral_back(keeps, gots, at, legendre, group[0], remap_mat, devices, after)
+        before, skip = [], 0
+        for some in [group] if parts == 1 else [group[:-1], group[-1:]]:
+            keeps, gots = [keep[u] for u in some], [back_other[u] for u in some]
+            back, mark = spectral_back(
+                keeps, gots, at, legendre, some[0], remap_mat, devices, before, skip, ()
+            )
+            before, skip = [back], len(some)
+        return back, mark
 
     def inverse(group, arrived, total, dtype, *after):
         at = Rows(lats, levels, len(group))
@@ -519,7 +536,7 @@
         arrived_a = exchange(gate(back_a, got_c, back_other[members[1][-2]], other[members[1][-1]]))
         adjoint(2, got_c)
         gradient_step(members[2])
-        back_b, _ = forward(middle)
+        back_b, _ = forward(middle, 2)
         arrived_b = exchange(gate(back_b, arrived_a, own[members[2][-1]]))
         back_c, _ = forward(late)
         total = inverse(early, arrived_a, None, jnp.float32)

time: 535 us -> 533 us (level)
  waiting for transfers between devices: 193 us -> 187 us
    ppermute x12, waiting for transfers between devices: 85.2 us -> 75.6 us  [from_behind(): return lax.ppermute(block, axis, route)]
    pallas_call x3 -> x4, Pallas kernels: 43.5 us -> 49.8 us  [spectral_back(): pl.pallas_call(behind(functools.partial(back_kernel, place, units, skip),...]
  transfers between devices with their start and end apart: 18 -> 18, of which waited for: 13 -> 14; matrix products, arithmetic and copies ran while one was open for 5% -> 5% of each run, Pallas kernels for 40% -> 41%
where the time goes in v4:
time: 533 us; the launch traced here: 528 us
  Pallas kernels  243 us (46%)
  waiting for transfers between devices  187 us (35%)
  starting transfers between devices  63.2 us (12%)
  local copies, waits for them, and re-layouts  27.7 us (5%)
    all_to_all x6, waiting for transfers between devices, exchange(): return lax.all_to_all(block, 'lat', split_axis=0, concat_axis=0, tiled=True)  112 us
    ppermute x12, waiting for transfers between devices, from_behind(): return lax.ppermute(block, axis, route)  75.6 us
    pallas_call x3, Pallas kernels, inverse_dft(): pl.pallas_call(behind(functools.partial(inverse_kernel, steps, place, len...  65.4 us
    pallas_call x4, Pallas kernels, spectral_back(): pl.pallas_call(behind(functools.partial(back_kernel, place, units, skip),...  49.8 us
    pallas_call x6, Pallas kernels, spectral(): pl.pallas_call(behind(functools.partial(spectral_kernel, place), 4, len(a...  48.8 us
    pallas_call x3, Pallas kernels, forward_dft(): pl.pallas_call(behind(functools.partial(dft_kernel, steps, place), 2, len...  48.1 us
    all_to_all x6, starting transfers between devices, exchange(): return lax.all_to_all(block, 'lat', split_axis=0, concat_axis=0, tiled=True)  37 us
    pallas_call x6, Pallas kernels, update(): pl.pallas_call(behind(update_kernel, 6, len(after)), grid=(1,), in_specs=...  30.4 us
  transfers between devices with their start and end apart: 18, of which 14 were waited for; matrix products, arithmetic and copies ran while one was open for 5% of the time, Pallas kernels for 41%

profile of v4, /device:TPU:15, one launch (start us, length us, event | category | flops | bytes accessed | tf_op | source)
XLA Modules:
  0.0 528.3 jit_solution(6239468703123299610)
XLA Ops:
  2.4 10.0 %forward_dft.3 = (f32[128,3456]{1,0:T(8,128)}, bf16[128,3072]{1,0:T(8,128)(2,1)}, f32[8,128]{1,0:T(8,128)}) custom-call(s32[128,1]{1,0:T(8,128)} %slice.59.refs_0_, bf16[70,48,1536]{2,1,0:T(8,128)(2,1)} %bitcast.40), custom_call_target="tpu_custom_call" | custom-call | flops 330301440 | tf_op jit(solution)/shard_map/forward_dft/pallas_call | solution.py:160
  12.4 6.9 %all-to-all-start = ((f32[16,8,3456]{2,1,0:T(8,128)}), f32[16,8,3456]{2,1,0:T(8,128)}, u32[]{:S(2)}, u32[]{:S(2)}) async-start(f32[16,8,3456]{2,1,0:T(8,128)} %bitcast.49), calls=%async_computation | async-start | bytes 3538944 | tf_op jit(solution)/shard_map/all_to_all | solution.py:443
  20.3 22.1 %forward_dft.4 = (f32[128,10112]{1,0:T(8,128)}, bf16[384,3072]{1,0:T(8,128)(2,1)}, f32[8,128]{1,0:T(8,128)}) custom-call(s32[384,1]{1,0:T(8,128)} %slice.60.refs_0_, bf16[70,48,1536]{2,1,0:T(8,128)(2,1)} %bitcast.41), custom_call_target="tpu_custom_call" | custom-call | flops 990904320 | tf_op jit(solution)/shard_map/forward_dft/pallas_call | solution.py:160
  42.4 17.2 %all-to-all-done.refs_0_.refs_1_.refs_2_ = f32[16,8,3456]{2,1,0:T(8,128)} async-done(((f32[16,8,3456]{2,1,0:T(8,128)}), f32[16,8,3456]{2,1,0:T(8,128)}, u32[]{:S(2)}, u32[]{:S(2)}) %all-to-all-start) | async-done | bytes 1769504 | tf_op jit(solution)/shard_map/all_to_all | solution.py:443
  59.7 5.4 %all-to-all-start.1 = ((f32[16,8,10112]{2,1,0:T(8,128)}), f32[16,8,10112]{2,1,0:T(8,128)}, u32[]{:S(2)}, u32[]{:S(2)}) async-start(f32[16,8,10112]{2,1,0:T(8,128)} %gate.5), calls=%async_computation.1 | async-start | bytes 10354688 | tf_op jit(solution)/shard_map/all_to_all | solution.py:443
  65.9 1.0 broadcast_multiply_fusion
  67.9 8.1 %spectral_adjoint.6 = (f32[4,144,384]{2,1,0:T(8,128)}, f32[4,144,384]{2,1,0:T(8,128)}) custom-call(f32[16,8,3456]{2,1,0:T(8,128)} %all-to-all-done.refs_0_.refs_1_.refs_2_, f32[16,8,3456]{2,1,0:T(8,128)} %all-to-all-done.refs_0_.refs_1_.refs_2_, f32[24,768,384]{2,1,0:T(8,128)} %refs_2_.15, f32[288,144]{1,0:T(8,128)} %copy-done.2), custom_call_target="tpu_custom_call" | custom-call | flops 254803968 | tf_op jit(solution)/shard_map/spectral_adjoint/pallas_call | solution.py:230
  76.0 3.1 collective-permute-start
  80.8 3.5 copy.22
  84.3 2.7 pad.25
  87.1 10.0 %collective-permute-done.refs_2_ = f32[4,144,384]{2,1,0:T(8,128)} collective-permute-done((f32[4,144,384]{2,1,0:T(8,128)}, f32[4,144,384]{2,1,0:T(8,128)}, u32[]{:S(2)}, u32[]{:S(2)}) %collective-permute-start) | collective-permute-done | bytes 884768 | tf_op jit(solution)/shard_map/ppermute | solution.py:27
  97.1 5.1 gradient_step.6
  102.2 1.7 collective-permute-start.4
  105.8 16.0 %forward_dft.5 = (f32[128,6784]{1,0:T(8,128)}, bf16[256,3072]{1,0:T(8,128)(2,1)}, f32[8,128]{1,0:T(8,128)}) custom-call(s32[256,1]{1,0:T(8,128)} %slice.61.refs_0_, bf16[70,48,1536]{2,1,0:T(8,128)(2,1)} %bitcast.42, f32[16,8,3456]{2,1,0:T(8,128)} %all-to-all-done.refs_0_.refs_1_.refs_2_), custom_call_target="tpu_custom_call" | custom-call | flops 660602880 | tf_op jit(solution)/shard_map/forward_dft/pallas_call | solution.py:160
  121.7 2.9 collective-permute-done.4.refs_2_
  124.6 53.9 %all-to-all-done.1.refs_0_.refs_1_ = f32[16,8,10112]{2,1,0:T(8,128)} async-done(((f32[16,8,10112]{2,1,0:T(8,128)}), f32[16,8,10112]{2,1,0:T(8,128)}, u32[]{:S(2)}, u32[]{:S(2)}) %all-to-all-start.1) | async-done | bytes 5177376 | tf_op jit(solution)/shard_map/all_to_all | solution.py:443
  178.5 4.9 all-to-all-start.2
  183.4 8.1 %spectral_adjoint.7 = (f32[4,144,384]{2,1,0:T(8,128)}, f32[4,144,384]{2,1,0:T(8,128)}) custom-call(f32[16,8,10112]{2,1,0:T(8,128)} %all-to-all-done.1.refs_0_.refs_1_, f32[16,8,10112]{2,1,0:T(8,128)} %all-to-all-done.1.refs_0_.refs_1_, f32[24,768,384]{2,1,0:T(8,128)} %refs_2_.15, f32[288,144]{1,0:T(8,128)} %copy-done.2), custom_call_target="tpu_custom_call" | custom-call | flops 254803968 | tf_op jit(solution)/shard_map/spectral_adjoint/pallas_call | solution.py:230
  191.5 3.2 collective-permute-start.1
  194.7 8.1 %spectral_adjoint.8 = (f32[4,144,384]{2,1,0:T(8,128)}, f32[4,144,384]{2,1,0:T(8,128)}) custom-call(f32[16,8,10112]{2,1,0:T(8,128)} %all-to-all-done.1.refs_0_.refs_1_, f32[16,8,10112]{2,1,0:T(8,128)} %all-to-all-done.1.refs_0_.refs_1_, f32[24,768,384]{2,1,0:T(8,128)} %refs_2_.15, f32[288,144]{1,0:T(8,128)} %copy-done.2, ...), custom_call_target="tpu_custom_call" | custom-call | flops 254803968 | tf_op jit(solution)/shard_map/spectral_adjoint/pallas_call | solution.py:230
  202.9 1.3 collective-permute-start.2
  204.2 8.4 %collective-permute-done.1.refs_2_ = f32[4,144,384]{2,1,0:T(8,128)} collective-permute-done((f32[4,144,384]{2,1,0:T(8,128)}, f32[4,144,384]{2,1,0:T(8,128)}, u32[]{:S(2)}, u32[]{:S(2)}) %collective-permute-start.1) | collective-permute-done | bytes 884768 | tf_op jit(solution)/shard_map/ppermute | solution.py:27
  212.6 5.1 gradient_step.7
  217.7 1.3 collective-permute-start.5
  219.0 8.2 %spectral_adjoint.9 = (f32[4,144,384]{2,1,0:T(8,128)}, f32[4,144,384]{2,1,0:T(8,128)}) custom-call(f32[16,8,10112]{2,1,0:T(8,128)} %all-to-all-done.1.refs_0_.refs_1_, f32[16,8,10112]{2,1,0:T(8,128)} %all-to-all-done.1.refs_0_.refs_1_, f32[24,768,384]{2,1,0:T(8,128)} %refs_2_.15, f32[288,144]{1,0:T(8,128)} %copy-done.2, ...), custom_call_target="tpu_custom_call" | custom-call | flops 254803968 | tf_op jit(solution)/shard_map/spectral_adjoint/pallas_call | solution.py:230
  227.1 6.0 %collective-permute-start.3 = (f32[4,144,384]{2,1,0:T(8,128)}, f32[4,144,384]{2,1,0:T(8,128)}, u32[]{:S(2)}, u32[]{:S(2)}) collective-permute-start(f32[4,144,384]{2,1,0:T(8,128)} %get-tuple-element.55), channel_id=1, source_target_pairs={{16,0},{17,1},{18,2},{19,3},{20,4},{21,5},{22,6},{23,7},{24,8},{25... | collective-permute-start | bytes 2654216 | tf_op jit(solution)/shard_map/ppermute | solution.py:27
  233.1 0.9 copy-done.11
  234.0 5.0 gradient_step.8
  239.1 1.5 collective-permute-start.10
  240.6 1.7 mul.127.refs_5_.refs_3_
  242.3 14.5 %spectral_forward.4 = (f32[16,8,6784]{2,1,0:T(8,128)}, f32[8,128]{1,0:T(8,128)}) custom-call(f32[4,144,384]{2,1,0:T(8,128)} %get-tuple-element.56.refs_0_, f32[4,144,384]{2,1,0:T(8,128)} %get-tuple-element.57.refs_1_, f32[4,144,384]{2,1,0:T(8,128)} %copy-done.4, f32[4,144,384]{2,1,0:T(8,128)} %collective-permute-done.5.refs_3_, f32[24,768,384]{2,1,0:T(8,128)} %refs_2_.15, ...), custom_call_target="tpu_custom_call" | custom-call | flops 509607936 | tf_op jit(solution)/shard_map/spectral_forward/pallas_call | solution.py:349
  256.7 3.2 collective-permute-done.10.refs_2_
  260.9 8.9 %all-to-all-start.3 = ((f32[16,8,6784]{2,1,0:T(8,128)}), f32[16,8,6784]{2,1,0:T(8,128)}, u32[]{:S(2)}, u32[]{:S(2)}) async-start(f32[16,8,6784]{2,1,0:T(8,128)} %gate.7), calls=%async_computation.3 | async-start | bytes 6946816 | tf_op jit(solution)/shard_map/all_to_all | solution.py:443
  269.8 8.1 %spectral_adjoint.10 = (f32[4,144,384]{2,1,0:T(8,128)}, f32[4,144,384]{2,1,0:T(8,128)}) custom-call(f32[16,8,6784]{2,1,0:T(8,128)} %all-to-all-done.2.refs_0_.refs_1_, f32[16,8,6784]{2,1,0:T(8,128)} %all-to-all-done.2.refs_0_.refs_1_, f32[24,768,384]{2,1,0:T(8,128)} %refs_2_.15, f32[288,144]{1,0:T(8,128)} %copy-done.2), custom_call_target="tpu_custom_call" | custom-call | flops 254803968 | tf_op jit(solution)/shard_map/spectral_adjoint/pallas_call | solution.py:230
  277.9 2.6 collective-permute-start.6
  280.5 5.0 gradient_step.9
  285.6 1.3 collective-permute-start.11
  286.9 11.3 %collective-permute-done.6.refs_2_ = f32[4,144,384]{2,1,0:T(8,128)} collective-permute-done((f32[4,144,384]{2,1,0:T(8,128)}, f32[4,144,384]{2,1,0:T(8,128)}, u32[]{:S(2)}, u32[]{:S(2)}) %collective-permute-start.6) | collective-permute-done | bytes 884768 | tf_op jit(solution)/shard_map/ppermute | solution.py:27
  298.2 5.1 gradient_step.10
  303.3 1.3 collective-permute-start.9
  304.6 3.7 collective-permute-done.11.refs_3_
  308.4 0.9 copy-done.9
  309.3 15.1 %spectral_forward.6 = (f32[16,8,10112]{2,1,0:T(8,128)}, f32[8,128]{1,0:T(8,128)}) custom-call(f32[4,144,384]{2,1,0:T(8,128)} %get-tuple-element.74.refs_0_, f32[4,144,384]{2,1,0:T(8,128)} %get-tuple-element.75.refs_1_, f32[4,144,384]{2,1,0:T(8,128)} %copy-done.5, f32[4,144,384]{2,1,0:T(8,128)} %copy-done.9, f32[24,768,384]{2,1,0:T(8,128)} %refs_2_.15, ...), custom_call_target="tpu_custom_call" | custom-call | flops 509607936 | tf_op jit(solution)/shard_map/spectral_forward/pallas_call | solution.py:349
  324.4 8.1 %spectral_adjoint.11 = (f32[4,144,384]{2,1,0:T(8,128)}, f32[4,144,384]{2,1,0:T(8,128)}) custom-call(f32[16,8,6784]{2,1,0:T(8,128)} %all-to-all-done.2.refs_0_.refs_1_, f32[16,8,6784]{2,1,0:T(8,128)} %all-to-all-done.2.refs_0_.refs_1_, f32[24,768,384]{2,1,0:T(8,128)} %refs_2_.15, f32[288,144]{1,0:T(8,128)} %copy-done.2, ...), custom_call_target="tpu_custom_call" | custom-call | flops 254803968 | tf_op jit(solution)/shard_map/spectral_adjoint/pallas_call | solution.py:230
  332.6 11.5 %spectral_forward.7 = (f32[16,8,10112]{2,1,0:T(8,128)}, f32[8,128]{1,0:T(8,128)}) custom-call(f32[4,144,384]{2,1,0:T(8,128)} %get-tuple-element.72.refs_0_, f32[4,144,384]{2,1,0:T(8,128)} %collective-permute-done.9.refs_1_, f32[24,768,384]{2,1,0:T(8,128)} %refs_2_.15, f32[144,144]{1,0:T(8,128)} %mul.127.refs_5_.refs_3_, ...), custom_call_target="tpu_custom_call" | custom-call | flops 254803968 | tf_op jit(solution)/shard_map/spectral_forward/pallas_call | solution.py:349
  344.1 2.8 all-to-all-done.3.refs_1_
  346.8 5.4 %all-to-all-start.4 = ((f32[16,8,10112]{2,1,0:T(8,128)}), f32[16,8,10112]{2,1,0:T(8,128)}, u32[]{:S(2)}, u32[]{:S(2)}) async-start(f32[16,8,10112]{2,1,0:T(8,128)} %gate.8), calls=%async_computation.4 | async-start | bytes 10354688 | tf_op jit(solution)/shard_map/all_to_all | solution.py:443
  352.3 1.3 collective-permute-start.7
  353.7 18.6 %collective-permute-done.7.refs_2_ = f32[4,144,384]{2,1,0:T(8,128)S(1)} collective-permute-done((f32[4,144,384]{2,1,0:T(8,128)S(1)}, f32[4,144,384]{2,1,0:T(8,128)S(1)}, u32[]{:S(2)}, u32[]{:S(2)}) %collective-permute-start.7) | collective-permute-done | bytes 884768 | tf_op jit(solution)/shard_map/ppermute | solution.py:27
  373.2 5.1 gradient_step.11
  378.3 1.5 collective-permute-start.8
  379.8 1.2 slice.55
  380.9 2.5 pad_maximum_fusion.1.refs_1_.refs_2_
  383.5 17.4 %collective-permute-done.8.refs_1_ = f32[4,144,384]{2,1,0:T(8,128)S(1)} collective-permute-done((f32[4,144,384]{2,1,0:T(8,128)}, f32[4,144,384]{2,1,0:T(8,128)S(1)}, u32[]{:S(2)}, u32[]{:S(2)}) %collective-permute-start.8) | collective-permute-done | bytes 884768 | tf_op jit(solution)/shard_map/ppermute | solution.py:27
  401.8 8.7 %spectral_forward.5 = (f32[16,8,3456]{2,1,0:T(8,128)}, f32[8,128]{1,0:T(8,128)}) custom-call(f32[4,144,384]{2,1,0:T(8,128)} %get-tuple-element.69.refs_0_, f32[4,144,384]{2,1,0:T(8,128)} %copy-done.10, f32[24,768,384]{2,1,0:T(8,128)} %refs_2_.15, f32[144,144]{1,0:T(8,128)} %mul.127.refs_5_.refs_3_), custom_call_target="tpu_custom_call" | custom-call | flops 254803968 | tf_op jit(solution)/shard_map/spectral_forward/pallas_call | solution.py:349
  410.5 19.4 %inverse_dft.3.refs_2_.refs_3_ = f32[70,48,1536]{2,1,0:T(8,128)} custom-call(f32[128,6784]{1,0:T(8,128)} %bitcast.13.refs_0_, bf16[256,3072]{1,0:T(8,128)(2,1)} %pad_maximum_fusion.1.refs_1_.refs_2_, bf16[256,3072]{1,0:T(8,128)(2,1)} %pad_maximum_fusion.1.refs_1_.refs_2_), custom_call_target="tpu_custom_call" | custom-call | flops 990904320 | tf_op jit(solution)/shard_map/inverse_dft/pallas_call | solution.py:412
  429.9 35.9 %all-to-all-done.4.refs_1_ = f32[16,8,10112]{2,1,0:T(8,128)} async-done(((f32[16,8,10112]{2,1,0:T(8,128)}), f32[16,8,10112]{2,1,0:T(8,128)}, u32[]{:S(2)}, u32[]{:S(2)}) %all-to-all-start.4) | async-done | bytes 5177376 | tf_op jit(solution)/shard_map/all_to_all | solution.py:443
  465.8 5.4 %all-to-all-start.5 = ((f32[16,8,3456]{2,1,0:T(8,128)}), f32[16,8,3456]{2,1,0:T(8,128)}, u32[]{:S(2)}, u32[]{:S(2)}) async-start(f32[16,8,3456]{2,1,0:T(8,128)} %gate.9), calls=%async_computation.5 | async-start | bytes 3538944 | tf_op jit(solution)/shard_map/all_to_all | solution.py:443
  471.4 2.5 fusion.2
  474.0 1.6 pad_maximum_fusion.refs_1_.refs_2_
  476.8 3.9 copy.28
  480.7 29.8 %inverse_dft.4.refs_3_ = f32[70,48,1536]{2,1,0:T(8,128)} custom-call(f32[128,10112]{1,0:T(8,128)} %bitcast.15.refs_0_, bf16[384,3072]{1,0:T(8,128)(2,1)} %pad_maximum_fusion.refs_1_.refs_2_, bf16[384,3072]{1,0:T(8,128)(2,1)} %pad_maximum_fusion.refs_1_.refs_2_, f32[70,48,1536]{2,1,0:T(8,128)} %inverse_dft.3.refs_2_.refs_3_), custom_call_target="tpu_custom_call" | custom-call | flops 1486356480 | tf_op jit(solution)/shard_map/inverse_dft/pallas_call | solution.py:412
  510.5 1.1 all-to-all-done.5
  511.6 16.2 %inverse_dft.5 = bf16[70,48,1536]{2,1,0:T(8,128)(2,1)} custom-call(f32[128,3456]{1,0:T(8,128)} %bitcast.14.refs_0_, bf16[128,3072]{1,0:T(8,128)(2,1)} %get-tuple-element.85.refs_1_.refs_2_, bf16[128,3072]{1,0:T(8,128)(2,1)} %get-tuple-element.85.refs_1_.refs_2_, f32[70,48,1536]{2,1,0:T(8,128)} %inverse_dft.4.refs_3_), custom_call_target="tpu_custom_call" | custom-call | flops 495452160 | tf_op jit(solution)/shard_map/inverse_dft/pallas_call | solution.py:412
  (94 shorter events, 11.4 us)
Async XLA Ops:
  0.6 64.7 %copy-start = (f32[70,70]{1,0:T(8,128)S(1)}, f32[70,70]{1,0:T(8,128)}, u32[]{:S(2)}) copy-start(f32[70,70]{1,0:T(8,128)} %param.11) | copy-start | bytes 58804
  1.4 17.9 %copy-start.19 = (s32[16,6,4]{2,1,0:T(8,128)}, s32[16,6,4]{2,1,0:T(8,128)S(1)}, u32[]{:S(2)}) copy-start(s32[16,6,4]{2,1,0:T(8,128)S(1)} %reshape.77) | copy-start | bytes 4612
  12.4 47.3 %all-to-all-start = ((f32[16,8,3456]{2,1,0:T(8,128)}), f32[16,8,3456]{2,1,0:T(8,128)}, u32[]{:S(2)}, u32[]{:S(2)}) async-start(f32[16,8,3456]{2,1,0:T(8,128)} %bitcast.49), calls=%async_computation | async-start | bytes 3538944 | tf_op jit(solution)/shard_map/all_to_all | solution.py:443
  59.7 5.4 %copy-start.18 = (f32[1,70,70]{2,0,1:T(1,128)S(1)}, f32[1,70,70]{2,0,1:T(1,128)}, u32[]{:S(2)}) copy-start(f32[1,70,70]{2,0,1:T(1,128)} %param.9) | copy-start | bytes 58804
  59.7 5.6 %copy-start.17 = (f32[1,70,70]{2,0,1:T(1,128)S(1)}, f32[1,70,70]{2,0,1:T(1,128)}, u32[]{:S(2)}) copy-start(f32[1,70,70]{2,0,1:T(1,128)} %param.10) | copy-start | bytes 58804
  59.7 118.8 %all-to-all-start.1 = ((f32[16,8,10112]{2,1,0:T(8,128)}), f32[16,8,10112]{2,1,0:T(8,128)}, u32[]{:S(2)}, u32[]{:S(2)}) async-start(f32[16,8,10112]{2,1,0:T(8,128)} %gate.5), calls=%async_computation.1 | async-start | bytes 10354688 | tf_op jit(solution)/shard_map/all_to_all | solution.py:443
  67.2 0.7 copy-start.2
  76.0 21.1 %collective-permute-start = (f32[4,144,384]{2,1,0:T(8,128)}, f32[4,144,384]{2,1,0:T(8,128)}, u32[]{:S(2)}, u32[]{:S(2)}) collective-permute-start(f32[4,144,384]{2,1,0:T(8,128)} %get-tuple-element.45), channel_id=1, source_target_pairs={{16,0},{17,1},{18,2},{19,3},{20,4},{21,5},{22,6},{23,7},{24,8},{25... | collective-permute-start | bytes 2654216 | tf_op jit(solution)/shard_map/ppermute | solution.py:27
  87.1 10.0 %copy-start.3 = (f32[288,144]{1,0:T(8,128)}, f32[288,144]{1,0:T(8,128)S(1)}, u32[]{:S(2)}) copy-start(f32[288,144]{1,0:T(8,128)S(1)} %constant_dynamic-update-slice_fusion.2.refs_5_) | copy-start | bytes 497668
  102.2 22.4 %collective-permute-start.4 = (f32[4,144,384]{2,1,0:T(8,128)}, f32[4,144,384]{2,1,0:T(8,128)S(1)}, u32[]{:S(2)}, u32[]{:S(2)}) collective-permute-start(f32[4,144,384]{2,1,0:T(8,128)} %get-tuple-element.58), channel_id=1, source_target_pairs={{0,16},{1,17},{2,18},{3,19},{4,20},{5,21},{6,22},{7,23},{8,24},{9,... | collective-permute-start | bytes 2654216 | tf_op jit(solution)/shard_map/ppermute | solution.py:27
  124.6 53.9 %copy-start.4 = (f32[4,144,384]{2,1,0:T(8,128)}, f32[4,144,384]{2,1,0:T(8,128)S(1)}, u32[]{:S(2)}) copy-start(f32[4,144,384]{2,1,0:T(8,128)S(1)} %collective-permute-done.4.refs_2_) | copy-start | bytes 2654212
  178.5 82.1 %all-to-all-start.2 = ((f32[16,8,6784]{2,1,0:T(8,128)}), f32[16,8,6784]{2,1,0:T(8,128)}, u32[]{:S(2)}, u32[]{:S(2)}) async-start(f32[16,8,6784]{2,1,0:T(8,128)} %gate.6), calls=%async_computation.2 | async-start | bytes 6946816 | tf_op jit(solution)/shard_map/all_to_all | solution.py:443
  191.5 21.1 %collective-permute-start.1 = (f32[4,144,384]{2,1,0:T(8,128)}, f32[4,144,384]{2,1,0:T(8,128)}, u32[]{:S(2)}, u32[]{:S(2)}) collective-permute-start(f32[4,144,384]{2,1,0:T(8,128)} %get-tuple-element.49), channel_id=1, source_target_pairs={{16,0},{17,1},{18,2},{19,3},{20,4},{21,5},{22,6},{23,7},{24,8},{25... | collective-permute-start | bytes 2654216 | tf_op jit(solution)/shard_map/ppermute | solution.py:27
  202.9 30.2 %collective-permute-start.2 = (f32[4,144,384]{2,1,0:T(8,128)}, f32[4,144,384]{2,1,0:T(8,128)S(1)}, u32[]{:S(2)}, u32[]{:S(2)}) collective-permute-start(f32[4,144,384]{2,1,0:T(8,128)} %get-tuple-element.52), channel_id=1, source_target_pairs={{16,0},{17,1},{18,2},{19,3},{20,4},{21,5},{22,6},{23,7},{24,8},{25... | collective-permute-start | bytes 2654216 | tf_op jit(solution)/shard_map/ppermute | solution.py:27
  217.7 24.6 %collective-permute-start.5 = (f32[4,144,384]{2,1,0:T(8,128)}, f32[4,144,384]{2,1,0:T(8,128)}, u32[]{:S(2)}, u32[]{:S(2)}) collective-permute-start(f32[4,144,384]{2,1,0:T(8,128)} %get-tuple-element.59), channel_id=1, source_target_pairs={{0,16},{1,17},{2,18},{3,19},{4,20},{5,21},{6,22},{7,23},{8,24},{9,... | collective-permute-start | bytes 2654216 | tf_op jit(solution)/shard_map/ppermute | solution.py:27
  227.1 29.6 %collective-permute-start.3 = (f32[4,144,384]{2,1,0:T(8,128)}, f32[4,144,384]{2,1,0:T(8,128)}, u32[]{:S(2)}, u32[]{:S(2)}) collective-permute-start(f32[4,144,384]{2,1,0:T(8,128)} %get-tuple-element.55), channel_id=1, source_target_pairs={{16,0},{17,1},{18,2},{19,3},{20,4},{21,5},{22,6},{23,7},{24,8},{25... | collective-permute-start | bytes 2654216 | tf_op jit(solution)/shard_map/ppermute | solution.py:27
  233.1 0.9 copy-start.11
  239.1 20.9 %collective-permute-start.10 = (f32[4,144,384]{2,1,0:T(8,128)}, f32[4,144,384]{2,1,0:T(8,128)S(1)}, u32[]{:S(2)}, u32[]{:S(2)}) collective-permute-start(f32[4,144,384]{2,1,0:T(8,128)} %get-tuple-element.76), channel_id=1, source_target_pairs={{0,16},{1,17},{2,18},{3,19},{4,20},{5,21},{6,22},{7,23},{8,24},{9,... | collective-permute-start | bytes 2654216 | tf_op jit(solution)/shard_map/ppermute | solution.py:27
  260.0 0.9 copy-start.5
  260.9 85.9 %all-to-all-start.3 = ((f32[16,8,6784]{2,1,0:T(8,128)}), f32[16,8,6784]{2,1,0:T(8,128)}, u32[]{:S(2)}, u32[]{:S(2)}) async-start(f32[16,8,6784]{2,1,0:T(8,128)} %gate.7), calls=%async_computation.3 | async-start | bytes 6946816 | tf_op jit(solution)/shard_map/all_to_all | solution.py:443
  277.9 20.3 %collective-permute-start.6 = (f32[4,144,384]{2,1,0:T(8,128)}, f32[4,144,384]{2,1,0:T(8,128)}, u32[]{:S(2)}, u32[]{:S(2)}) collective-permute-start(f32[4,144,384]{2,1,0:T(8,128)} %get-tuple-element.64), channel_id=1, source_target_pairs={{16,0},{17,1},{18,2},{19,3},{20,4},{21,5},{22,6},{23,7},{24,8},{25... | collective-permute-start | bytes 2654216 | tf_op jit(solution)/shard_map/ppermute | solution.py:27
  285.6 22.8 %collective-permute-start.11 = (f32[4,144,384]{2,1,0:T(8,128)}, f32[4,144,384]{2,1,0:T(8,128)S(1)}, u32[]{:S(2)}, u32[]{:S(2)}) collective-permute-start(f32[4,144,384]{2,1,0:T(8,128)} %get-tuple-element.77), channel_id=1, source_target_pairs={{0,16},{1,17},{2,18},{3,19},{4,20},{5,21},{6,22},{7,23},{8,24},{9,... | collective-permute-start | bytes 2654216 | tf_op jit(solution)/shard_map/ppermute | solution.py:27
  303.3 29.2 %collective-permute-start.9 = (f32[4,144,384]{2,1,0:T(8,128)}, f32[4,144,384]{2,1,0:T(8,128)}, u32[]{:S(2)}, u32[]{:S(2)}) collective-permute-start(f32[4,144,384]{2,1,0:T(8,128)} %get-tuple-element.73), channel_id=1, source_target_pairs={{0,16},{1,17},{2,18},{3,19},{4,20},{5,21},{6,22},{7,23},{8,24},{9,... | collective-permute-start | bytes 2654216 | tf_op jit(solution)/shard_map/ppermute | solution.py:27
  308.4 0.9 copy-start.9
  346.8 5.5 %copy-start.20 = (f32[4,144,384]{2,1,0:T(8,128)S(1)}, f32[4,144,384]{2,1,0:T(8,128)}, u32[]{:S(2)}) copy-start(f32[4,144,384]{2,1,0:T(8,128)} %get-tuple-element.67) | copy-start | bytes 2654212
  346.8 119.0 %all-to-all-start.4 = ((f32[16,8,10112]{2,1,0:T(8,128)}), f32[16,8,10112]{2,1,0:T(8,128)}, u32[]{:S(2)}, u32[]{:S(2)}) async-start(f32[16,8,10112]{2,1,0:T(8,128)} %gate.8), calls=%async_computation.4 | async-start | bytes 10354688 | tf_op jit(solution)/shard_map/all_to_all | solution.py:443
  352.3 20.0 %collective-permute-start.7 = (f32[4,144,384]{2,1,0:T(8,128)S(1)}, f32[4,144,384]{2,1,0:T(8,128)S(1)}, u32[]{:S(2)}, u32[]{:S(2)}) collective-permute-start(f32[4,144,384]{2,1,0:T(8,128)S(1)} %copy-done.20), channel_id=1, source_target_pairs={{16,0},{17,1},{18,2},{19,3},{20,4},{21,5},{22,6},{23,7},{24,8},{25... | collective-permute-start | bytes 2654216 | tf_op jit(solution)/shard_map/ppermute | solution.py:27
  372.3 0.9 copy-start.12
  378.3 22.6 %collective-permute-start.8 = (f32[4,144,384]{2,1,0:T(8,128)}, f32[4,144,384]{2,1,0:T(8,128)S(1)}, u32[]{:S(2)}, u32[]{:S(2)}) collective-permute-start(f32[4,144,384]{2,1,0:T(8,128)} %get-tuple-element.70), channel_id=1, source_target_pairs={{0,16},{1,17},{2,18},{3,19},{4,20},{5,21},{6,22},{7,23},{8,24},{9,... | collective-permute-start | bytes 2654216 | tf_op jit(solution)/shard_map/ppermute | solution.py:27
  400.9 0.9 copy-start.10
  465.8 5.4 %copy-start.8 = (bf16[384,3072]{1,0:T(8,128)(2,1)S(1)}, bf16[384,3072]{1,0:T(8,128)(2,1)}, u32[]{:S(2)}) copy-start(bf16[384,3072]{1,0:T(8,128)(2,1)} %get-tuple-element.82) | copy-start | bytes 7077892
  465.8 45.8 %all-to-all-start.5 = ((f32[16,8,3456]{2,1,0:T(8,128)}), f32[16,8,3456]{2,1,0:T(8,128)}, u32[]{:S(2)}, u32[]{:S(2)}) async-start(f32[16,8,3456]{2,1,0:T(8,128)} %gate.9), calls=%async_computation.5 | async-start | bytes 3538944 | tf_op jit(solution)/shard_map/all_to_all | solution.py:443
  471.3 4.2 copy-start.13
  471.4 4.2 copy-start.6
  471.4 4.3 copy-start.14
  474.0 1.8 copy-start.15
  474.0 2.3 copy-start.7
  475.5 1.2 copy-start.16
  511.6 16.2 %copy-start.1 = (f32[70,70]{1,0:T(8,128)S(1)}, f32[70,70]{1,0:T(8,128)}, u32[]{:S(2)}) copy-start(f32[70,70]{1,0:T(8,128)} %param.11) | copy-start | bytes 58804

commit v5 on v4

--- a/solution.py
+++ b/solution.py
@@ -533,7 +533,7 @@
         early, middle, late = members[0] + members[1][:1], members[1][1:] + members[2][:1], members[2][1:]
         back_a, mark = forward(early)
         gradient_step(members[1][-1:], mark)
-        arrived_a = exchange(gate(back_a, got_c, back_other[members[1][-2]], other[members[1][-1]]))
+        arrived_a = exchange(gate(back_a, got_c, other[members[1][-1]]))
         adjoint(2, got_c)
         gradient_step(members[2])
         back_b, _ = forward(middle, 2)

time: 533 us -> 564 us (1.058)
  waiting for transfers between devices: 187 us -> 213 us
    ppermute x12, waiting for transfers between devices: 75.6 us -> 104 us  [from_behind(): return lax.ppermute(block, axis, route)]
  transfers between devices with their start and end apart: 18 -> 18, of which waited for: 14 -> 15; matrix products, arithmetic and copies ran while one was open for 5% -> 5% of each run, Pallas kernels for 41% -> 39%
where the time goes in v5:
time: 564 us; the launch traced here: 559 us
  Pallas kernels  243 us (43%)
  waiting for transfers between devices  213 us (38%)
  starting transfers between devices  68.5 us (12%)
  local copies, waits for them, and re-layouts  27.4 us (5%)
    all_to_all x6, waiting for transfers between devices, exchange(): return lax.all_to_all(block, 'lat', split_axis=0, concat_axis=0, tiled=True)  109 us
    ppermute x12, waiting for transfers between devices, from_behind(): return lax.ppermute(block, axis, route)  104 us
    pallas_call x3, Pallas kernels, inverse_dft(): pl.pallas_call(behind(functools.partial(inverse_kernel, steps, place, len...  65.5 us
    pallas_call x4, Pallas kernels, spectral_back(): pl.pallas_call(behind(functools.partial(back_kernel, place, units, skip),...  49.8 us
    pallas_call x6, Pallas kernels, spectral(): pl.pallas_call(behind(functools.partial(spectral_kernel, place), 4, len(a...  48.8 us
    pallas_call x3, Pallas kernels, forward_dft(): pl.pallas_call(behind(functools.partial(dft_kernel, steps, place), 2, len...  48.1 us
    all_to_all x6, starting transfers between devices, exchange(): return lax.all_to_all(block, 'lat', split_axis=0, concat_axis=0, tiled=True)  41.4 us
    pallas_call x6, Pallas kernels, update(): pl.pallas_call(behind(update_kernel, 6, len(after)), grid=(1,), in_specs=...  30.5 us
  transfers between devices with their start and end apart: 18, of which 15 were waited for; matrix products, arithmetic and copies ran while one was open for 5% of the time, Pallas kernels for 39%

profile of v5, /device:TPU:15, one launch (start us, length us, event | category | flops | bytes accessed | tf_op | source)
XLA Modules:
  0.0 559.3 jit_solution(6449152377278240059)
XLA Ops:
  2.4 10.0 %forward_dft.3 = (f32[128,3456]{1,0:T(8,128)}, bf16[128,3072]{1,0:T(8,128)(2,1)}, f32[8,128]{1,0:T(8,128)}) custom-call(s32[128,1]{1,0:T(8,128)} %slice.59.refs_0_, bf16[70,48,1536]{2,1,0:T(8,128)(2,1)} %bitcast.40), custom_call_target="tpu_custom_call" | custom-call | flops 330301440 | tf_op jit(solution)/shard_map/forward_dft/pallas_call | solution.py:160
  12.4 6.9 %all-to-all-start = ((f32[16,8,3456]{2,1,0:T(8,128)}), f32[16,8,3456]{2,1,0:T(8,128)}, u32[]{:S(2)}, u32[]{:S(2)}) async-start(f32[16,8,3456]{2,1,0:T(8,128)} %bitcast.49), calls=%async_computation | async-start | bytes 3538944 | tf_op jit(solution)/shard_map/all_to_all | solution.py:443
  20.3 22.1 %forward_dft.4 = (f32[128,10112]{1,0:T(8,128)}, bf16[384,3072]{1,0:T(8,128)(2,1)}, f32[8,128]{1,0:T(8,128)}) custom-call(s32[384,1]{1,0:T(8,128)} %slice.60.refs_0_, bf16[70,48,1536]{2,1,0:T(8,128)(2,1)} %bitcast.41), custom_call_target="tpu_custom_call" | custom-call | flops 990904320 | tf_op jit(solution)/shard_map/forward_dft/pallas_call | solution.py:160
  42.4 17.2 %all-to-all-done.refs_0_.refs_1_.refs_2_ = f32[16,8,3456]{2,1,0:T(8,128)} async-done(((f32[16,8,3456]{2,1,0:T(8,128)}), f32[16,8,3456]{2,1,0:T(8,128)}, u32[]{:S(2)}, u32[]{:S(2)}) %all-to-all-start) | async-done | bytes 1769504 | tf_op jit(solution)/shard_map/all_to_all | solution.py:443
  59.7 5.4 all-to-all-start.1
  65.9 1.0 broadcast_multiply_fusion
  67.9 8.1 %spectral_adjoint.6 = (f32[4,144,384]{2,1,0:T(8,128)}, f32[4,144,384]{2,1,0:T(8,128)}) custom-call(f32[16,8,3456]{2,1,0:T(8,128)} %all-to-all-done.refs_0_.refs_1_.refs_2_, f32[16,8,3456]{2,1,0:T(8,128)} %all-to-all-done.refs_0_.refs_1_.refs_2_, f32[24,768,384]{2,1,0:T(8,128)} %refs_2_.15, f32[288,144]{1,0:T(8,128)} %copy-done.2), custom_call_target="tpu_custom_call" | custom-call | flops 254803968 | tf_op jit(solution)/shard_map/spectral_adjoint/pallas_call | solution.py:230
  76.0 3.1 collective-permute-start
  80.8 3.5 copy.22
  84.3 2.7 pad.25
  87.1 10.0 %collective-permute-done.refs_2_ = f32[4,144,384]{2,1,0:T(8,128)} collective-permute-done((f32[4,144,384]{2,1,0:T(8,128)}, f32[4,144,384]{2,1,0:T(8,128)}, u32[]{:S(2)}, u32[]{:S(2)}) %collective-permute-start) | collective-permute-done | bytes 884768 | tf_op jit(solution)/shard_map/ppermute | solution.py:27
  97.1 5.1 gradient_step.6
  102.2 1.7 collective-permute-start.4
  105.8 16.0 %forward_dft.5 = (f32[128,6784]{1,0:T(8,128)}, bf16[256,3072]{1,0:T(8,128)(2,1)}, f32[8,128]{1,0:T(8,128)}) custom-call(s32[256,1]{1,0:T(8,128)} %slice.61.refs_0_, bf16[70,48,1536]{2,1,0:T(8,128)(2,1)} %bitcast.42, f32[16,8,3456]{2,1,0:T(8,128)} %all-to-all-done.refs_0_.refs_1_.refs_2_), custom_call_target="tpu_custom_call" | custom-call | flops 660602880 | tf_op jit(solution)/shard_map/forward_dft/pallas_call | solution.py:160
  121.7 2.9 collective-permute-done.4.refs_2_
  124.6 53.9 %all-to-all-done.1.refs_0_.refs_1_ = f32[16,8,10112]{2,1,0:T(8,128)} async-done(((f32[16,8,10112]{2,1,0:T(8,128)}), f32[16,8,10112]{2,1,0:T(8,128)}, u32[]{:S(2)}, u32[]{:S(2)}) %all-to-all-start.1) | async-done | bytes 5177376 | tf_op jit(solution)/shard_map/all_to_all | solution.py:443
  178.5 4.9 all-to-all-start.2
  183.4 8.1 %spectral_adjoint.7 = (f32[4,144,384]{2,1,0:T(8,128)}, f32[4,144,384]{2,1,0:T(8,128)}) custom-call(f32[16,8,10112]{2,1,0:T(8,128)} %all-to-all-done.1.refs_0_.refs_1_, f32[16,8,10112]{2,1,0:T(8,128)} %all-to-all-done.1.refs_0_.refs_1_, f32[24,768,384]{2,1,0:T(8,128)} %refs_2_.15, f32[288,144]{1,0:T(8,128)} %copy-done.2), custom_call_target="tpu_custom_call" | custom-call | flops 254803968 | tf_op jit(solution)/shard_map/spectral_adjoint/pallas_call | solution.py:230
  191.5 2.4 collective-permute-start.1
  193.9 18.7 %collective-permute-done.1.refs_2_ = f32[4,144,384]{2,1,0:T(8,128)S(1)} collective-permute-done((f32[4,144,384]{2,1,0:T(8,128)}, f32[4,144,384]{2,1,0:T(8,128)S(1)}, u32[]{:S(2)}, u32[]{:S(2)}) %collective-permute-start.1) | collective-permute-done | bytes 884768 | tf_op jit(solution)/shard_map/ppermute | solution.py:27
  213.5 5.1 gradient_step.7
  218.6 1.3 collective-permute-start.5
  219.9 8.2 %spectral_adjoint.8 = (f32[4,144,384]{2,1,0:T(8,128)}, f32[4,144,384]{2,1,0:T(8,128)}) custom-call(f32[16,8,10112]{2,1,0:T(8,128)} %all-to-all-done.1.refs_0_.refs_1_, f32[16,8,10112]{2,1,0:T(8,128)} %all-to-all-done.1.refs_0_.refs_1_, f32[24,768,384]{2,1,0:T(8,128)} %refs_2_.15, f32[288,144]{1,0:T(8,128)} %copy-done.2, ...), custom_call_target="tpu_custom_call" | custom-call | flops 254803968 | tf_op jit(solution)/shard_map/spectral_adjoint/pallas_call | solution.py:230
  228.1 8.2 %spectral_adjoint.9 = (f32[4,144,384]{2,1,0:T(8,128)}, f32[4,144,384]{2,1,0:T(8,128)}) custom-call(f32[16,8,10112]{2,1,0:T(8,128)} %all-to-all-done.1.refs_0_.refs_1_, f32[16,8,10112]{2,1,0:T(8,128)} %all-to-all-done.1.refs_0_.refs_1_, f32[24,768,384]{2,1,0:T(8,128)} %refs_2_.15, f32[288,144]{1,0:T(8,128)} %copy-done.2, ...), custom_call_target="tpu_custom_call" | custom-call | flops 254803968 | tf_op jit(solution)/shard_map/spectral_adjoint/pallas_call | solution.py:230
  236.2 5.3 collective-permute-start.3
  241.5 1.7 mul.127.refs_5_.refs_3_
  243.2 14.5 %spectral_forward.4 = (f32[16,8,6784]{2,1,0:T(8,128)}, f32[8,128]{1,0:T(8,128)}) custom-call(f32[4,144,384]{2,1,0:T(8,128)} %get-tuple-element.56.refs_0_, f32[4,144,384]{2,1,0:T(8,128)} %get-tuple-element.57.refs_1_, f32[4,144,384]{2,1,0:T(8,128)} %copy-done.4, f32[4,144,384]{2,1,0:T(8,128)} %collective-permute-done.5.refs_3_, f32[24,768,384]{2,1,0:T(8,128)} %refs_2_.15, ...), custom_call_target="tpu_custom_call" | custom-call | flops 509607936 | tf_op jit(solution)/shard_map/spectral_forward/pallas_call | solution.py:349
  257.7 1.5 collective-permute-done.3.refs_2_
  259.1 1.3 all-to-all-done.2.refs_0_.refs_1_
  260.4 7.6 %all-to-all-start.3 = ((f32[16,8,6784]{2,1,0:T(8,128)}), f32[16,8,6784]{2,1,0:T(8,128)}, u32[]{:S(2)}, u32[]{:S(2)}) async-start(f32[16,8,6784]{2,1,0:T(8,128)} %gate.7), calls=%async_computation.3 | async-start | bytes 6946816 | tf_op jit(solution)/shard_map/all_to_all | solution.py:443
  267.9 4.0 collective-permute-start.2
  272.0 8.1 %spectral_adjoint.10 = (f32[4,144,384]{2,1,0:T(8,128)}, f32[4,144,384]{2,1,0:T(8,128)}) custom-call(f32[16,8,6784]{2,1,0:T(8,128)} %all-to-all-done.2.refs_0_.refs_1_, f32[16,8,6784]{2,1,0:T(8,128)} %all-to-all-done.2.refs_0_.refs_1_, f32[24,768,384]{2,1,0:T(8,128)} %refs_2_.15, f32[288,144]{1,0:T(8,128)} %copy-done.2), custom_call_target="tpu_custom_call" | custom-call | flops 254803968 | tf_op jit(solution)/shard_map/spectral_adjoint/pallas_call | solution.py:230
  280.1 2.6 collective-permute-start.6
  282.7 8.2 %collective-permute-done.2.refs_2_ = f32[4,144,384]{2,1,0:T(8,128)S(1)} collective-permute-done((f32[4,144,384]{2,1,0:T(8,128)}, f32[4,144,384]{2,1,0:T(8,128)S(1)}, u32[]{:S(2)}, u32[]{:S(2)}) %collective-permute-start.2) | collective-permute-done | bytes 884768 | tf_op jit(solution)/shard_map/ppermute | solution.py:27
  291.8 5.1 gradient_step.8
  296.9 1.3 collective-permute-start.10
  298.2 5.1 gradient_step.9
  303.3 1.3 collective-permute-start.11
  304.6 5.3 collective-permute-done.6.refs_2_
  309.9 5.1 gradient_step.10
  315.0 1.3 collective-permute-start.9
  316.3 2.0 collective-permute-done.10.refs_2_
  318.3 19.0 %collective-permute-done.11.refs_3_ = f32[4,144,384]{2,1,0:T(8,128)} collective-permute-done((f32[4,144,384]{2,1,0:T(8,128)}, f32[4,144,384]{2,1,0:T(8,128)}, u32[]{:S(2)}, u32[]{:S(2)}) %collective-permute-start.11) | collective-permute-done | bytes 884768 | tf_op jit(solution)/shard_map/ppermute | solution.py:27
  337.2 15.2 %spectral_forward.6 = (f32[16,8,10112]{2,1,0:T(8,128)}, f32[8,128]{1,0:T(8,128)}) custom-call(f32[4,144,384]{2,1,0:T(8,128)} %get-tuple-element.74.refs_0_, f32[4,144,384]{2,1,0:T(8,128)} %get-tuple-element.75.refs_1_, f32[4,144,384]{2,1,0:T(8,128)} %copy-done.9, f32[4,144,384]{2,1,0:T(8,128)} %collective-permute-done.11.refs_3_, f32[24,768,384]{2,1,0:T(8,128)} %refs_2_.15, ...), custom_call_target="tpu_custom_call" | custom-call | flops 509607936 | tf_op jit(solution)/shard_map/spectral_forward/pallas_call | solution.py:349
  352.4 8.2 %spectral_adjoint.11 = (f32[4,144,384]{2,1,0:T(8,128)}, f32[4,144,384]{2,1,0:T(8,128)}) custom-call(f32[16,8,6784]{2,1,0:T(8,128)} %all-to-all-done.2.refs_0_.refs_1_, f32[16,8,6784]{2,1,0:T(8,128)} %all-to-all-done.2.refs_0_.refs_1_, f32[24,768,384]{2,1,0:T(8,128)} %refs_2_.15, f32[288,144]{1,0:T(8,128)} %copy-done.2, ...), custom_call_target="tpu_custom_call" | custom-call | flops 254803968 | tf_op jit(solution)/shard_map/spectral_adjoint/pallas_call | solution.py:230
  360.6 11.5 %spectral_forward.7 = (f32[16,8,10112]{2,1,0:T(8,128)}, f32[8,128]{1,0:T(8,128)}) custom-call(f32[4,144,384]{2,1,0:T(8,128)} %get-tuple-element.72.refs_0_, f32[4,144,384]{2,1,0:T(8,128)} %collective-permute-done.9.refs_1_, f32[24,768,384]{2,1,0:T(8,128)} %refs_2_.15, f32[144,144]{1,0:T(8,128)} %mul.127.refs_5_.refs_3_, ...), custom_call_target="tpu_custom_call" | custom-call | flops 254803968 | tf_op jit(solution)/shard_map/spectral_forward/pallas_call | solution.py:349
  372.1 11.2 %all-to-all-start.4 = ((f32[16,8,10112]{2,1,0:T(8,128)}), f32[16,8,10112]{2,1,0:T(8,128)}, u32[]{:S(2)}, u32[]{:S(2)}) async-start(f32[16,8,10112]{2,1,0:T(8,128)} %gate.8), calls=%async_computation.4 | async-start | bytes 10354688 | tf_op jit(solution)/shard_map/all_to_all | solution.py:443
  383.3 1.3 collective-permute-start.7
  384.6 18.7 %collective-permute-done.7.refs_2_ = f32[4,144,384]{2,1,0:T(8,128)S(1)} collective-permute-done((f32[4,144,384]{2,1,0:T(8,128)S(1)}, f32[4,144,384]{2,1,0:T(8,128)S(1)}, u32[]{:S(2)}, u32[]{:S(2)}) %collective-permute-start.7) | collective-permute-done | bytes 884768 | tf_op jit(solution)/shard_map/ppermute | solution.py:27
  404.3 5.1 gradient_step.11
  409.3 1.5 collective-permute-start.8
  410.8 1.2 slice.55
  412.0 2.5 pad_maximum_fusion.1.refs_1_.refs_2_
  414.5 17.5 %collective-permute-done.8.refs_1_ = f32[4,144,384]{2,1,0:T(8,128)S(1)} collective-permute-done((f32[4,144,384]{2,1,0:T(8,128)}, f32[4,144,384]{2,1,0:T(8,128)S(1)}, u32[]{:S(2)}, u32[]{:S(2)}) %collective-permute-start.8) | collective-permute-done | bytes 884768 | tf_op jit(solution)/shard_map/ppermute | solution.py:27
  433.0 8.7 %spectral_forward.5 = (f32[16,8,3456]{2,1,0:T(8,128)}, f32[8,128]{1,0:T(8,128)}) custom-call(f32[4,144,384]{2,1,0:T(8,128)} %get-tuple-element.69.refs_0_, f32[4,144,384]{2,1,0:T(8,128)} %copy-done.10, f32[24,768,384]{2,1,0:T(8,128)} %refs_2_.15, f32[144,144]{1,0:T(8,128)} %mul.127.refs_5_.refs_3_), custom_call_target="tpu_custom_call" | custom-call | flops 254803968 | tf_op jit(solution)/shard_map/spectral_forward/pallas_call | solution.py:349
  441.7 19.4 %inverse_dft.3.refs_2_.refs_3_ = f32[70,48,1536]{2,1,0:T(8,128)} custom-call(f32[128,6784]{1,0:T(8,128)} %bitcast.13.refs_0_, bf16[256,3072]{1,0:T(8,128)(2,1)} %pad_maximum_fusion.1.refs_1_.refs_2_, bf16[256,3072]{1,0:T(8,128)(2,1)} %pad_maximum_fusion.1.refs_1_.refs_2_), custom_call_target="tpu_custom_call" | custom-call | flops 990904320 | tf_op jit(solution)/shard_map/inverse_dft/pallas_call | solution.py:412
  461.1 35.7 %all-to-all-done.4.refs_1_ = f32[16,8,10112]{2,1,0:T(8,128)} async-done(((f32[16,8,10112]{2,1,0:T(8,128)}), f32[16,8,10112]{2,1,0:T(8,128)}, u32[]{:S(2)}, u32[]{:S(2)}) %all-to-all-start.4) | async-done | bytes 5177376 | tf_op jit(solution)/shard_map/all_to_all | solution.py:443
  496.8 5.4 all-to-all-start.5
  502.4 2.5 fusion.2
  504.9 1.6 pad_maximum_fusion.refs_1_.refs_2_
  507.8 3.9 copy.28
  511.7 29.8 %inverse_dft.4.refs_3_ = f32[70,48,1536]{2,1,0:T(8,128)} custom-call(f32[128,10112]{1,0:T(8,128)} %bitcast.15.refs_0_, bf16[384,3072]{1,0:T(8,128)(2,1)} %pad_maximum_fusion.refs_1_.refs_2_, bf16[384,3072]{1,0:T(8,128)(2,1)} %pad_maximum_fusion.refs_1_.refs_2_, f32[70,48,1536]{2,1,0:T(8,128)} %inverse_dft.3.refs_2_.refs_3_), custom_call_target="tpu_custom_call" | custom-call | flops 1486356480 | tf_op jit(solution)/shard_map/inverse_dft/pallas_call | solution.py:412
  541.5 1.1 all-to-all-done.5
  542.6 16.2 %inverse_dft.5 = bf16[70,48,1536]{2,1,0:T(8,128)(2,1)} custom-call(f32[128,3456]{1,0:T(8,128)} %bitcast.14.refs_0_, bf16[128,3072]{1,0:T(8,128)(2,1)} %get-tuple-element.85.refs_1_.refs_2_, bf16[128,3072]{1,0:T(8,128)(2,1)} %get-tuple-element.85.refs_1_.refs_2_, f32[70,48,1536]{2,1,0:T(8,128)} %inverse_dft.4.refs_3_), custom_call_target="tpu_custom_call" | custom-call | flops 495452160 | tf_op jit(solution)/shard_map/inverse_dft/pallas_call | solution.py:412
  (96 shorter events, 12.4 us)
Async XLA Ops:
  0.6 64.7 %copy-start = (f32[70,70]{1,0:T(8,128)S(1)}, f32[70,70]{1,0:T(8,128)}, u32[]{:S(2)}) copy-start(f32[70,70]{1,0:T(8,128)} %param.11) | copy-start | bytes 58804
  1.4 17.9 %copy-start.20 = (s32[16,6,4]{2,1,0:T(8,128)}, s32[16,6,4]{2,1,0:T(8,128)S(1)}, u32[]{:S(2)}) copy-start(s32[16,6,4]{2,1,0:T(8,128)S(1)} %reshape.77) | copy-start | bytes 4612
  12.4 47.3 %all-to-all-start = ((f32[16,8,3456]{2,1,0:T(8,128)}), f32[16,8,3456]{2,1,0:T(8,128)}, u32[]{:S(2)}, u32[]{:S(2)}) async-start(f32[16,8,3456]{2,1,0:T(8,128)} %bitcast.49), calls=%async_computation | async-start | bytes 3538944 | tf_op jit(solution)/shard_map/all_to_all | solution.py:443
  59.7 5.4 copy-start.19
  59.7 5.6 copy-start.18
  59.7 118.8 %all-to-all-start.1 = ((f32[16,8,10112]{2,1,0:T(8,128)}), f32[16,8,10112]{2,1,0:T(8,128)}, u32[]{:S(2)}, u32[]{:S(2)}) async-start(f32[16,8,10112]{2,1,0:T(8,128)} %gate.5), calls=%async_computation.1 | async-start | bytes 10354688 | tf_op jit(solution)/shard_map/all_to_all | solution.py:443
  67.2 0.7 copy-start.2
  76.0 21.1 %collective-permute-start = (f32[4,144,384]{2,1,0:T(8,128)}, f32[4,144,384]{2,1,0:T(8,128)}, u32[]{:S(2)}, u32[]{:S(2)}) collective-permute-start(f32[4,144,384]{2,1,0:T(8,128)} %get-tuple-element.45), channel_id=1, source_target_pairs={{16,0},{17,1},{18,2},{19,3},{20,4},{21,5},{22,6},{23,7},{24,8},{25... | collective-permute-start | bytes 2654216 | tf_op jit(solution)/shard_map/ppermute | solution.py:27
  87.1 10.1 %copy-start.3 = (f32[288,144]{1,0:T(8,128)}, f32[288,144]{1,0:T(8,128)S(1)}, u32[]{:S(2)}) copy-start(f32[288,144]{1,0:T(8,128)S(1)} %constant_dynamic-update-slice_fusion.2.refs_5_) | copy-start | bytes 497668
  102.2 22.4 %collective-permute-start.4 = (f32[4,144,384]{2,1,0:T(8,128)}, f32[4,144,384]{2,1,0:T(8,128)S(1)}, u32[]{:S(2)}, u32[]{:S(2)}) collective-permute-start(f32[4,144,384]{2,1,0:T(8,128)} %get-tuple-element.58), channel_id=1, source_target_pairs={{0,16},{1,17},{2,18},{3,19},{4,20},{5,21},{6,22},{7,23},{8,24},{9,... | collective-permute-start | bytes 2654216 | tf_op jit(solution)/shard_map/ppermute | solution.py:27
  124.6 53.9 %copy-start.4 = (f32[4,144,384]{2,1,0:T(8,128)}, f32[4,144,384]{2,1,0:T(8,128)S(1)}, u32[]{:S(2)}) copy-start(f32[4,144,384]{2,1,0:T(8,128)S(1)} %collective-permute-done.4.refs_2_) | copy-start | bytes 2654212
  178.5 81.9 %all-to-all-start.2 = ((f32[16,8,6784]{2,1,0:T(8,128)}), f32[16,8,6784]{2,1,0:T(8,128)}, u32[]{:S(2)}, u32[]{:S(2)}) async-start(f32[16,8,6784]{2,1,0:T(8,128)} %gate.6), calls=%async_computation.2 | async-start | bytes 6946816 | tf_op jit(solution)/shard_map/all_to_all | solution.py:443
  191.5 21.1 %collective-permute-start.1 = (f32[4,144,384]{2,1,0:T(8,128)}, f32[4,144,384]{2,1,0:T(8,128)S(1)}, u32[]{:S(2)}, u32[]{:S(2)}) collective-permute-start(f32[4,144,384]{2,1,0:T(8,128)} %get-tuple-element.49), channel_id=1, source_target_pairs={{16,0},{17,1},{18,2},{19,3},{20,4},{21,5},{22,6},{23,7},{24,8},{25... | collective-permute-start | bytes 2654216 | tf_op jit(solution)/shard_map/ppermute | solution.py:27
  212.6 1.0 copy-start.17
  218.6 24.6 %collective-permute-start.5 = (f32[4,144,384]{2,1,0:T(8,128)}, f32[4,144,384]{2,1,0:T(8,128)}, u32[]{:S(2)}, u32[]{:S(2)}) collective-permute-start(f32[4,144,384]{2,1,0:T(8,128)} %get-tuple-element.59), channel_id=1, source_target_pairs={{0,16},{1,17},{2,18},{3,19},{4,20},{5,21},{6,22},{7,23},{8,24},{9,... | collective-permute-start | bytes 2654216 | tf_op jit(solution)/shard_map/ppermute | solution.py:27
  236.2 22.9 %collective-permute-start.3 = (f32[4,144,384]{2,1,0:T(8,128)}, f32[4,144,384]{2,1,0:T(8,128)S(1)}, u32[]{:S(2)}, u32[]{:S(2)}) collective-permute-start(f32[4,144,384]{2,1,0:T(8,128)} %get-tuple-element.55), channel_id=1, source_target_pairs={{16,0},{17,1},{18,2},{19,3},{20,4},{21,5},{22,6},{23,7},{24,8},{25... | collective-permute-start | bytes 2654216 | tf_op jit(solution)/shard_map/ppermute | solution.py:27
  259.1 1.3 copy-start.7
  260.4 111.7 %all-to-all-start.3 = ((f32[16,8,6784]{2,1,0:T(8,128)}), f32[16,8,6784]{2,1,0:T(8,128)}, u32[]{:S(2)}, u32[]{:S(2)}) async-start(f32[16,8,6784]{2,1,0:T(8,128)} %gate.7), calls=%async_computation.3 | async-start | bytes 6946816 | tf_op jit(solution)/shard_map/all_to_all | solution.py:443
  267.9 23.0 %collective-permute-start.2 = (f32[4,144,384]{2,1,0:T(8,128)}, f32[4,144,384]{2,1,0:T(8,128)S(1)}, u32[]{:S(2)}, u32[]{:S(2)}) collective-permute-start(f32[4,144,384]{2,1,0:T(8,128)} %get-tuple-element.52), channel_id=1, source_target_pairs={{16,0},{17,1},{18,2},{19,3},{20,4},{21,5},{22,6},{23,7},{24,8},{25... | collective-permute-start | bytes 2654216 | tf_op jit(solution)/shard_map/ppermute | solution.py:27
  280.1 29.7 %collective-permute-start.6 = (f32[4,144,384]{2,1,0:T(8,128)}, f32[4,144,384]{2,1,0:T(8,128)}, u32[]{:S(2)}, u32[]{:S(2)}) collective-permute-start(f32[4,144,384]{2,1,0:T(8,128)} %get-tuple-element.64), channel_id=1, source_target_pairs={{16,0},{17,1},{18,2},{19,3},{20,4},{21,5},{22,6},{23,7},{24,8},{25... | collective-permute-start | bytes 2654216 | tf_op jit(solution)/shard_map/ppermute | solution.py:27
  290.9 0.9 copy-start.11
  296.9 21.4 %collective-permute-start.10 = (f32[4,144,384]{2,1,0:T(8,128)}, f32[4,144,384]{2,1,0:T(8,128)S(1)}, u32[]{:S(2)}, u32[]{:S(2)}) collective-permute-start(f32[4,144,384]{2,1,0:T(8,128)} %get-tuple-element.76), channel_id=1, source_target_pairs={{0,16},{1,17},{2,18},{3,19},{4,20},{5,21},{6,22},{7,23},{8,24},{9,... | collective-permute-start | bytes 2654216 | tf_op jit(solution)/shard_map/ppermute | solution.py:27
  303.3 33.9 %collective-permute-start.11 = (f32[4,144,384]{2,1,0:T(8,128)}, f32[4,144,384]{2,1,0:T(8,128)}, u32[]{:S(2)}, u32[]{:S(2)}) collective-permute-start(f32[4,144,384]{2,1,0:T(8,128)} %get-tuple-element.77), channel_id=1, source_target_pairs={{0,16},{1,17},{2,18},{3,19},{4,20},{5,21},{6,22},{7,23},{8,24},{9,... | collective-permute-start | bytes 2654216 | tf_op jit(solution)/shard_map/ppermute | solution.py:27
  315.0 45.6 %collective-permute-start.9 = (f32[4,144,384]{2,1,0:T(8,128)}, f32[4,144,384]{2,1,0:T(8,128)}, u32[]{:S(2)}, u32[]{:S(2)}) collective-permute-start(f32[4,144,384]{2,1,0:T(8,128)} %get-tuple-element.73), channel_id=1, source_target_pairs={{0,16},{1,17},{2,18},{3,19},{4,20},{5,21},{6,22},{7,23},{8,24},{9,... | collective-permute-start | bytes 2654216 | tf_op jit(solution)/shard_map/ppermute | solution.py:27
  318.3 19.0 %copy-start.9 = (f32[4,144,384]{2,1,0:T(8,128)}, f32[4,144,384]{2,1,0:T(8,128)S(1)}, u32[]{:S(2)}) copy-start(f32[4,144,384]{2,1,0:T(8,128)S(1)} %collective-permute-done.10.refs_2_) | copy-start | bytes 2654212
  372.1 11.2 %copy-start.21 = (f32[4,144,384]{2,1,0:T(8,128)S(1)}, f32[4,144,384]{2,1,0:T(8,128)}, u32[]{:S(2)}) copy-start(f32[4,144,384]{2,1,0:T(8,128)} %get-tuple-element.67) | copy-start | bytes 2654212
  372.1 124.7 %all-to-all-start.4 = ((f32[16,8,10112]{2,1,0:T(8,128)}), f32[16,8,10112]{2,1,0:T(8,128)}, u32[]{:S(2)}, u32[]{:S(2)}) async-start(f32[16,8,10112]{2,1,0:T(8,128)} %gate.8), calls=%async_computation.4 | async-start | bytes 10354688 | tf_op jit(solution)/shard_map/all_to_all | solution.py:443
  383.3 20.1 %collective-permute-start.7 = (f32[4,144,384]{2,1,0:T(8,128)S(1)}, f32[4,144,384]{2,1,0:T(8,128)S(1)}, u32[]{:S(2)}, u32[]{:S(2)}) collective-permute-start(f32[4,144,384]{2,1,0:T(8,128)S(1)} %copy-done.21), channel_id=1, source_target_pairs={{16,0},{17,1},{18,2},{19,3},{20,4},{21,5},{22,6},{23,7},{24,8},{25... | collective-permute-start | bytes 2654216 | tf_op jit(solution)/shard_map/ppermute | solution.py:27
  403.4 0.9 copy-start.12
  409.3 22.8 %collective-permute-start.8 = (f32[4,144,384]{2,1,0:T(8,128)}, f32[4,144,384]{2,1,0:T(8,128)S(1)}, u32[]{:S(2)}, u32[]{:S(2)}) collective-permute-start(f32[4,144,384]{2,1,0:T(8,128)} %get-tuple-element.70), channel_id=1, source_target_pairs={{0,16},{1,17},{2,18},{3,19},{4,20},{5,21},{6,22},{7,23},{8,24},{9,... | collective-permute-start | bytes 2654216 | tf_op jit(solution)/shard_map/ppermute | solution.py:27
  432.1 0.9 copy-start.10
  496.8 5.4 copy-start.8
  496.8 45.8 %all-to-all-start.5 = ((f32[16,8,3456]{2,1,0:T(8,128)}), f32[16,8,3456]{2,1,0:T(8,128)}, u32[]{:S(2)}, u32[]{:S(2)}) async-start(f32[16,8,3456]{2,1,0:T(8,128)} %gate.9), calls=%async_computation.5 | async-start | bytes 3538944 | tf_op jit(solution)/shard_map/all_to_all | solution.py:443
  502.3 4.2 copy-start.13
  502.4 4.2 copy-start.5
  502.4 4.3 copy-start.14
  504.9 1.8 copy-start.15
  504.9 2.3 copy-start.6
  506.5 1.2 copy-start.16
  542.6 16.2 %copy-start.1 = (f32[70,70]{1,0:T(8,128)S(1)}, f32[70,70]{1,0:T(8,128)}, u32[]{:S(2)}) copy-start(f32[70,70]{1,0:T(8,128)} %param.11) | copy-start | bytes 58804
